TPU v7x, 128 devices: a whole 4x4x4 slice. The times are simulated.
128 devices in a mesh: gx: 8 (over z, core), gy: 16 (over y, x).
Axes of the slice: x: 4, y: 4, z: 4, core: 2. Of those that a mesh axis runs over, the one named last changes fastest.
Arguments:
- block_vectors: bfloat16 [3, 128, 294912], P(None, None, ('gx', 'gy')), may hold values from -6 to 6
- connectivity: int32 [8, 294912], P(None, ('gx', 'gy')), may hold values from 0 to 2303
- density: float32 [294912], P(('gx', 'gy')), may hold values from 0.1 to 1
- stiff_factor: bfloat16 [24, 24], replicated, may hold values from -1.25 to 1.25
- mass_factor: bfloat16 [24, 24], replicated, may hold values from -1.25 to 1.25
- send_slot: int32 [128, 8, 96], P(('gx', 'gy')), may hold values from 0 to 2303, as said below
- send_count: int32 [128, 8], P(('gx', 'gy')), may hold values from 0 to 96, as said below
- recv_target: int32 [128, 8, 96], P(('gx', 'gy')), may hold values from 0 to 2303, as said below
- recv_weight: float32 [128, 8, 96], P(('gx', 'gy')), may hold values from 0.2 to 1
Outputs:
- filtered_density: float32 [294912], P(('gx', 'gy'))
- filtered_sens: float32 [294912], P(('gx', 'gy'))
- ritz_sum: float32 [], replicated
Inputs may be any that keep to these rules, and one draw needn't show every extreme that they name: `send_slot`: a tile's live slots name distinct elements of the sender's rim layer, 2 elements deep, that faces the neighbour in that direction. `send_count`: 0 towards neighbours off the slab; otherwise at least three quarters of the facing rim layer on the four sides and at least half of it on the four corners; every device's tile to the next device along gy (the last one's: to the previous) is full. `recv_target`: elements of the owner's rim layer, 2 elements deep, that faces the sender.
All inputs are finite; a program needn't handle non-finite values.
Results may differ from a plain program's by a relative error of at most 0.0011.
Values sent between devices are 32-bit elements; how exact they have to be, the bound alone decides.
No kernel may reach another device: no remote copies, remote signals or barrier semaphores. Data moves between devices by JAX's collectives and lax.ppermute only.
A program may use at most 64 MiB of HBM per device.

v0:
```python
import jax
import jax.numpy as jnp
from jax import lax
from jax.sharding import PartitionSpec as P

DIRECTIONS = ((-1, -1), (-1, 0), (-1, 1), (0, -1), (0, 1), (1, -1), (1, 0), (1, 1))


def shifted(shard, axis, by):
    length = lax.axis_size(axis)
    pairs = [(i, i + by) for i in range(length) if 0 <= i + by < length]
    return lax.ppermute(shard, axis, pairs)


def invert_spd(gram, vec_count):
    factor_low = jnp.linalg.cholesky(gram)
    eye = jnp.eye(vec_count, dtype=gram.dtype)
    lower_inv = lax.linalg.triangular_solve(factor_low, eye, left_side=True, lower=True)
    return lax.linalg.triangular_solve(
        factor_low, lower_inv, left_side=True, lower=True, transpose_a=True
    )


def project(vectors, conn_block, factors, vec_count):
    width = conn_block.shape[1]
    picked = vectors[:, :, conn_block]
    picked = jnp.transpose(picked, (0, 2, 1, 3)).reshape(24, vec_count * width)
    projected = jnp.dot(factors, picked, preferred_element_type=jnp.float32).astype(jnp.bfloat16)
    return projected.reshape(48, vec_count, width)


def per_device(
    block_vectors,
    connectivity,
    density,
    stiff_factor,
    mass_factor,
    send_slot,
    send_count,
    recv_target,
    recv_weight,
):
    highest_precision = lax.Precision.HIGHEST
    vec_count = block_vectors.shape[1]
    elem_count = density.shape[0]
    block = min(256, elem_count)
    blocks = elem_count // block
    factors = jnp.concatenate([stiff_factor, mass_factor], axis=0)
    conn_blocks = connectivity.reshape(8, blocks, block).transpose(1, 0, 2)
    dens_blocks = density.reshape(blocks, block)

    def gram_step(totals, block_item):
        conn_block, dens_block = block_item
        projected = project(block_vectors, conn_block, factors, vec_count)
        proj_stiff = projected[:24]
        projected_mass_matrix = projected[24:]
        weighted_stiff = (proj_stiff * (dens_block**3)[None, None, :]).astype(jnp.bfloat16)
        weighted_mass = (projected_mass_matrix * dens_block[None, None, :]).astype(jnp.bfloat16)
        part_stiff = jnp.einsum(
            "ivb,iwb->vw", weighted_stiff, proj_stiff, preferred_element_type=jnp.float32
        )
        part_mass = jnp.einsum(
            "ivb,iwb->vw", weighted_mass, projected_mass_matrix, preferred_element_type=jnp.float32
        )
        return ((totals[0] + part_stiff, totals[1] + part_mass), None)

    zero_gram = jnp.zeros((vec_count, vec_count), jnp.float32)
    (stiffness_gram_matrix, gram_mass), _ = lax.scan(
        gram_step, (zero_gram, zero_gram), (conn_blocks, dens_blocks)
    )
    stiffness_gram_matrix = 0.5 * (stiffness_gram_matrix + stiffness_gram_matrix.T)
    gram_mass = 0.5 * (gram_mass + gram_mass.T)
    stiffness_gram_matrix, gram_mass = lax.psum((stiffness_gram_matrix, gram_mass), ("gx", "gy"))
    inv_mass = invert_spd(gram_mass, vec_count)
    sandwich_product = jnp.dot(
        jnp.dot(inv_mass, stiffness_gram_matrix, precision=highest_precision),
        inv_mass,
        precision=highest_precision,
    )
    ritz_sum = jnp.sum(inv_mass * stiffness_gram_matrix) / vec_count
    inv_round = inv_mass.astype(jnp.bfloat16)
    sandwich_rounding = sandwich_product.astype(jnp.bfloat16)
    rows_gx = lax.axis_size("gx")
    rows_gy = lax.axis_size("gy")
    peers = rows_gx * rows_gy
    scaling = float(elem_count * peers) / vec_count

    def energy_step(unused, block_item):
        conn_block, dens_block = block_item
        projected = project(block_vectors, conn_block, factors, vec_count)
        proj_stiff = projected[:24]
        projected_mass_matrix = projected[24:]
        inner_stiff = jnp.einsum(
            "fc,hca->hfa", inv_round, proj_stiff, preferred_element_type=jnp.float32
        )
        inner_mass_product = jnp.einsum(
            "fc,hca->hfa",
            sandwich_rounding,
            projected_mass_matrix,
            preferred_element_type=jnp.float32,
        )
        energy_stiff = jnp.sum(inner_stiff * proj_stiff, axis=(0, 1))
        energy_mass = jnp.sum(inner_mass_product * projected_mass_matrix, axis=(0, 1))
        return (unused, scaling * (3.0 * dens_block * dens_block * energy_stiff - energy_mass))

    _, sens_blocks = lax.scan(energy_step, jnp.zeros((), jnp.float32), (conn_blocks, dens_blocks))
    sensitivity = sens_blocks.reshape(elem_count)
    slot_table = send_slot[0]
    capacity = slot_table.shape[1]
    counts = send_count[0]
    live_slots = lax.broadcasted_iota(jnp.int32, slot_table.shape, 1) < counts[:, None]
    tile_values = jnp.stack(
        [
            jnp.where(live_slots, density[slot_table], 0.0),
            jnp.where(live_slots, sensitivity[slot_table], 0.0),
        ],
        axis=0,
    )
    gx_index = lax.axis_index("gx")
    gy_index = lax.axis_index("gy")
    parts_values, parts_counts = ([], [])
    for position, (step_row, step_col) in enumerate(DIRECTIONS):
        moved_values, moved_count = shifted(
            (tile_values[:, position], counts[position : position + 1]),
            ("gx", "gy"),
            step_row * rows_gy + step_col,
        )
        src_row = gx_index - step_row
        src_col = gy_index - step_col
        valid = (src_row >= 0) & (src_row < rows_gx) & (src_col >= 0) & (src_col < rows_gy)
        parts_values.append(jnp.where(valid, moved_values, 0.0))
        parts_counts.append(jnp.where(valid, moved_count[0], 0))
    recv_values = jnp.stack(parts_values, axis=1)
    recv_counts = jnp.stack(parts_counts)
    live_in = lax.broadcasted_iota(jnp.int32, (8, capacity), 1) < recv_counts[:, None]
    live_weight = jnp.where(live_in, recv_weight[0], 0.0)
    stacked = jnp.stack(
        [live_weight, live_weight * recv_values[0], live_weight * recv_values[1]], axis=-1
    ).reshape(8 * capacity, 3)
    sums = jax.ops.segment_sum(
        stacked, recv_target[0].reshape(8 * capacity), num_segments=elem_count
    )
    denominator = 1.0 + sums[:, 0]
    filtered_density = (density + sums[:, 1]) / denominator
    filtered_sens = (sensitivity + sums[:, 2]) / denominator
    return (filtered_density, filtered_sens, ritz_sum)


def solution(mesh):
    placed = (
        P(None, None, ("gx", "gy")),
        P(None, ("gx", "gy")),
        P(("gx", "gy")),
        P(),
        P(),
        P(("gx", "gy"), None, None),
        P(("gx", "gy"), None),
        P(("gx", "gy"), None, None),
        P(("gx", "gy"), None, None),
    )
    return jax.shard_map(
        per_device,
        mesh=mesh,
        in_specs=placed,
        out_specs=(P(("gx", "gy")), P(("gx", "gy")), P()),
        check_vma=False,
    )
```

profile of v0, /device:TPU:0, one launch (start us, length us, event | category | flops | bytes accessed | tf_op | source)
XLA Modules:
  0.0 651.6 jit_solution(18225430280258432065)
XLA Ops:
  11.4 8.4 %collective-permute-start.5 = (s32[1]{0:T(128)}, s32[1]{0:T(128)}, u32[]{:S(2)}, u32[]{:S(2)}) collective-permute-start(s32[1]{0:T(128)} %bitcast.25), channel_id=1, source_target_pairs={{0,15},{1,16},{2,17},{3,18},{4,19},{5,20},{6,21},{7,22},{8,23},{9,... | collective-permute-start | bytes 20 | tf_op jit(solution)/shard_map/ppermute | solution.py:12
  19.9 5.1 collective-permute-start.7
  26.3 4.3 copy.47
  30.9 198.8 %while.24 = (s32[]{:T(128)}, f32[128,128]{1,0:T(8,128)S(1)}, f32[128,128]{1,0:T(8,128)S(1)}, s32[9,8,256]{2,1,0:T(8,128)}, bf16[3,128,2304]{1,0,2:T(4,128)(2,1)S...) while((s32[]{:T(128)}, f32[128,128]{1,0:T(8,128)S(1)}, ...), condition=%wide.region_1.2_spmd.clone, body=%wide.region_0.1_spmd.clone.sunk | while | flops 484516352 | bytes 41222564 | solution.py:68
  31.7 14.4 %gather_fusion.1 = bf16[2048,3,128]{2,1,0:T(4,128)(2,1)} fusion(bf16[3,128,2304]{1,0,2:T(4,128)(2,1)S(1)} %get-tuple-element.330, s32[2048]{0:T(1024)S(1)} %broadcast_clamp_fusion.5), kind=kCustom, calls=%fused_computation.clone.clone.1 | custom fusion | bytes 3153920 | tf_op jit(solution)/shard_map/while/body/eval_jaxpr/gather | solution.py:26
  46.1 2.7 copy.79
  53.8 14.4 %gather_fusion.1 = bf16[2048,3,128]{2,1,0:T(4,128)(2,1)} fusion(bf16[3,128,2304]{1,0,2:T(4,128)(2,1)S(1)} %get-tuple-element.330, s32[2048]{0:T(1024)S(1)} %broadcast_clamp_fusion.5), kind=kCustom, calls=%fused_computation.clone.clone.1 | custom fusion | bytes 3153920 | tf_op jit(solution)/shard_map/while/body/eval_jaxpr/gather | solution.py:26
  68.2 2.7 copy.79
  75.8 14.4 %gather_fusion.1 = bf16[2048,3,128]{2,1,0:T(4,128)(2,1)} fusion(bf16[3,128,2304]{1,0,2:T(4,128)(2,1)S(1)} %get-tuple-element.330, s32[2048]{0:T(1024)S(1)} %broadcast_clamp_fusion.5), kind=kCustom, calls=%fused_computation.clone.clone.1 | custom fusion | bytes 3153920 | tf_op jit(solution)/shard_map/while/body/eval_jaxpr/gather | solution.py:26
  90.3 2.7 copy.79
  97.9 14.4 %gather_fusion.1 = bf16[2048,3,128]{2,1,0:T(4,128)(2,1)} fusion(bf16[3,128,2304]{1,0,2:T(4,128)(2,1)S(1)} %get-tuple-element.330, s32[2048]{0:T(1024)S(1)} %broadcast_clamp_fusion.5), kind=kCustom, calls=%fused_computation.clone.clone.1 | custom fusion | bytes 3153920 | tf_op jit(solution)/shard_map/while/body/eval_jaxpr/gather | solution.py:26
  112.4 2.7 copy.79
  120.0 14.4 %gather_fusion.1 = bf16[2048,3,128]{2,1,0:T(4,128)(2,1)} fusion(bf16[3,128,2304]{1,0,2:T(4,128)(2,1)S(1)} %get-tuple-element.330, s32[2048]{0:T(1024)S(1)} %broadcast_clamp_fusion.5), kind=kCustom, calls=%fused_computation.clone.clone.1 | custom fusion | bytes 3153920 | tf_op jit(solution)/shard_map/while/body/eval_jaxpr/gather | solution.py:26
  134.4 2.7 copy.79
  142.1 14.4 %gather_fusion.1 = bf16[2048,3,128]{2,1,0:T(4,128)(2,1)} fusion(bf16[3,128,2304]{1,0,2:T(4,128)(2,1)S(1)} %get-tuple-element.330, s32[2048]{0:T(1024)S(1)} %broadcast_clamp_fusion.5), kind=kCustom, calls=%fused_computation.clone.clone.1 | custom fusion | bytes 3153920 | tf_op jit(solution)/shard_map/while/body/eval_jaxpr/gather | solution.py:26
  156.5 2.7 copy.79
  164.2 14.4 %gather_fusion.1 = bf16[2048,3,128]{2,1,0:T(4,128)(2,1)} fusion(bf16[3,128,2304]{1,0,2:T(4,128)(2,1)S(1)} %get-tuple-element.330, s32[2048]{0:T(1024)S(1)} %broadcast_clamp_fusion.5), kind=kCustom, calls=%fused_computation.clone.clone.1 | custom fusion | bytes 3153920 | tf_op jit(solution)/shard_map/while/body/eval_jaxpr/gather | solution.py:26
  178.6 2.7 copy.79
  186.3 14.4 %gather_fusion.1 = bf16[2048,3,128]{2,1,0:T(4,128)(2,1)} fusion(bf16[3,128,2304]{1,0,2:T(4,128)(2,1)S(1)} %get-tuple-element.330, s32[2048]{0:T(1024)S(1)} %broadcast_clamp_fusion.5), kind=kCustom, calls=%fused_computation.clone.clone.1 | custom fusion | bytes 3153920 | tf_op jit(solution)/shard_map/while/body/eval_jaxpr/gather | solution.py:26
  200.7 2.7 copy.79
  208.4 14.4 %gather_fusion.1 = bf16[2048,3,128]{2,1,0:T(4,128)(2,1)} fusion(bf16[3,128,2304]{1,0,2:T(4,128)(2,1)S(1)} %get-tuple-element.330, s32[2048]{0:T(1024)S(1)} %broadcast_clamp_fusion.5), kind=kCustom, calls=%fused_computation.clone.clone.1 | custom fusion | bytes 3153920 | tf_op jit(solution)/shard_map/while/body/eval_jaxpr/gather | solution.py:26
  222.8 2.7 copy.79
  230.8 4.5 gather_fusion.2
  235.5 5.2 collective-permute-start.4
  243.2 9.5 %collective-permute-start.6 = (s32[1]{0:T(128)}, s32[1]{0:T(128)}, u32[]{:S(2)}, u32[]{:S(2)}) collective-permute-start(s32[1]{0:T(128)} %bitcast.28), channel_id=1, source_target_pairs={{0,16},{1,17},{2,18},{3,19},{4,20},{5,21},{6,22},{7,23},{8,24},{9,... | collective-permute-start | bytes 20 | tf_op jit(solution)/shard_map/ppermute | solution.py:12
  256.7 121.0 %all-reduce.3.cloned.1.call-done = (f32[128,128]{1,0:T(8,128)}, f32[128,128]{1,0:T(8,128)}) async-done(((f32[128,128]{1,0:T(8,128)}, f32[128,128]{1,0:T(8,128)}), (f32[128,128]{1,0:T(8,128)}, f32[128,128]{1,0:T(8,128)})) %all-reduce.3.cloned.1.call-update) | async-done | bytes 131088 | tf_op jit(solution)/shard_map/psum | solution.py:73
  379.5 11.7 %cholesky.16 = f32[128,128]{1,0:T(8,128)S(1)} custom-call(f32[128,128]{1,0:T(8,128)S(1)} %fusion.28), custom_call_target="Cholesky" | custom-call | tf_op jit(solution)/shard_map/jit(cholesky)/cholesky | solution.py:16
  392.5 9.8 %custom-call.8 = f32[1,128,128]{1,2,0:T(8,128)S(1)} custom-call(f32[1,128,128]{2,1,0:T(8,128)S(1)} %fusion.22), custom_call_target="InvertDiagBlocksLowerTriangular" | custom-call | tf_op jit(solution)/shard_map/triangular_solve | solution.py:19
  405.5 195.2 %while.23 = (s32[]{:T(128)}, f32[9,256]{1,0:T(8,128)S(1)}, f32[9,256]{1,0:T(8,128)S(1)}, s32[9,8,256]{2,1,0:T(8,128)}, bf16[3,128,2304]{1,0,2:T(4,128)(2,1)S(1)}...) while((s32[]{:T(128)}, f32[9,256]{1,0:T(8,128)S(1)}, ...), condition=%wide.region_9.10_spmd, body=%wide.region_6.0_spmd.sunk | while | flops 484451072 | bytes 41028008 | solution.py:106
  406.3 14.4 %gather_fusion = bf16[2048,3,128]{2,1,0:T(4,128)(2,1)} fusion(bf16[3,128,2304]{1,0,2:T(4,128)(2,1)S(1)} %get-tuple-element.359, s32[2048]{0:T(1024)S(1)} %broadcast_clamp_fusion.4), kind=kCustom, calls=%fused_computation.1.clone.1 | custom fusion | bytes 3153920 | tf_op jit(solution)/shard_map/while/body/eval_jaxpr/gather | solution.py:26
  428.0 14.4 %gather_fusion = bf16[2048,3,128]{2,1,0:T(4,128)(2,1)} fusion(bf16[3,128,2304]{1,0,2:T(4,128)(2,1)S(1)} %get-tuple-element.359, s32[2048]{0:T(1024)S(1)} %broadcast_clamp_fusion.4), kind=kCustom, calls=%fused_computation.1.clone.1 | custom fusion | bytes 3153920 | tf_op jit(solution)/shard_map/while/body/eval_jaxpr/gather | solution.py:26
  442.4 2.7 copy.75
  449.7 14.4 %gather_fusion = bf16[2048,3,128]{2,1,0:T(4,128)(2,1)} fusion(bf16[3,128,2304]{1,0,2:T(4,128)(2,1)S(1)} %get-tuple-element.359, s32[2048]{0:T(1024)S(1)} %broadcast_clamp_fusion.4), kind=kCustom, calls=%fused_computation.1.clone.1 | custom fusion | bytes 3153920 | tf_op jit(solution)/shard_map/while/body/eval_jaxpr/gather | solution.py:26
  464.1 2.7 copy.75
  471.3 14.4 %gather_fusion = bf16[2048,3,128]{2,1,0:T(4,128)(2,1)} fusion(bf16[3,128,2304]{1,0,2:T(4,128)(2,1)S(1)} %get-tuple-element.359, s32[2048]{0:T(1024)S(1)} %broadcast_clamp_fusion.4), kind=kCustom, calls=%fused_computation.1.clone.1 | custom fusion | bytes 3153920 | tf_op jit(solution)/shard_map/while/body/eval_jaxpr/gather | solution.py:26
  485.8 2.7 copy.75
  493.0 14.4 %gather_fusion = bf16[2048,3,128]{2,1,0:T(4,128)(2,1)} fusion(bf16[3,128,2304]{1,0,2:T(4,128)(2,1)S(1)} %get-tuple-element.359, s32[2048]{0:T(1024)S(1)} %broadcast_clamp_fusion.4), kind=kCustom, calls=%fused_computation.1.clone.1 | custom fusion | bytes 3153920 | tf_op jit(solution)/shard_map/while/body/eval_jaxpr/gather | solution.py:26
  507.4 2.7 copy.75
  514.7 14.4 %gather_fusion = bf16[2048,3,128]{2,1,0:T(4,128)(2,1)} fusion(bf16[3,128,2304]{1,0,2:T(4,128)(2,1)S(1)} %get-tuple-element.359, s32[2048]{0:T(1024)S(1)} %broadcast_clamp_fusion.4), kind=kCustom, calls=%fused_computation.1.clone.1 | custom fusion | bytes 3153920 | tf_op jit(solution)/shard_map/while/body/eval_jaxpr/gather | solution.py:26
  536.4 14.4 %gather_fusion = bf16[2048,3,128]{2,1,0:T(4,128)(2,1)} fusion(bf16[3,128,2304]{1,0,2:T(4,128)(2,1)S(1)} %get-tuple-element.359, s32[2048]{0:T(1024)S(1)} %broadcast_clamp_fusion.4), kind=kCustom, calls=%fused_computation.1.clone.1 | custom fusion | bytes 3153920 | tf_op jit(solution)/shard_map/while/body/eval_jaxpr/gather | solution.py:26
  558.1 14.4 %gather_fusion = bf16[2048,3,128]{2,1,0:T(4,128)(2,1)} fusion(bf16[3,128,2304]{1,0,2:T(4,128)(2,1)S(1)} %get-tuple-element.359, s32[2048]{0:T(1024)S(1)} %broadcast_clamp_fusion.4), kind=kCustom, calls=%fused_computation.1.clone.1 | custom fusion | bytes 3153920 | tf_op jit(solution)/shard_map/while/body/eval_jaxpr/gather | solution.py:26
  579.7 14.4 %gather_fusion = bf16[2048,3,128]{2,1,0:T(4,128)(2,1)} fusion(bf16[3,128,2304]{1,0,2:T(4,128)(2,1)S(1)} %get-tuple-element.359, s32[2048]{0:T(1024)S(1)} %broadcast_clamp_fusion.4), kind=kCustom, calls=%fused_computation.1.clone.1 | custom fusion | bytes 3153920 | tf_op jit(solution)/shard_map/while/body/eval_jaxpr/gather | solution.py:26
  600.7 4.5 gather_fusion.3
  606.8 7.9 %collective-permute-start.13 = (f32[2,96]{1,0:T(2,128)S(1)}, f32[2,96]{1,0:T(2,128)S(1)}, u32[]{:S(2)}, u32[]{:S(2)}) collective-permute-start(f32[2,96]{1,0:T(2,128)S(1)} %get-tuple-element.193), channel_id=1, source_target_pairs={{0,15},{1,16},{2,17},{3,18},{4,19},{5,20},{6,21},{7,22},{8,23},{9,... | collective-permute-start | bytes 2312 | tf_op jit(solution)/shard_map/ppermute | solution.py:12
  619.2 4.5 collective-permute-start.12
  623.8 5.9 collective-permute-start.14
  631.4 3.3 collective-permute-done.8
  635.1 6.3 scatter_custom_fusion
  (366 shorter events, 122.4 us)
Async XLA Ops:
  7.2 370.5 %all-reduce.3.cloned.1.call-start = ((), (), s32[]{:S(2)}) async-start(), calls=%async_computation | async-start | bytes 262144 | tf_op jit(solution)/shard_map/psum | solution.py:73
  8.8 226.7 %collective-permute-start = (s32[1]{0:T(128)}, s32[1]{0:T(128)}, u32[]{:S(2)}, u32[]{:S(2)}) collective-permute-start(s32[1]{0:T(128)} %bitcast.10), channel_id=1, source_target_pairs={{17,0},{18,1},{19,2},{20,3},{21,4},{22,5},{23,6},{24,7},{25,8},{26... | collective-permute-start | bytes 20 | tf_op jit(solution)/shard_map/ppermute | solution.py:12
  10.1 231.1 %collective-permute-start.2 = (s32[1]{0:T(128)}, s32[1]{0:T(128)}, u32[]{:S(2)}, u32[]{:S(2)}) collective-permute-start(s32[1]{0:T(128)} %bitcast.16), channel_id=1, source_target_pairs={{15,0},{16,1},{17,2},{18,3},{19,4},{20,5},{21,6},{22,7},{23,8},{24... | collective-permute-start | bytes 20 | tf_op jit(solution)/shard_map/ppermute | solution.py:12
  11.4 231.8 %collective-permute-start.5 = (s32[1]{0:T(128)}, s32[1]{0:T(128)}, u32[]{:S(2)}, u32[]{:S(2)}) collective-permute-start(s32[1]{0:T(128)} %bitcast.25), channel_id=1, source_target_pairs={{0,15},{1,16},{2,17},{3,18},{4,19},{5,20},{6,21},{7,22},{8,23},{9,... | collective-permute-start | bytes 20 | tf_op jit(solution)/shard_map/ppermute | solution.py:12
  19.9 233.5 %collective-permute-start.7 = (s32[1]{0:T(128)}, s32[1]{0:T(128)}, u32[]{:S(2)}, u32[]{:S(2)}) collective-permute-start(s32[1]{0:T(128)} %bitcast.31), channel_id=1, source_target_pairs={{0,17},{1,18},{2,19},{3,20},{4,21},{5,22},{6,23},{7,24},{8,25},{9,... | collective-permute-start | bytes 20 | tf_op jit(solution)/shard_map/ppermute | solution.py:12
  24.9 229.1 %collective-permute-start.3 = (s32[1]{0:T(128)}, s32[1]{0:T(128)}, u32[]{:S(2)}, u32[]{:S(2)}) collective-permute-start(s32[1]{0:T(128)} %bitcast.19), channel_id=1, source_target_pairs={{1,0},{2,1},{3,2},{4,3},{5,4},{6,5},{7,6},{8,7},{9,8},{10,9},{11,1... | collective-permute-start | bytes 20 | tf_op jit(solution)/shard_map/ppermute | solution.py:12
  26.2 4.4 copy-start.6
  26.3 4.5 copy-start.7
  26.3 4.5 copy-start
  30.9 199.7 %copy-start.9 = (s32[1,8,96]{2,1,0:T(8,128)S(1)}, s32[1,8,96]{2,1,0:T(8,128)}, u32[]{:S(2)}) copy-start(s32[1,8,96]{2,1,0:T(8,128)} %param.18) | copy-start | bytes 9220
  30.9 15.2 %copy-start.1 = (bf16[3,128,2304]{1,0,2:T(4,128)(2,1)}, bf16[3,128,2304]{1,0,2:T(4,128)(2,1)S(1)}, u32[]{:S(2)}) copy-start(bf16[3,128,2304]{1,0,2:T(4,128)(2,1)S(1)} %get-tuple-element.330) | copy-start | bytes 5308420 | tf_op jit(solution)/shard_map/while
  53.0 15.2 %copy-start.1 = (bf16[3,128,2304]{1,0,2:T(4,128)(2,1)}, bf16[3,128,2304]{1,0,2:T(4,128)(2,1)S(1)}, u32[]{:S(2)}) copy-start(bf16[3,128,2304]{1,0,2:T(4,128)(2,1)S(1)} %get-tuple-element.330) | copy-start | bytes 5308420 | tf_op jit(solution)/shard_map/while
  75.1 15.2 %copy-start.1 = (bf16[3,128,2304]{1,0,2:T(4,128)(2,1)}, bf16[3,128,2304]{1,0,2:T(4,128)(2,1)S(1)}, u32[]{:S(2)}) copy-start(bf16[3,128,2304]{1,0,2:T(4,128)(2,1)S(1)} %get-tuple-element.330) | copy-start | bytes 5308420 | tf_op jit(solution)/shard_map/while
  97.2 15.1 %copy-start.1 = (bf16[3,128,2304]{1,0,2:T(4,128)(2,1)}, bf16[3,128,2304]{1,0,2:T(4,128)(2,1)S(1)}, u32[]{:S(2)}) copy-start(bf16[3,128,2304]{1,0,2:T(4,128)(2,1)S(1)} %get-tuple-element.330) | copy-start | bytes 5308420 | tf_op jit(solution)/shard_map/while
  119.3 15.2 %copy-start.1 = (bf16[3,128,2304]{1,0,2:T(4,128)(2,1)}, bf16[3,128,2304]{1,0,2:T(4,128)(2,1)S(1)}, u32[]{:S(2)}) copy-start(bf16[3,128,2304]{1,0,2:T(4,128)(2,1)S(1)} %get-tuple-element.330) | copy-start | bytes 5308420 | tf_op jit(solution)/shard_map/while
  141.4 15.2 %copy-start.1 = (bf16[3,128,2304]{1,0,2:T(4,128)(2,1)}, bf16[3,128,2304]{1,0,2:T(4,128)(2,1)S(1)}, u32[]{:S(2)}) copy-start(bf16[3,128,2304]{1,0,2:T(4,128)(2,1)S(1)} %get-tuple-element.330) | copy-start | bytes 5308420 | tf_op jit(solution)/shard_map/while
  163.5 15.2 %copy-start.1 = (bf16[3,128,2304]{1,0,2:T(4,128)(2,1)}, bf16[3,128,2304]{1,0,2:T(4,128)(2,1)S(1)}, u32[]{:S(2)}) copy-start(bf16[3,128,2304]{1,0,2:T(4,128)(2,1)S(1)} %get-tuple-element.330) | copy-start | bytes 5308420 | tf_op jit(solution)/shard_map/while
  185.5 15.2 %copy-start.1 = (bf16[3,128,2304]{1,0,2:T(4,128)(2,1)}, bf16[3,128,2304]{1,0,2:T(4,128)(2,1)S(1)}, u32[]{:S(2)}) copy-start(bf16[3,128,2304]{1,0,2:T(4,128)(2,1)S(1)} %get-tuple-element.330) | copy-start | bytes 5308420 | tf_op jit(solution)/shard_map/while
  207.6 15.2 %copy-start.1 = (bf16[3,128,2304]{1,0,2:T(4,128)(2,1)}, bf16[3,128,2304]{1,0,2:T(4,128)(2,1)S(1)}, u32[]{:S(2)}) copy-start(bf16[3,128,2304]{1,0,2:T(4,128)(2,1)S(1)} %get-tuple-element.330) | copy-start | bytes 5308420 | tf_op jit(solution)/shard_map/while
  230.7 4.6 copy-start.8
  230.8 4.6 copy-start.10
  235.5 19.2 %collective-permute-start.4 = (s32[1]{0:T(128)}, s32[1]{0:T(128)}, u32[]{:S(2)}, u32[]{:S(2)}) collective-permute-start(s32[1]{0:T(128)} %bitcast.22), channel_id=1, source_target_pairs={{0,1},{1,2},{2,3},{3,4},{4,5},{5,6},{6,7},{7,8},{8,9},{9,10},{10,1... | collective-permute-start | bytes 20 | tf_op jit(solution)/shard_map/ppermute | solution.py:12
  241.2 14.1 %collective-permute-start.1 = (s32[1]{0:T(128)}, s32[1]{0:T(128)}, u32[]{:S(2)}, u32[]{:S(2)}) collective-permute-start(s32[1]{0:T(128)} %bitcast.13), channel_id=1, source_target_pairs={{16,0},{17,1},{18,2},{19,3},{20,4},{21,5},{22,6},{23,7},{24,8},{25... | collective-permute-start | bytes 20 | tf_op jit(solution)/shard_map/ppermute | solution.py:12
  243.2 12.7 %collective-permute-start.6 = (s32[1]{0:T(128)}, s32[1]{0:T(128)}, u32[]{:S(2)}, u32[]{:S(2)}) collective-permute-start(s32[1]{0:T(128)} %bitcast.28), channel_id=1, source_target_pairs={{0,16},{1,17},{2,18},{3,19},{4,20},{5,21},{6,22},{7,23},{8,24},{9,... | collective-permute-start | bytes 20 | tf_op jit(solution)/shard_map/ppermute | solution.py:12
  405.5 15.2 %copy-start.3 = (bf16[3,128,2304]{1,0,2:T(4,128)(2,1)}, bf16[3,128,2304]{1,0,2:T(4,128)(2,1)S(1)}, u32[]{:S(2)}) copy-start(bf16[3,128,2304]{1,0,2:T(4,128)(2,1)S(1)} %get-tuple-element.359) | copy-start | bytes 5308420 | tf_op jit(solution)/shard_map/while
  425.6 1.7 copy-start.4
  427.3 15.2 %copy-start.3 = (bf16[3,128,2304]{1,0,2:T(4,128)(2,1)}, bf16[3,128,2304]{1,0,2:T(4,128)(2,1)S(1)}, u32[]{:S(2)}) copy-start(bf16[3,128,2304]{1,0,2:T(4,128)(2,1)S(1)} %get-tuple-element.359) | copy-start | bytes 5308420 | tf_op jit(solution)/shard_map/while
  447.3 1.7 copy-start.4
  448.9 15.2 %copy-start.3 = (bf16[3,128,2304]{1,0,2:T(4,128)(2,1)}, bf16[3,128,2304]{1,0,2:T(4,128)(2,1)S(1)}, u32[]{:S(2)}) copy-start(bf16[3,128,2304]{1,0,2:T(4,128)(2,1)S(1)} %get-tuple-element.359) | copy-start | bytes 5308420 | tf_op jit(solution)/shard_map/while
  469.0 1.7 copy-start.4
  470.6 15.1 %copy-start.3 = (bf16[3,128,2304]{1,0,2:T(4,128)(2,1)}, bf16[3,128,2304]{1,0,2:T(4,128)(2,1)S(1)}, u32[]{:S(2)}) copy-start(bf16[3,128,2304]{1,0,2:T(4,128)(2,1)S(1)} %get-tuple-element.359) | copy-start | bytes 5308420 | tf_op jit(solution)/shard_map/while
  492.3 15.2 %copy-start.3 = (bf16[3,128,2304]{1,0,2:T(4,128)(2,1)}, bf16[3,128,2304]{1,0,2:T(4,128)(2,1)S(1)}, u32[]{:S(2)}) copy-start(bf16[3,128,2304]{1,0,2:T(4,128)(2,1)S(1)} %get-tuple-element.359) | copy-start | bytes 5308420 | tf_op jit(solution)/shard_map/while
  512.3 1.7 copy-start.4
  514.0 15.2 %copy-start.3 = (bf16[3,128,2304]{1,0,2:T(4,128)(2,1)}, bf16[3,128,2304]{1,0,2:T(4,128)(2,1)S(1)}, u32[]{:S(2)}) copy-start(bf16[3,128,2304]{1,0,2:T(4,128)(2,1)S(1)} %get-tuple-element.359) | copy-start | bytes 5308420 | tf_op jit(solution)/shard_map/while
  535.7 15.2 %copy-start.3 = (bf16[3,128,2304]{1,0,2:T(4,128)(2,1)}, bf16[3,128,2304]{1,0,2:T(4,128)(2,1)S(1)}, u32[]{:S(2)}) copy-start(bf16[3,128,2304]{1,0,2:T(4,128)(2,1)S(1)} %get-tuple-element.359) | copy-start | bytes 5308420 | tf_op jit(solution)/shard_map/while
  555.7 1.7 copy-start.4
  557.3 15.2 %copy-start.3 = (bf16[3,128,2304]{1,0,2:T(4,128)(2,1)}, bf16[3,128,2304]{1,0,2:T(4,128)(2,1)S(1)}, u32[]{:S(2)}) copy-start(bf16[3,128,2304]{1,0,2:T(4,128)(2,1)S(1)} %get-tuple-element.359) | copy-start | bytes 5308420 | tf_op jit(solution)/shard_map/while
  579.0 15.2 %copy-start.3 = (bf16[3,128,2304]{1,0,2:T(4,128)(2,1)}, bf16[3,128,2304]{1,0,2:T(4,128)(2,1)S(1)}, u32[]{:S(2)}) copy-start(bf16[3,128,2304]{1,0,2:T(4,128)(2,1)S(1)} %get-tuple-element.359) | copy-start | bytes 5308420 | tf_op jit(solution)/shard_map/while
  599.0 1.7 copy-start.4
  600.7 4.5 copy-start.5
  605.4 13.9 %collective-permute-start.10 = (f32[2,96]{1,0:T(2,128)S(1)}, f32[2,96]{1,0:T(2,128)S(1)}, u32[]{:S(2)}, u32[]{:S(2)}) collective-permute-start(f32[2,96]{1,0:T(2,128)S(1)} %get-tuple-element.190), channel_id=1, source_target_pairs={{15,0},{16,1},{17,2},{18,3},{19,4},{20,5},{21,6},{22,7},{23,8},{24... | collective-permute-start | bytes 2312 | tf_op jit(solution)/shard_map/ppermute | solution.py:12
  606.8 17.0 %collective-permute-start.13 = (f32[2,96]{1,0:T(2,128)S(1)}, f32[2,96]{1,0:T(2,128)S(1)}, u32[]{:S(2)}, u32[]{:S(2)}) collective-permute-start(f32[2,96]{1,0:T(2,128)S(1)} %get-tuple-element.193), channel_id=1, source_target_pairs={{0,15},{1,16},{2,17},{3,18},{4,19},{5,20},{6,21},{7,22},{8,23},{9,... | collective-permute-start | bytes 2312 | tf_op jit(solution)/shard_map/ppermute | solution.py:12
  614.7 15.1 %collective-permute-start.15 = (f32[2,96]{1,0:T(2,128)S(1)}, f32[2,96]{1,0:T(2,128)S(1)}, u32[]{:S(2)}, u32[]{:S(2)}) collective-permute-start(f32[2,96]{1,0:T(2,128)S(1)} %get-tuple-element.187), channel_id=1, source_target_pairs={{0,17},{1,18},{2,19},{3,20},{4,21},{5,22},{6,23},{7,24},{8,25},{9,... | collective-permute-start | bytes 2312 | tf_op jit(solution)/shard_map/ppermute | solution.py:12
  616.0 15.3 %collective-permute-start.9 = (f32[2,96]{1,0:T(2,128)S(1)}, f32[2,96]{1,0:T(2,128)S(1)}, u32[]{:S(2)}, u32[]{:S(2)}) collective-permute-start(f32[2,96]{1,0:T(2,128)S(1)} %get-tuple-element.189), channel_id=1, source_target_pairs={{16,0},{17,1},{18,2},{19,3},{20,4},{21,5},{22,6},{23,7},{24,8},{25... | collective-permute-start | bytes 2312 | tf_op jit(solution)/shard_map/ppermute | solution.py:12
  617.3 14.0 %collective-permute-start.11 = (f32[2,96]{1,0:T(2,128)S(1)}, f32[2,96]{1,0:T(2,128)S(1)}, u32[]{:S(2)}, u32[]{:S(2)}) collective-permute-start(f32[2,96]{1,0:T(2,128)S(1)} %get-tuple-element.191), channel_id=1, source_target_pairs={{1,0},{2,1},{3,2},{4,3},{5,4},{6,5},{7,6},{8,7},{9,8},{10,9},{11,1... | collective-permute-start | bytes 2312 | tf_op jit(solution)/shard_map/ppermute | solution.py:12
  619.2 12.1 %collective-permute-start.12 = (f32[2,96]{1,0:T(2,128)S(1)}, f32[2,96]{1,0:T(2,128)S(1)}, u32[]{:S(2)}, u32[]{:S(2)}) collective-permute-start(f32[2,96]{1,0:T(2,128)S(1)} %get-tuple-element.192), channel_id=1, source_target_pairs={{0,1},{1,2},{2,3},{3,4},{4,5},{5,6},{6,7},{7,8},{8,9},{9,10},{10,1... | collective-permute-start | bytes 2312 | tf_op jit(solution)/shard_map/ppermute | solution.py:12
  623.8 7.5 %collective-permute-start.14 = (f32[2,96]{1,0:T(2,128)S(1)}, f32[2,96]{1,0:T(2,128)S(1)}, u32[]{:S(2)}, u32[]{:S(2)}) collective-permute-start(f32[2,96]{1,0:T(2,128)S(1)} %get-tuple-element.194), channel_id=1, source_target_pairs={{0,16},{1,17},{2,18},{3,19},{4,20},{5,21},{6,22},{7,23},{8,24},{9,... | collective-permute-start | bytes 2312 | tf_op jit(solution)/shard_map/ppermute | solution.py:12
  629.7 4.9 collective-permute-start.8
  (12 other events, 20.0 us)
Sparse Core Ops, SparseCore 0:
  230.7 146.9 all-reduce.2
where the time goes:
time: 661 us; the launch traced here: 652 us
  local copies, waits for them, and re-layouts  357 us (54%)
  waiting for transfers between devices  124 us (19%)
  starting transfers between devices  58.4 us (9%)
  other arithmetic  46.3 us (7%)
  matrix products  42.6 us (6%)
  between operations  21.3 us (3%)
    gather x18, local copies, waits for them, and re-layouts, project(): picked = vectors[:, :, conn_block]  260 us
    psum x1, waiting for transfers between devices, per_device(): lax.psum((stiffness_gram_matrix, gram_mass), ('gx', 'gy'))  121 us
    while x144, local copies, waits for them, and re-layouts  76 us
    ppermute x16, starting transfers between devices, shifted(): return lax.ppermute(shard, axis, pairs)  58.4 us
    dot_general x18, matrix products, project(): jnp.dot(factors, picked, preferred_element_type=jnp.float32)  18.2 us
  transfers between devices with their start and end apart: 17, of which 2 were waited for; matrix products, arithmetic and copies ran while one was open for 31% of the time, Pallas kernels for 0%

commit v1 on v0

v1 whole, which is shorter than its diff:
```python
import jax
import jax.numpy as jnp
from jax import lax
from jax.experimental import pallas as pl
from jax.experimental.pallas import tpu as pltpu
from jax.sharding import PartitionSpec as P

SIDE = 48
RIM = 2
LANES = 128
GROUP = 8
UNIT = 32
ROWS = 24 * GROUP
AXES = ("gx", "gy")
VMEM_LIMIT = 60 * 1024 * 1024
F32 = jnp.float32
BF16 = jnp.bfloat16
HIGHEST = lax.Precision.HIGHEST


def iota(shape, dim):
    return lax.broadcasted_iota(jnp.int32, shape, dim)


def density_columns(dens_ref, dcol):
    for j in range(dens_ref.shape[0]):
        row = jnp.broadcast_to(dens_ref[j : j + 1, :], (LANES, LANES))
        dcol[pl.ds(j * LANES, LANES), :] = row.T


PIECES = (
    ((0, 0), (1, 3), (2, 6)),
    ((2, -2), (3, 1), (4, 4), (5, 7)),
    ((5, -1), (6, 2), (7, 5)),
)


def gram_kernel(
    elems, per_step, conn_ref, vec_ref, dens_ref, w_ref, p_ref, out_ref, table, dcol, x_even, x_odd, weighted, acc
):
    step = pl.program_id(0)
    units = elems // UNIT
    sub = iota((8, LANES), 0)

    def gather(unit, xbuf):
        base = unit * UNIT
        for q in range(UNIT // 16):
            for h in range(2):
                for pair in range(4):
                    regs = []
                    for e in range(2):
                        at = base + (q * 16 + h * 8 + pair * 2 + e)
                        rows = [conn_ref[a * elems + at] for a in range(8)]
                        for pieces in PIECES:
                            value = None
                            for corner, first in pieces:
                                got = table[pl.ds(rows[corner] + (8 - first), 8), :]
                                value = got if value is None else jnp.where(sub >= first, got, value)
                            regs.append(value)
                    block = jnp.concatenate(regs, axis=0).astype(BF16)
                    xbuf[q, pl.ds(pair * 48, 48), pl.ds(h * LANES, LANES)] = block

    @pl.when(step == 0)
    def _():
        for c in range(3):
            for j in range(elems // LANES):
                block = vec_ref[c, :, pl.ds(j * LANES, LANES)].astype(F32).T
                table[pl.ds(8 + 3 * LANES * j + c, LANES, stride=3), :] = block
        density_columns(dens_ref, dcol)
        acc[...] = jnp.zeros_like(acc)
        gather(0, x_even)

    def compute(unit, local, xbuf):
        for q in range(UNIT // 16):
            full = jnp.dot(w_ref[...], xbuf[q], preferred_element_type=F32).astype(BF16)
            for h in range(2):
                part = full[:, h * LANES : (h + 1) * LANES]
                chunk = 2 * q + h
                p_ref[local * 4 + chunk] = part
                wide = part.astype(F32).reshape(2, 24, 8, LANES)
                dens = dcol[pl.ds(pl.multiple_of(unit * UNIT + chunk * 8, 8), 8), :]
                weighted[0, chunk] = (wide[0] * (dens * dens * dens)[None]).reshape(ROWS, LANES).astype(BF16)
                weighted[1, chunk] = (wide[1] * dens[None]).reshape(ROWS, LANES).astype(BF16)
        for kind in range(2):
            left = weighted[kind].reshape(4 * ROWS, LANES)
            right = p_ref[pl.ds(local * 4, 4), pl.ds(kind * ROWS, ROWS), :].reshape(4 * ROWS, LANES)
            acc[kind] += lax.dot_general(left, right, (((0,), (0,)), ((), ())), preferred_element_type=F32)

    def body(it, _):
        unit = step * per_step + 2 * it
        gather(unit + 1, x_odd)
        compute(unit, 2 * it, x_even)
        gather(jnp.minimum(unit + 2, units - 1), x_even)
        compute(unit + 1, 2 * it + 1, x_odd)
        return 0

    lax.fori_loop(0, per_step // 2, body, 0)

    @pl.when(step == pl.num_programs(0) - 1)
    def _():
        stiff = 0.5 * (acc[0] + acc[0].T)
        mass = 0.5 * (acc[1] + acc[1].T)
        row, col = iota((LANES, LANES), 0), iota((LANES, LANES), 1)
        out_ref[0:LANES, :] = jnp.where(row <= col, stiff, mass)
        diag = jnp.sum(jnp.where(row == col, mass, 0.0), axis=0, keepdims=True)
        out_ref[LANES : LANES + 8, :] = jnp.broadcast_to(diag, (8, LANES))


def invert_spd(gram):
    lane = iota((8, LANES), 1)
    sub = iota((8, LANES), 0)
    regs = [gram[8 * g : 8 * g + 8, :] for g in range(16)]
    for k in range(LANES):
        own, at = k // 8, k % 8
        row = regs[own][at : at + 1, :]
        inverse = 1.0 / row[:, k : k + 1]
        row = jnp.where(lane[:1] == k, inverse, row * inverse)
        row = jnp.broadcast_to(row, (8, LANES))
        here = lane == k
        for g in range(16):
            col = jnp.broadcast_to(regs[g][:, k : k + 1], (8, LANES))
            new = jnp.where(here, 0.0, regs[g]) - col * row
            regs[g] = jnp.where(sub == at, row, new) if g == own else new
    return jnp.concatenate(regs, axis=0)


def rims(column, scale):
    elems = column.shape[0]

    def summed(rows):
        return jnp.sum(rows.T, axis=0, keepdims=True) * scale

    def side(first):
        parts = [column[pl.ds(first + c, SIDE, stride=SIDE), :] for c in range(RIM)]
        parts.append(jnp.zeros((LANES - RIM * SIDE, LANES), F32))
        return summed(jnp.concatenate(parts, axis=0))

    top = summed(column[pl.ds(0, LANES), :])
    bottom = summed(column[pl.ds(elems - LANES, LANES), :])
    left, right = side(0), side(SIDE - RIM)
    return jnp.concatenate([top, top, top, left, right, bottom, bottom, bottom], axis=0)


def energy_kernel(
    scale, gram_ref, p_hbm, dens_ref, slot_ref, live_ref, sens_ref, tile_ref, ritz_ref, p_vmem, dcol, both, total, sems
):
    elems = dcol.shape[0]
    groups = elems // GROUP
    pieces = sems.shape[0]
    span = groups // pieces
    copies = [
        pltpu.make_async_copy(
            p_hbm.at[pl.ds(i * span, span)], p_vmem.at[pl.ds(i * span, span)], sems.at[i]
        )
        for i in range(pieces)
    ]
    for copy in copies:
        copy.start()
    density_columns(dens_ref, dcol)
    slots = slot_ref[...]
    live = live_ref[...]
    tile_dens = jnp.take_along_axis(rims(dcol, 1.0 / LANES), slots, axis=1) * live

    row, col = iota((LANES, LANES), 0), iota((LANES, LANES), 1)
    packed = gram_ref[0:LANES, :]
    above = jnp.where(row < col, packed, 0.0)
    below = jnp.where(row > col, packed, 0.0)
    stiff = above + above.T + jnp.where(row == col, packed, 0.0)
    mass = below + below.T + jnp.where(row == col, gram_ref[LANES : LANES + 1, :], 0.0)
    inv_mass = invert_spd(mass)
    ritz_ref[0, 0] = jnp.sum(inv_mass * stiff) * (1.0 / LANES)
    half = jnp.dot(inv_mass, stiff, precision=HIGHEST, preferred_element_type=F32)
    sandwich = jnp.dot(half, inv_mass, precision=HIGHEST, preferred_element_type=F32)
    both[...] = jnp.zeros_like(both)
    both[0:LANES, 0:LANES] = inv_mass.astype(BF16)
    both[LANES:, LANES:] = sandwich.astype(BF16)

    per_piece = span * GROUP // UNIT
    for i in range(pieces):
        copies[i].wait()

        def body(it, _, i=i):
            unit = i * per_piece + it
            stiffs = p_vmem[pl.ds(unit * 4, 4), 0:ROWS, :].reshape(4 * ROWS, LANES)
            masses = p_vmem[pl.ds(unit * 4, 4), ROWS:, :].reshape(4 * ROWS, LANES)
            inner = jnp.dot(
                jnp.concatenate([stiffs, masses], axis=1), both[...], preferred_element_type=F32
            )
            part_stiff = (inner[:, :LANES] * stiffs.astype(F32)).reshape(4, 24, 8, LANES).sum(axis=1)
            part_mass = (inner[:, LANES:] * masses.astype(F32)).reshape(4, 24, 8, LANES).sum(axis=1)
            at = pl.ds(pl.multiple_of(unit * UNIT, UNIT), UNIT)
            dens = dcol[at, :]
            total[at, :] = 3.0 * dens * dens * part_stiff.reshape(UNIT, LANES) - part_mass.reshape(UNIT, LANES)
            return 0

        lax.fori_loop(0, per_piece, body, 0)

    for j in range(elems // LANES):
        block = total[pl.ds(j * LANES, LANES), :]
        sens_ref[j : j + 1, :] = jnp.sum(block.T, axis=0, keepdims=True) * scale
    tile_sens = jnp.take_along_axis(rims(total, scale), slots, axis=1) * live
    tile_ref[...] = jnp.zeros_like(tile_ref)
    for ch, value in enumerate((live, tile_dens, tile_sens)):
        tile_ref[0, 3 * ch : 3 * ch + 3, :] = value[0:3]
        tile_ref[1, 3 * ch : 3 * ch + 3, :] = value[5:8]
        tile_ref[2, ch : ch + 1, :] = value[3:4]
        tile_ref[3, ch : ch + 1, :] = value[4:5]


def split3(value):
    high = value.astype(BF16)
    rest = value - high.astype(F32)
    mid = rest.astype(BF16)
    low = (rest - mid.astype(F32)).astype(BF16)
    return high, mid, low


def owner_kernel(up_ref, down_ref, left_ref, right_ref, target_ref, weight_ref, dens_ref, sens_ref, fdens_ref, fsens_ref):
    lane = iota((1, LANES), 1)

    def lanes_of(main, corner):
        return jnp.where(lane < 96, main, pltpu.roll(corner, 96, 1))

    values = [[], [], []]
    for ch in range(3):
        up = up_ref[3 * ch + 1 : 3 * ch + 2, :]
        down = down_ref[3 * ch + 1 : 3 * ch + 2, :]
        left = left_ref[3 * ch : 3 * ch + 3, :]
        right = right_ref[3 * ch : 3 * ch + 3, :]
        sides = (
            lanes_of(up, left[1:2]),
            lanes_of(down, left[2:3]),
            lanes_of(left[0:1], right[1:2]),
            lanes_of(right[0:1], right[2:3]),
        )
        for side in range(4):
            values[ch].append(sides[side] * weight_ref[side : side + 1, :])
    stacked = jnp.concatenate([jnp.concatenate(v, axis=1) for v in values], axis=0)
    high, mid, low = split3(stacked)
    left = jnp.concatenate([high, mid, low, jnp.zeros((7, 4 * LANES), BF16)], axis=0)
    targets = jnp.concatenate([target_ref[i : i + 1, :] for i in range(4)], axis=1)
    for j in range(dens_ref.shape[0]):
        hit = targets == iota((LANES, 4 * LANES), 0) + j * LANES
        hot = jnp.where(hit, 1.0, 0.0).astype(BF16)
        sums = lax.dot_general(left, hot, (((1,), (1,)), ((), ())), preferred_element_type=F32)
        sums = sums[0:3] + sums[3:6] + sums[6:9]
        under = 1.0 + sums[0:1]
        fdens_ref[j : j + 1, :] = (dens_ref[j : j + 1, :] + sums[1:2]) / under
        fsens_ref[j : j + 1, :] = (sens_ref[j : j + 1, :] + sums[2:3]) / under


def place(index, sizes):
    rows, cols = sizes
    return [index // cols // 2, index // cols % 2, index % cols // 4, index % 4]


def swapped(sizes, axis, step):
    rows, cols = sizes
    lengths = [rows // 2, 2, cols // 4, 4]
    pairs = []
    for i in range(rows * cols):
        at = place(i, sizes)
        at[axis] = (at[axis] + step) % lengths[axis]
        pairs.append((i, ((at[0] * 2 + at[1]) * lengths[2] + at[2]) * 4 + at[3]))
    return pairs


def sum_over_devices(value, sizes):
    value = value + lax.ppermute(value, AXES, swapped(sizes, 1, 1))
    lengths = [sizes[0] // 2, 2, sizes[1] // 4, 4]
    for axis in (3, 2, 0):
        others = [lax.ppermute(value, AXES, swapped(sizes, axis, s)) for s in range(1, lengths[axis])]
        for other in others:
            value = value + other
    return value


def torus(axis, step):
    size = lax.axis_size(axis)
    return [(i, (i + step) % size) for i in range(size)]


def per_device(
    block_vectors, connectivity, density, stiff_factor, mass_factor, send_slot, send_count, recv_target, recv_weight
):
    vec_count = block_vectors.shape[1]
    elems = density.shape[0]
    groups = elems // GROUP
    sizes = (lax.axis_size("gx"), lax.axis_size("gy"))
    scale = float(elems * sizes[0] * sizes[1]) / vec_count

    factors = jnp.stack([stiff_factor, mass_factor]).reshape(2, 24, 3, 8).transpose(0, 1, 3, 2).reshape(48, 24)
    eye = jnp.eye(GROUP, dtype=BF16)
    spread = (factors[:, None, None, :] * eye[None, :, :, None]).reshape(48 * GROUP, ROWS)
    conn_rows = (connectivity * 3).reshape(8 * elems)
    dens_rows = density.reshape(elems // LANES, LANES)

    steps = 9
    per_step = elems // UNIT // steps
    vmem = pl.BlockSpec(memory_space=pltpu.VMEM)
    smem = pl.BlockSpec(memory_space=pltpu.SMEM)
    proj, gram = pl.pallas_call(
        lambda *refs: gram_kernel(elems, per_step, *refs),
        grid=(steps,),
        out_shape=(
            jax.ShapeDtypeStruct((groups, 2 * ROWS, LANES), BF16),
            jax.ShapeDtypeStruct((LANES + 8, LANES), F32),
        ),
        in_specs=[smem, vmem, vmem, vmem],
        out_specs=(
            pl.BlockSpec((groups // steps, 2 * ROWS, LANES), lambda i: (i, 0, 0)),
            pl.BlockSpec((LANES + 8, LANES), lambda i: (0, 0)),
        ),
        scratch_shapes=[
            pltpu.VMEM((3 * elems + 24, LANES), F32),
            pltpu.VMEM((elems, LANES), F32),
            pltpu.VMEM((UNIT // 16, ROWS, 2 * LANES), BF16),
            pltpu.VMEM((UNIT // 16, ROWS, 2 * LANES), BF16),
            pltpu.VMEM((2, UNIT // GROUP, ROWS, LANES), BF16),
            pltpu.VMEM((2, LANES, LANES), F32),
        ],
        compiler_params=pltpu.CompilerParams(vmem_limit_bytes=VMEM_LIMIT),
        name="gram",
    )(conn_rows, block_vectors, dens_rows, spread)

    gram = sum_over_devices(gram, sizes)

    slots = send_slot[0]
    live = iota(slots.shape, 1) < send_count[0][:, None]
    row, col = slots // SIDE, slots % SIDE
    k = iota(slots.shape, 0)
    rim_place = jnp.where(
        k < 3,
        slots,
        jnp.where(
            k == 3,
            col * SIDE + row,
            jnp.where(k == 4, (col - (SIDE - RIM)) * SIDE + row, slots - (elems - LANES)),
        ),
    )
    pad = ((0, 0), (0, LANES - slots.shape[1]))
    rim_place = jnp.pad(jnp.where(live, rim_place, 0), pad)
    live = jnp.pad(live.astype(F32), pad)

    sens_rows, tiles, ritz = pl.pallas_call(
        lambda *refs: energy_kernel(scale, *refs),
        out_shape=(
            jax.ShapeDtypeStruct((elems // LANES, LANES), F32),
            jax.ShapeDtypeStruct((4, 16, LANES), F32),
            jax.ShapeDtypeStruct((1, 1), F32),
        ),
        in_specs=[vmem, pl.BlockSpec(memory_space=pl.ANY), vmem, vmem, vmem],
        out_specs=(vmem, vmem, smem),
        scratch_shapes=[
            pltpu.VMEM((groups, 2 * ROWS, LANES), BF16),
            pltpu.VMEM((elems, LANES), F32),
            pltpu.VMEM((2 * LANES, 2 * LANES), BF16),
            pltpu.VMEM((elems, LANES), F32),
            pltpu.SemaphoreType.DMA((6,)),
        ],
        compiler_params=pltpu.CompilerParams(vmem_limit_bytes=VMEM_LIMIT),
        name="energy",
    )(gram, proj, dens_rows, rim_place, live)

    up = lax.ppermute(tiles[0], "gx", torus("gx", -1))
    down = lax.ppermute(tiles[1], "gx", torus("gx", 1))
    to_left = jnp.stack([tiles[2, 0:3], up[0:9:3], down[0:9:3]], axis=1).reshape(9, LANES)
    to_right = jnp.stack([tiles[3, 0:3], up[2:9:3], down[2:9:3]], axis=1).reshape(9, LANES)
    left = lax.ppermute(to_left, "gy", torus("gy", -1))
    right = lax.ppermute(to_right, "gy", torus("gy", 1))

    def by_side(table):
        corner = LANES - table.shape[2]
        rows = [table[0, main : main + 1] for main in (1, 6, 3, 4)]
        ends = [table[0, k : k + 1, :corner] for k in (0, 5, 2, 7)]
        return jnp.concatenate(
            [jnp.concatenate(rows, axis=0), jnp.concatenate(ends, axis=0)], axis=1
        )

    fdens, fsens = pl.pallas_call(
        owner_kernel,
        out_shape=(jax.ShapeDtypeStruct((elems // LANES, LANES), F32),) * 2,
        in_specs=[vmem] * 8,
        out_specs=(vmem, vmem),
        name="owner",
    )(up, down, left, right, by_side(recv_target), by_side(recv_weight), dens_rows, sens_rows)
    return fdens.reshape(elems), fsens.reshape(elems), ritz.reshape(())


def solution(mesh):
    placed = (
        P(None, None, ("gx", "gy")),
        P(None, ("gx", "gy")),
        P(("gx", "gy")),
        P(),
        P(),
        P(("gx", "gy"), None, None),
        P(("gx", "gy"), None),
        P(("gx", "gy"), None, None),
        P(("gx", "gy"), None, None),
    )
    return jax.shard_map(
        per_device,
        mesh=mesh,
        in_specs=placed,
        out_specs=(P(("gx", "gy")), P(("gx", "gy")), P()),
        check_vma=False,
    )
```

time: 661 us -> 132 us (0.20); the launches traced: 652 us -> 131 us
  local copies, waits for them, and re-layouts: 357 us -> 9.59 us
  waiting for transfers between devices: 124 us -> 10.4 us
  Pallas kernels: 0 us -> 80.1 us
  matrix products: 42.6 us -> 0 us
  other arithmetic: 46.3 us -> 6.06 us
  starting transfers between devices: 58.4 us -> 24.3 us
  between operations: 21.3 us -> 0.72 us
    gather x22 -> x0, local copies, waits for them, and re-layouts: 269 us -> none  [the longest x18 260 us: project(): picked = vectors[:, :, conn_block]]
    psum x1 -> x0, waiting for transfers between devices: 121 us -> none  [per_device(): lax.psum((stiffness_gram_matrix, gram_mass), ('gx', 'gy'))]
    while x147 -> x0, local copies, waits for them, and re-layouts: 80.5 us -> none
    pallas_call x0 -> x3, Pallas kernels: none -> 80.1 us  [the longest x1 44.7 us: per_device(): pl.pallas_call(lambda *refs: gram_kernel(elems, per_step, *refs), grid=(s...]
    dot_general x56 -> x0, matrix products: 40.7 us -> none  [the longest x18 18.2 us: project(): jnp.dot(factors, picked, preferred_element_type=jnp.float32)]
    ppermute x16 -> x14, starting transfers between devices: 58.4 us -> 24.3 us  [the longest x9 18.3 us: sum_over_devices(): lax.ppermute(value, AXES, swapped(sizes, axis, s))]
    another operation x6 -> x2, other arithmetic: 22.9 us -> 0.01 us  [the longest x1 0.01 us: per_device(): jnp.stack([tiles[2, 0:3], up[0:9:3], down[0:9:3]], axis=1).reshape(9, LANES)]
    while x18 -> x0, other arithmetic: 12.6 us -> none
  transfers between devices with their start and end apart: 17 -> 14, of which waited for: 2 -> 9; matrix products, arithmetic and copies ran while one was open for 31% -> 6% of each run, Pallas kernels for 0% -> 0%
where the time goes in v1:
time: 132 us; the launch traced here: 131 us
  Pallas kernels  80.1 us (61%)
  starting transfers between devices  24.3 us (18%)
  waiting for transfers between devices  10.4 us (8%)
  local copies, waits for them, and re-layouts  9.59 us (7%)
  other arithmetic  6.06 us (5%)
    pallas_call x1, Pallas kernels, per_device(): pl.pallas_call(lambda *refs: gram_kernel(elems, per_step, *refs), grid=(s...  44.7 us
    pallas_call x1, Pallas kernels, per_device(): pl.pallas_call(lambda *refs: energy_kernel(scale, *refs), out_shape=(jax....  33.2 us
    ppermute x9, starting transfers between devices, sum_over_devices(): lax.ppermute(value, AXES, swapped(sizes, axis, s))  18.3 us
    ppermute x9, waiting for transfers between devices, sum_over_devices(): lax.ppermute(value, AXES, swapped(sizes, axis, s))  6.53 us
    ppermute x1, starting transfers between devices, per_device(): left = lax.ppermute(to_left, 'gy', torus('gy', -1))  4.33 us
    ppermute x1, waiting for transfers between devices, per_device(): down = lax.ppermute(tiles[1], 'gx', torus('gx', 1))  2.9 us
  transfers between devices with their start and end apart: 14, of which 9 were waited for; matrix products, arithmetic and copies ran while one was open for 6% of the time, Pallas kernels for 0%

profile of v1, /device:TPU:0, one launch (start us, length us, event | category | flops | bytes accessed | tf_op | source)
XLA Modules:
  0.0 131.2 jit_solution(4810693931342371423)
XLA Ops:
  0.6 0.8 copy.14
  1.4 0.8 copy.15
  2.2 0.1 mul.33
  2.3 0.1 copy.17
  2.4 0.1 broadcast_multiply_fusion
  2.5 1.2 mul.37.refs_3_
  3.7 0.9 broadcast_multiply_fusion.1
  4.6 0.6 reshape.46.refs_0_
  5.2 44.7 %gram.1 = (bf16[288,384,128]{2,1,0:T(8,128)(2,1)}, f32[136,128]{1,0:T(8,128)}) custom-call(s32[18432]{0:T(1024)} %reshape.46.refs_0_, bf16[3,128,2304]{2,1,0:T(8,128)(2,1)} %refs_1_.1, f32[18,128]{1,0:T(8,128)} %bitcast.87, bf16[384,192]{1,0:T(8,128)(2,1)} %mul.37.refs_3_), custom_call_target="tpu_custom_call" | custom-call | tf_op jit(solution)/shard_map/gram/pallas_call | solution.py:302
  49.9 0.8 slice_bitcast_fusion.19
  50.8 0.8 slice_bitcast_fusion.15
  51.6 0.8 slice_bitcast_fusion.11
  52.5 0.8 fusion.3
  53.2 0.8 slice_bitcast_fusion.7
  54.1 0.9 add.47
  55.0 1.7 %collective-permute-start.1 = (f32[136,128]{1,0:T(8,128)S(1)}, f32[136,128]{1,0:T(8,128)S(1)}, u32[]{:S(2)}, u32[]{:S(2)}) collective-permute-start(f32[136,128]{1,0:T(8,128)S(1)} %add.47), channel_id=1, source_target_pairs={{0,1},{1,2},{2,3},{3,0},{4,5},{5,6},{6,7},{7,4},{8,9},{9,10},{10,1... | collective-permute-start | bytes 208904 | tf_op jit(solution)/shard_map/ppermute | solution.py:272
  56.6 2.7 %collective-permute-start.2 = (f32[136,128]{1,0:T(8,128)S(1)}, f32[136,128]{1,0:T(8,128)S(1)}, u32[]{:S(2)}, u32[]{:S(2)}) collective-permute-start(f32[136,128]{1,0:T(8,128)S(1)} %add.47), channel_id=1, source_target_pairs={{0,2},{1,3},{2,0},{3,1},{4,6},{5,7},{6,4},{7,5},{8,10},{9,11},{10,... | collective-permute-start | bytes 208904 | tf_op jit(solution)/shard_map/ppermute | solution.py:272
  59.3 1.4 %collective-permute-start.3 = (f32[136,128]{1,0:T(8,128)S(1)}, f32[136,128]{1,0:T(8,128)S(1)}, u32[]{:S(2)}, u32[]{:S(2)}) collective-permute-start(f32[136,128]{1,0:T(8,128)S(1)} %add.47), channel_id=1, source_target_pairs={{0,3},{1,0},{2,1},{3,2},{4,7},{5,4},{6,5},{7,6},{8,11},{9,8},{10,9... | collective-permute-start | bytes 208904 | tf_op jit(solution)/shard_map/ppermute | solution.py:272
  60.8 0.7 iota_compare_fusion
  61.5 0.6 pad.10.refs_3_
  62.1 1.3 collective-permute-done.2
  63.4 0.3 collective-permute-done.3
  63.7 1.6 %collective-permute-start.4 = (f32[136,128]{1,0:T(8,128)S(1)}, f32[136,128]{1,0:T(8,128)S(1)}, u32[]{:S(2)}, u32[]{:S(2)}) collective-permute-start(f32[136,128]{1,0:T(8,128)S(1)} %add_add_fusion.2), channel_id=1, source_target_pairs={{0,4},{1,5},{2,6},{3,7},{4,8},{5,9},{6,10},{7,11},{8,12},{9,13},{1... | collective-permute-start | bytes 208904 | tf_op jit(solution)/shard_map/ppermute | solution.py:272
  65.3 2.9 %collective-permute-start.5 = (f32[136,128]{1,0:T(8,128)S(1)}, f32[136,128]{1,0:T(8,128)S(1)}, u32[]{:S(2)}, u32[]{:S(2)}) collective-permute-start(f32[136,128]{1,0:T(8,128)S(1)} %add_add_fusion.2), channel_id=1, source_target_pairs={{0,8},{1,9},{2,10},{3,11},{4,12},{5,13},{6,14},{7,15},{8,0},{9,1},... | collective-permute-start | bytes 208904 | tf_op jit(solution)/shard_map/ppermute | solution.py:272
  68.3 1.3 %collective-permute-start.6 = (f32[136,128]{1,0:T(8,128)S(1)}, f32[136,128]{1,0:T(8,128)S(1)}, u32[]{:S(2)}, u32[]{:S(2)}) collective-permute-start(f32[136,128]{1,0:T(8,128)S(1)} %add_add_fusion.2), channel_id=1, source_target_pairs={{0,12},{1,13},{2,14},{3,15},{4,0},{5,1},{6,2},{7,3},{8,4},{9,5},{1... | collective-permute-start | bytes 208904 | tf_op jit(solution)/shard_map/ppermute | solution.py:272
  69.6 0.6 pad_convert_fusion.refs_4_
  70.2 1.1 collective-permute-done.5
  71.3 1.3 collective-permute-done.6
  72.6 2.0 %collective-permute-start.7 = (f32[136,128]{1,0:T(8,128)S(1)}, f32[136,128]{1,0:T(8,128)S(1)}, u32[]{:S(2)}, u32[]{:S(2)}) collective-permute-start(f32[136,128]{1,0:T(8,128)S(1)} %add_add_fusion.1), channel_id=1, source_target_pairs={{0,32},{1,33},{2,34},{3,35},{4,36},{5,37},{6,38},{7,39},{8,40},{9,... | collective-permute-start | bytes 208904 | tf_op jit(solution)/shard_map/ppermute | solution.py:272
  74.5 3.6 %collective-permute-start.8 = (f32[136,128]{1,0:T(8,128)S(1)}, f32[136,128]{1,0:T(8,128)S(1)}, u32[]{:S(2)}, u32[]{:S(2)}) collective-permute-start(f32[136,128]{1,0:T(8,128)S(1)} %add_add_fusion.1), channel_id=1, source_target_pairs={{0,64},{1,65},{2,66},{3,67},{4,68},{5,69},{6,70},{7,71},{8,72},{9,... | collective-permute-start | bytes 208904 | tf_op jit(solution)/shard_map/ppermute | solution.py:272
  78.1 1.1 collective-permute-start.9
  79.2 0.7 add_add_fusion.3.target_ref
  79.8 1.3 collective-permute-done.8
  81.1 1.3 collective-permute-done.9
  82.4 0.6 add_add_fusion.refs_0_
  83.1 33.2 %energy.1 = (f32[18,128]{1,0:T(8,128)}, f32[4,16,128]{2,1,0:T(8,128)}, f32[1,1]{1,0:T(1,128)}) custom-call(f32[136,128]{1,0:T(8,128)} %add_add_fusion.refs_0_, bf16[288,384,128]{2,1,0:T(8,128)(2,1)} %get-tuple-element.11.refs_1_, f32[18,128]{1,0:T(8,128)} %bitcast.88, s32[8,128]{1,0:T(8,128)} %pad.10.refs_3_, f32[8,128]{1,0:T(8,128)} %pad_convert_fusion.refs_4_), custom_call_target="tpu_custom_call" | custom-call | tf_op jit(solution)/shard_map/energy/pallas_call | solution.py:345
  116.3 0.7 slice_bitcast_fusion
  117.0 0.5 collective-permute-start.11
  117.5 0.7 slice_bitcast_fusion.2
  118.2 0.2 collective-permute-done.10.up_ref
  118.4 2.9 %collective-permute-done.11.down_ref = f32[16,128]{1,0:T(8,128)S(1)} collective-permute-done((f32[16,128]{1,0:T(8,128)S(1)}, f32[16,128]{1,0:T(8,128)S(1)}, u32[]{:S(2)}, u32[]{:S(2)}) %collective-permute-start.11) | collective-permute-done | bytes 8224 | tf_op jit(solution)/shard_map/ppermute | solution.py:366
  121.3 1.1 collective-permute-start.13
  122.6 4.3 %collective-permute-start.12 = (f32[9,128]{1,0:T(8,128)S(1)}, f32[9,128]{1,0:T(8,128)S(1)}, u32[]{:S(2)}, u32[]{:S(2)}) collective-permute-start(f32[9,128]{1,0:T(8,128)S(1)} %reshape.48), channel_id=1, source_target_pairs={{0,15},{1,0},{2,1},{3,2},{4,3},{5,4},{6,5},{7,6},{8,7},{9,8},{10,9... | collective-permute-start | bytes 13832 | tf_op jit(solution)/shard_map/ppermute | solution.py:369
  126.9 0.7 maximum_maximum_fusion.weight_ref
  127.6 0.8 collective-permute-done.13.right_ref
  128.4 0.6 copy-done.2
  129.0 0.0 copy-done.3
  129.0 2.2 %owner.1 = (f32[18,128]{1,0:T(8,128)}, f32[18,128]{1,0:T(8,128)}) custom-call(f32[16,128]{1,0:T(8,128)} %copy-done, f32[16,128]{1,0:T(8,128)} %copy-done.1, f32[9,128]{1,0:T(8,128)} %copy-done.3, f32[9,128]{1,0:T(8,128)} %copy-done.2, s32[4,128]{1,0:T(4,128)} %add_add_fusion.3.target_ref, f32[4,128]{1,0:T(4,128)} %maximum_maximum_fusion.weight_ref, ...), custom_call_target="tpu_custom_call" | custom-call | tf_op jit(solution)/shard_map/owner/pallas_call | solution.py:380
  (30 shorter events, 0.2 us)
Async XLA Ops:
  49.9 4.1 %collective-permute-start = (f32[136,128]{1,0:T(8,128)}, f32[136,128]{1,0:T(8,128)S(1)}, u32[]{:S(2)}, u32[]{:S(2)}) collective-permute-start(f32[136,128]{1,0:T(8,128)} %get-tuple-element.10), channel_id=1, source_target_pairs={{0,16},{1,17},{2,18},{3,19},{4,20},{5,21},{6,22},{7,23},{8,24},{9,... | collective-permute-start | bytes 208904 | tf_op jit(solution)/shard_map/ppermute | solution.py:269
  55.0 7.1 %collective-permute-start.1 = (f32[136,128]{1,0:T(8,128)S(1)}, f32[136,128]{1,0:T(8,128)S(1)}, u32[]{:S(2)}, u32[]{:S(2)}) collective-permute-start(f32[136,128]{1,0:T(8,128)S(1)} %add.47), channel_id=1, source_target_pairs={{0,1},{1,2},{2,3},{3,0},{4,5},{5,6},{6,7},{7,4},{8,9},{9,10},{10,1... | collective-permute-start | bytes 208904 | tf_op jit(solution)/shard_map/ppermute | solution.py:272
  56.6 6.8 %collective-permute-start.2 = (f32[136,128]{1,0:T(8,128)S(1)}, f32[136,128]{1,0:T(8,128)S(1)}, u32[]{:S(2)}, u32[]{:S(2)}) collective-permute-start(f32[136,128]{1,0:T(8,128)S(1)} %add.47), channel_id=1, source_target_pairs={{0,2},{1,3},{2,0},{3,1},{4,6},{5,7},{6,4},{7,5},{8,10},{9,11},{10,... | collective-permute-start | bytes 208904 | tf_op jit(solution)/shard_map/ppermute | solution.py:272
  59.3 4.3 %collective-permute-start.3 = (f32[136,128]{1,0:T(8,128)S(1)}, f32[136,128]{1,0:T(8,128)S(1)}, u32[]{:S(2)}, u32[]{:S(2)}) collective-permute-start(f32[136,128]{1,0:T(8,128)S(1)} %add.47), channel_id=1, source_target_pairs={{0,3},{1,0},{2,1},{3,2},{4,7},{5,4},{6,5},{7,6},{8,11},{9,8},{10,9... | collective-permute-start | bytes 208904 | tf_op jit(solution)/shard_map/ppermute | solution.py:272
  63.7 6.5 %collective-permute-start.4 = (f32[136,128]{1,0:T(8,128)S(1)}, f32[136,128]{1,0:T(8,128)S(1)}, u32[]{:S(2)}, u32[]{:S(2)}) collective-permute-start(f32[136,128]{1,0:T(8,128)S(1)} %add_add_fusion.2), channel_id=1, source_target_pairs={{0,4},{1,5},{2,6},{3,7},{4,8},{5,9},{6,10},{7,11},{8,12},{9,13},{1... | collective-permute-start | bytes 208904 | tf_op jit(solution)/shard_map/ppermute | solution.py:272
  65.3 6.0 %collective-permute-start.5 = (f32[136,128]{1,0:T(8,128)S(1)}, f32[136,128]{1,0:T(8,128)S(1)}, u32[]{:S(2)}, u32[]{:S(2)}) collective-permute-start(f32[136,128]{1,0:T(8,128)S(1)} %add_add_fusion.2), channel_id=1, source_target_pairs={{0,8},{1,9},{2,10},{3,11},{4,12},{5,13},{6,14},{7,15},{8,0},{9,1},... | collective-permute-start | bytes 208904 | tf_op jit(solution)/shard_map/ppermute | solution.py:272
  68.3 4.3 %collective-permute-start.6 = (f32[136,128]{1,0:T(8,128)S(1)}, f32[136,128]{1,0:T(8,128)S(1)}, u32[]{:S(2)}, u32[]{:S(2)}) collective-permute-start(f32[136,128]{1,0:T(8,128)S(1)} %add_add_fusion.2), channel_id=1, source_target_pairs={{0,12},{1,13},{2,14},{3,15},{4,0},{5,1},{6,2},{7,3},{8,4},{9,5},{1... | collective-permute-start | bytes 208904 | tf_op jit(solution)/shard_map/ppermute | solution.py:272
  72.6 7.2 %collective-permute-start.7 = (f32[136,128]{1,0:T(8,128)S(1)}, f32[136,128]{1,0:T(8,128)S(1)}, u32[]{:S(2)}, u32[]{:S(2)}) collective-permute-start(f32[136,128]{1,0:T(8,128)S(1)} %add_add_fusion.1), channel_id=1, source_target_pairs={{0,32},{1,33},{2,34},{3,35},{4,36},{5,37},{6,38},{7,39},{8,40},{9,... | collective-permute-start | bytes 208904 | tf_op jit(solution)/shard_map/ppermute | solution.py:272
  74.5 6.6 %collective-permute-start.8 = (f32[136,128]{1,0:T(8,128)S(1)}, f32[136,128]{1,0:T(8,128)S(1)}, u32[]{:S(2)}, u32[]{:S(2)}) collective-permute-start(f32[136,128]{1,0:T(8,128)S(1)} %add_add_fusion.1), channel_id=1, source_target_pairs={{0,64},{1,65},{2,66},{3,67},{4,68},{5,69},{6,70},{7,71},{8,72},{9,... | collective-permute-start | bytes 208904 | tf_op jit(solution)/shard_map/ppermute | solution.py:272
  78.1 4.3 %collective-permute-start.9 = (f32[136,128]{1,0:T(8,128)S(1)}, f32[136,128]{1,0:T(8,128)S(1)}, u32[]{:S(2)}, u32[]{:S(2)}) collective-permute-start(f32[136,128]{1,0:T(8,128)S(1)} %add_add_fusion.1), channel_id=1, source_target_pairs={{0,96},{1,97},{2,98},{3,99},{4,100},{5,101},{6,102},{7,103},{8,104... | collective-permute-start | bytes 208904 | tf_op jit(solution)/shard_map/ppermute | solution.py:272
  117.0 1.4 %collective-permute-start.10 = (f32[16,128]{1,0:T(8,128)S(1)}, f32[16,128]{1,0:T(8,128)S(1)}, u32[]{:S(2)}, u32[]{:S(2)}) collective-permute-start(f32[16,128]{1,0:T(8,128)S(1)} %get-tuple-element.20), channel_id=1, source_target_pairs={{0,112},{16,0},{32,16},{48,32},{64,48},{80,64},{96,80},{112,96},{1... | collective-permute-start | bytes 24584 | tf_op jit(solution)/shard_map/ppermute | solution.py:365
  117.0 4.3 %collective-permute-start.11 = (f32[16,128]{1,0:T(8,128)S(1)}, f32[16,128]{1,0:T(8,128)S(1)}, u32[]{:S(2)}, u32[]{:S(2)}) collective-permute-start(f32[16,128]{1,0:T(8,128)S(1)} %get-tuple-element.19), channel_id=1, source_target_pairs={{0,16},{16,32},{32,48},{48,64},{64,80},{80,96},{96,112},{112,0},{1... | collective-permute-start | bytes 24584 | tf_op jit(solution)/shard_map/ppermute | solution.py:366
  118.4 10.0 %copy-start = (f32[16,128]{1,0:T(8,128)}, f32[16,128]{1,0:T(8,128)S(1)}, u32[]{:S(2)}) copy-start(f32[16,128]{1,0:T(8,128)S(1)} %collective-permute-done.10.up_ref) | copy-start | bytes 24580
  121.3 7.1 %copy-start.1 = (f32[16,128]{1,0:T(8,128)}, f32[16,128]{1,0:T(8,128)S(1)}, u32[]{:S(2)}) copy-start(f32[16,128]{1,0:T(8,128)S(1)} %collective-permute-done.11.down_ref) | copy-start | bytes 24580
  121.3 7.0 %collective-permute-start.13 = (f32[9,128]{1,0:T(8,128)S(1)}, f32[9,128]{1,0:T(8,128)S(1)}, u32[]{:S(2)}, u32[]{:S(2)}) collective-permute-start(f32[9,128]{1,0:T(8,128)S(1)} %reshape.49), channel_id=1, source_target_pairs={{0,1},{1,2},{2,3},{3,4},{4,5},{5,6},{6,7},{7,8},{8,9},{9,10},{10,1... | collective-permute-start | bytes 13832 | tf_op jit(solution)/shard_map/ppermute | solution.py:370
  122.6 5.8 %collective-permute-start.12 = (f32[9,128]{1,0:T(8,128)S(1)}, f32[9,128]{1,0:T(8,128)S(1)}, u32[]{:S(2)}, u32[]{:S(2)}) collective-permute-start(f32[9,128]{1,0:T(8,128)S(1)} %reshape.48), channel_id=1, source_target_pairs={{0,15},{1,0},{2,1},{3,2},{4,3},{5,4},{6,5},{7,6},{8,7},{9,8},{10,9... | collective-permute-start | bytes 13832 | tf_op jit(solution)/shard_map/ppermute | solution.py:369
  128.4 0.6 copy-start.2
  128.4 0.6 copy-start.3

commit v2 on v1

--- a/solution.py
+++ b/solution.py
@@ -35,22 +35,38 @@
 )
 
 
+def spread(factor):
+    dofs = factor.shape[0]
+    wide, tall = (ROWS, dofs), (dofs, ROWS)
+    take_row = (iota(wide, 0) >> 3) == iota(wide, 1)
+    out = iota(tall, 1)
+    within = lax.rem(out, dofs)
+    corner = within // 3
+    take_col = (within - 3 * corner) * 8 + corner == iota(tall, 0)
+    picked = jnp.dot(jnp.where(take_row, 1.0, 0.0).astype(BF16), factor, preferred_element_type=F32)
+    full = jnp.dot(picked.astype(BF16), jnp.where(take_col, 1.0, 0.0).astype(BF16), preferred_element_type=F32)
+    square = (ROWS, ROWS)
+    same = (iota(square, 0) & 7) == iota(square, 1) // dofs
+    return jnp.where(same, full, 0.0).astype(BF16)
+
+
 def gram_kernel(
-    elems, per_step, conn_ref, vec_ref, dens_ref, w_ref, p_ref, out_ref, table, dcol, x_even, x_odd, weighted, acc
+    elems, per_step, conn_ref, vec_ref, dens_ref, stiff_ref, mass_ref, p_ref, out_ref,
+    table, dcol, w_ref, tripled, rows_smem, x_even, x_odd, k_even, k_odd, acc, sem
 ):
     step = pl.program_id(0)
     units = elems // UNIT
     sub = iota((8, LANES), 0)
 
-    def gather(unit, xbuf):
+    def gather(unit, xbuf, qs=tuple(range(UNIT // 16))):
         base = unit * UNIT
-        for q in range(UNIT // 16):
+        for q in qs:
             for h in range(2):
                 for pair in range(4):
                     regs = []
                     for e in range(2):
                         at = base + (q * 16 + h * 8 + pair * 2 + e)
-                        rows = [conn_ref[a * elems + at] for a in range(8)]
+                        rows = [rows_smem[a * elems + at] for a in range(8)]
                         for pieces in PIECES:
                             value = None
                             for corner, first in pieces:
@@ -62,16 +78,27 @@
 
     @pl.when(step == 0)
     def _():
+        tripled[...] = conn_ref[...] * 3
+        copies = [
+            pltpu.make_async_copy(tripled.at[a], rows_smem.at[pl.ds(a * elems, elems)], sem.at[a]) for a in range(8)
+        ]
+        for copy in copies:
+            copy.start()
+        w_ref[0:ROWS] = spread(stiff_ref[...])
+        w_ref[ROWS:] = spread(mass_ref[...])
         for c in range(3):
             for j in range(elems // LANES):
                 block = vec_ref[c, :, pl.ds(j * LANES, LANES)].astype(F32).T
                 table[pl.ds(8 + 3 * LANES * j + c, LANES, stride=3), :] = block
         density_columns(dens_ref, dcol)
         acc[...] = jnp.zeros_like(acc)
+        k_odd[...] = jnp.zeros_like(k_odd)
+        for copy in copies:
+            copy.wait()
         gather(0, x_even)
 
-    def compute(unit, local, xbuf):
-        for q in range(UNIT // 16):
+    def project(unit, local, xbuf, kept, qs):
+        for q in qs:
             full = jnp.dot(w_ref[...], xbuf[q], preferred_element_type=F32).astype(BF16)
             for h in range(2):
                 part = full[:, h * LANES : (h + 1) * LANES]
@@ -79,25 +106,35 @@
                 p_ref[local * 4 + chunk] = part
                 wide = part.astype(F32).reshape(2, 24, 8, LANES)
                 dens = dcol[pl.ds(pl.multiple_of(unit * UNIT + chunk * 8, 8), 8), :]
-                weighted[0, chunk] = (wide[0] * (dens * dens * dens)[None]).reshape(ROWS, LANES).astype(BF16)
-                weighted[1, chunk] = (wide[1] * dens[None]).reshape(ROWS, LANES).astype(BF16)
-        for kind in range(2):
-            left = weighted[kind].reshape(4 * ROWS, LANES)
-            right = p_ref[pl.ds(local * 4, 4), pl.ds(kind * ROWS, ROWS), :].reshape(4 * ROWS, LANES)
-            acc[kind] += lax.dot_general(left, right, (((0,), (0,)), ((), ())), preferred_element_type=F32)
+                for kind, factor in enumerate((dens * dens * dens, dens)):
+                    kept[kind, chunk] = part[kind * ROWS : (kind + 1) * ROWS]
+                    kept[2 + kind, chunk] = (wide[kind] * factor[None]).reshape(ROWS, LANES).astype(BF16)
+
+    def add_grams(kept):
+        left = jnp.concatenate([kept[2 + kind].reshape(4 * ROWS, LANES) for kind in range(2)], axis=1)
+        right = jnp.concatenate([kept[kind].reshape(4 * ROWS, LANES) for kind in range(2)], axis=1)
+        full = lax.dot_general(left, right, (((0,), (0,)), ((), ())), preferred_element_type=F32)
+        acc[0] += full[:LANES, :LANES]
+        acc[1] += full[LANES:, LANES:]
 
     def body(it, _):
         unit = step * per_step + 2 * it
-        gather(unit + 1, x_odd)
-        compute(unit, 2 * it, x_even)
-        gather(jnp.minimum(unit + 2, units - 1), x_even)
-        compute(unit + 1, 2 * it + 1, x_odd)
+        for q in range(UNIT // 16):
+            gather(unit + 1, x_odd, (q,))
+            project(unit, 2 * it, x_even, k_even, (q,))
+        add_grams(k_odd)
+        after = jnp.minimum(unit + 2, units - 1)
+        for q in range(UNIT // 16):
+            gather(after, x_even, (q,))
+            project(unit + 1, 2 * it + 1, x_odd, k_odd, (q,))
+        add_grams(k_even)
         return 0
 
     lax.fori_loop(0, per_step // 2, body, 0)
 
     @pl.when(step == pl.num_programs(0) - 1)
     def _():
+        add_grams(k_odd)
         stiff = 0.5 * (acc[0] + acc[0].T)
         mass = 0.5 * (acc[1] + acc[1].T)
         row, col = iota((LANES, LANES), 0), iota((LANES, LANES), 1)
@@ -141,8 +178,21 @@
     return jnp.concatenate([top, top, top, left, right, bottom, bottom, bottom], axis=0)
 
 
+def rim_places(slots, count_ref, elems):
+    slots = jnp.concatenate([slots, jnp.zeros((8, LANES - slots.shape[1]), jnp.int32)], axis=1)
+    lane = iota((1, LANES), 1)
+    row = slots // SIDE
+    col = slots - row * SIDE
+    k = iota(slots.shape, 0)
+    across = jnp.where(k == 3, col, col - (SIDE - RIM)) * SIDE + row
+    place = jnp.where(k < 3, slots, jnp.where(k < 5, across, slots - (elems - LANES)))
+    live = jnp.concatenate([jnp.where(lane < count_ref[0, d], 1.0, 0.0) for d in range(8)], axis=0)
+    return jnp.where(live > 0.0, place, 0), live
+
+
 def energy_kernel(
-    scale, gram_ref, p_hbm, dens_ref, slot_ref, live_ref, sens_ref, tile_ref, ritz_ref, p_vmem, dcol, both, total, sems
+    scale, gram_ref, p_hbm, dens_ref, slot_ref, count_ref, sens_ref, up_ref, down_ref, left_ref, right_ref, ritz_ref,
+    p_vmem, dcol, both, total, sems
 ):
     elems = dcol.shape[0]
     groups = elems // GROUP
@@ -157,8 +207,7 @@
     for copy in copies:
         copy.start()
     density_columns(dens_ref, dcol)
-    slots = slot_ref[...]
-    live = live_ref[...]
+    slots, live = rim_places(slot_ref[...], count_ref, elems)
     tile_dens = jnp.take_along_axis(rims(dcol, 1.0 / LANES), slots, axis=1) * live
 
     row, col = iota((LANES, LANES), 0), iota((LANES, LANES), 1)
@@ -193,18 +242,91 @@
             total[at, :] = 3.0 * dens * dens * part_stiff.reshape(UNIT, LANES) - part_mass.reshape(UNIT, LANES)
             return 0
 
-        lax.fori_loop(0, per_piece, body, 0)
+        lax.fori_loop(0, per_piece, body, 0, unroll=6)
 
     for j in range(elems // LANES):
         block = total[pl.ds(j * LANES, LANES), :]
         sens_ref[j : j + 1, :] = jnp.sum(block.T, axis=0, keepdims=True) * scale
     tile_sens = jnp.take_along_axis(rims(total, scale), slots, axis=1) * live
-    tile_ref[...] = jnp.zeros_like(tile_ref)
-    for ch, value in enumerate((live, tile_dens, tile_sens)):
-        tile_ref[0, 3 * ch : 3 * ch + 3, :] = value[0:3]
-        tile_ref[1, 3 * ch : 3 * ch + 3, :] = value[5:8]
-        tile_ref[2, ch : ch + 1, :] = value[3:4]
-        tile_ref[3, ch : ch + 1, :] = value[4:5]
+    for ref, first, count in ((up_ref, 0, 3), (down_ref, 5, 3), (left_ref, 3, 1), (right_ref, 4, 1)):
+        ref[...] = jnp.zeros_like(ref)
+        for ch, value in enumerate((live, tile_dens, tile_sens)):
+            ref[count * ch : count * ch + count, :] = value[first : first + count]
+
+
+def pass_kernel(up_ref, down_ref, left_ref, right_ref, to_left_ref, to_right_ref):
+    for out, own, at in ((to_left_ref, left_ref, 0), (to_right_ref, right_ref, 2)):
+        out[...] = jnp.zeros_like(out)
+        for ch in range(3):
+            out[3 * ch : 3 * ch + 1, :] = own[ch : ch + 1, :]
+            out[3 * ch + 1 : 3 * ch + 2, :] = up_ref[3 * ch + at : 3 * ch + at + 1, :]
+            out[3 * ch + 2 : 3 * ch + 3, :] = down_ref[3 * ch + at : 3 * ch + at + 1, :]
+
+
+def project_and_gram(connectivity, block_vectors, dens_rows, stiff_factor, mass_factor):
+    elems = dens_rows.size
+    groups = elems // GROUP
+    steps = 9
+    per_step = elems // UNIT // steps
+    vmem = pl.BlockSpec(memory_space=pltpu.VMEM)
+    smem = pl.BlockSpec(memory_space=pltpu.SMEM)
+    return pl.pallas_call(
+        lambda *refs: gram_kernel(elems, per_step, *refs),
+        grid=(steps,),
+        out_shape=(
+            jax.ShapeDtypeStruct((groups, 2 * ROWS, LANES), BF16),
+            jax.ShapeDtypeStruct((LANES + 8, LANES), F32),
+        ),
+        in_specs=[vmem] * 5,
+        out_specs=(
+            pl.BlockSpec((groups // steps, 2 * ROWS, LANES), lambda i: (i, 0, 0)),
+            pl.BlockSpec((LANES + 8, LANES), lambda i: (0, 0)),
+        ),
+        scratch_shapes=[
+            pltpu.VMEM((3 * elems + 24, LANES), F32),
+            pltpu.VMEM((elems, LANES), F32),
+            pltpu.VMEM((2 * ROWS, ROWS), BF16),
+            pltpu.VMEM((8, elems), jnp.int32),
+            pltpu.SMEM((8 * elems,), jnp.int32),
+            pltpu.VMEM((UNIT // 16, ROWS, 2 * LANES), BF16),
+            pltpu.VMEM((UNIT // 16, ROWS, 2 * LANES), BF16),
+            pltpu.VMEM((4, UNIT // GROUP, ROWS, LANES), BF16),
+            pltpu.VMEM((4, UNIT // GROUP, ROWS, LANES), BF16),
+            pltpu.VMEM((2, LANES, LANES), F32),
+            pltpu.SemaphoreType.DMA((8,)),
+        ],
+        compiler_params=pltpu.CompilerParams(vmem_limit_bytes=VMEM_LIMIT),
+        name="gram",
+    )(connectivity, block_vectors, dens_rows, stiff_factor, mass_factor)
+
+
+def energies(scale, gram, proj, dens_rows, send_slot, send_count):
+    elems = dens_rows.size
+    groups = elems // GROUP
+    vmem = pl.BlockSpec(memory_space=pltpu.VMEM)
+    smem = pl.BlockSpec(memory_space=pltpu.SMEM)
+    return pl.pallas_call(
+        lambda *refs: energy_kernel(scale, *refs),
+        out_shape=(
+            jax.ShapeDtypeStruct((elems // LANES, LANES), F32),
+            jax.ShapeDtypeStruct((16, LANES), F32),
+            jax.ShapeDtypeStruct((16, LANES), F32),
+            jax.ShapeDtypeStruct((8, LANES), F32),
+            jax.ShapeDtypeStruct((8, LANES), F32),
+            jax.ShapeDtypeStruct((1, 1), F32),
+        ),
+        in_specs=[vmem, pl.BlockSpec(memory_space=pl.ANY), vmem, vmem, smem],
+        out_specs=(vmem,) * 5 + (smem,),
+        scratch_shapes=[
+            pltpu.VMEM((groups, 2 * ROWS, LANES), BF16),
+            pltpu.VMEM((elems, LANES), F32),
+            pltpu.VMEM((2 * LANES, 2 * LANES), BF16),
+            pltpu.VMEM((elems, LANES), F32),
+            pltpu.SemaphoreType.DMA((6,)),
+        ],
+        compiler_params=pltpu.CompilerParams(vmem_limit_bytes=VMEM_LIMIT),
+        name="energy",
+    )(gram, proj, dens_rows, send_slot, send_count)
 
 
 def split3(value):
@@ -221,6 +343,13 @@
     def lanes_of(main, corner):
         return jnp.where(lane < 96, main, pltpu.roll(corner, 96, 1))
 
+    def by_side(table):
+        table = jnp.concatenate([table, jnp.zeros((8, LANES - table.shape[1]), table.dtype)], axis=1)
+        pairs = ((1, 0), (6, 5), (3, 2), (4, 7))
+        return [lanes_of(table[m : m + 1], table[c : c + 1]) for m, c in pairs]
+
+    weights = by_side(weight_ref[...])
+    targets = jnp.concatenate(by_side(target_ref[...]), axis=1)
     values = [[], [], []]
     for ch in range(3):
         up = up_ref[3 * ch + 1 : 3 * ch + 2, :]
@@ -234,11 +363,10 @@
             lanes_of(right[0:1], right[2:3]),
         )
         for side in range(4):
-            values[ch].append(sides[side] * weight_ref[side : side + 1, :])
+            values[ch].append(sides[side] * weights[side])
     stacked = jnp.concatenate([jnp.concatenate(v, axis=1) for v in values], axis=0)
     high, mid, low = split3(stacked)
     left = jnp.concatenate([high, mid, low, jnp.zeros((7, 4 * LANES), BF16)], axis=0)
-    targets = jnp.concatenate([target_ref[i : i + 1, :] for i in range(4)], axis=1)
     for j in range(dens_ref.shape[0]):
         hit = targets == iota((LANES, 4 * LANES), 0) + j * LANES
         hot = jnp.where(hit, 1.0, 0.0).astype(BF16)
@@ -285,97 +413,28 @@
 ):
     vec_count = block_vectors.shape[1]
     elems = density.shape[0]
-    groups = elems // GROUP
     sizes = (lax.axis_size("gx"), lax.axis_size("gy"))
     scale = float(elems * sizes[0] * sizes[1]) / vec_count
 
-    factors = jnp.stack([stiff_factor, mass_factor]).reshape(2, 24, 3, 8).transpose(0, 1, 3, 2).reshape(48, 24)
-    eye = jnp.eye(GROUP, dtype=BF16)
-    spread = (factors[:, None, None, :] * eye[None, :, :, None]).reshape(48 * GROUP, ROWS)
-    conn_rows = (connectivity * 3).reshape(8 * elems)
     dens_rows = density.reshape(elems // LANES, LANES)
 
-    steps = 9
-    per_step = elems // UNIT // steps
+    proj, gram = project_and_gram(connectivity, block_vectors, dens_rows, stiff_factor, mass_factor)
+    gram = sum_over_devices(gram, sizes)
+
+    sens_rows, up, down, left, right, ritz = energies(scale, gram, proj, dens_rows, send_slot[0], send_count)
+
+    up = lax.ppermute(up, "gx", torus("gx", -1))
+    down = lax.ppermute(down, "gx", torus("gx", 1))
     vmem = pl.BlockSpec(memory_space=pltpu.VMEM)
-    smem = pl.BlockSpec(memory_space=pltpu.SMEM)
-    proj, gram = pl.pallas_call(
-        lambda *refs: gram_kernel(elems, per_step, *refs),
-        grid=(steps,),
-        out_shape=(
-            jax.ShapeDtypeStruct((groups, 2 * ROWS, LANES), BF16),
-            jax.ShapeDtypeStruct((LANES + 8, LANES), F32),
-        ),
-        in_specs=[smem, vmem, vmem, vmem],
-        out_specs=(
-            pl.BlockSpec((groups // steps, 2 * ROWS, LANES), lambda i: (i, 0, 0)),
-            pl.BlockSpec((LANES + 8, LANES), lambda i: (0, 0)),
-        ),
-        scratch_shapes=[
-            pltpu.VMEM((3 * elems + 24, LANES), F32),
-            pltpu.VMEM((elems, LANES), F32),
-            pltpu.VMEM((UNIT // 16, ROWS, 2 * LANES), BF16),
-            pltpu.VMEM((UNIT // 16, ROWS, 2 * LANES), BF16),
-            pltpu.VMEM((2, UNIT // GROUP, ROWS, LANES), BF16),
-            pltpu.VMEM((2, LANES, LANES), F32),
-        ],
-        compiler_params=pltpu.CompilerParams(vmem_limit_bytes=VMEM_LIMIT),
-        name="gram",
-    )(conn_rows, block_vectors, dens_rows, spread)
-
-    gram = sum_over_devices(gram, sizes)
-
-    slots = send_slot[0]
-    live = iota(slots.shape, 1) < send_count[0][:, None]
-    row, col = slots // SIDE, slots % SIDE
-    k = iota(slots.shape, 0)
-    rim_place = jnp.where(
-        k < 3,
-        slots,
-        jnp.where(
-            k == 3,
-            col * SIDE + row,
-            jnp.where(k == 4, (col - (SIDE - RIM)) * SIDE + row, slots - (elems - LANES)),
-        ),
-    )
-    pad = ((0, 0), (0, LANES - slots.shape[1]))
-    rim_place = jnp.pad(jnp.where(live, rim_place, 0), pad)
-    live = jnp.pad(live.astype(F32), pad)
-
-    sens_rows, tiles, ritz = pl.pallas_call(
-        lambda *refs: energy_kernel(scale, *refs),
-        out_shape=(
-            jax.ShapeDtypeStruct((elems // LANES, LANES), F32),
-            jax.ShapeDtypeStruct((4, 16, LANES), F32),
-            jax.ShapeDtypeStruct((1, 1), F32),
-        ),
-        in_specs=[vmem, pl.BlockSpec(memory_space=pl.ANY), vmem, vmem, vmem],
-        out_specs=(vmem, vmem, smem),
-        scratch_shapes=[
-            pltpu.VMEM((groups, 2 * ROWS, LANES), BF16),
-            pltpu.VMEM((elems, LANES), F32),
-            pltpu.VMEM((2 * LANES, 2 * LANES), BF16),
-            pltpu.VMEM((elems, LANES), F32),
-            pltpu.SemaphoreType.DMA((6,)),
-        ],
-        compiler_params=pltpu.CompilerParams(vmem_limit_bytes=VMEM_LIMIT),
-        name="energy",
-    )(gram, proj, dens_rows, rim_place, live)
-
-    up = lax.ppermute(tiles[0], "gx", torus("gx", -1))
-    down = lax.ppermute(tiles[1], "gx", torus("gx", 1))
-    to_left = jnp.stack([tiles[2, 0:3], up[0:9:3], down[0:9:3]], axis=1).reshape(9, LANES)
-    to_right = jnp.stack([tiles[3, 0:3], up[2:9:3], down[2:9:3]], axis=1).reshape(9, LANES)
-    left = lax.ppermute(to_left, "gy", torus("gy", -1))
-    right = lax.ppermute(to_right, "gy", torus("gy", 1))
-
-    def by_side(table):
-        corner = LANES - table.shape[2]
-        rows = [table[0, main : main + 1] for main in (1, 6, 3, 4)]
-        ends = [table[0, k : k + 1, :corner] for k in (0, 5, 2, 7)]
-        return jnp.concatenate(
-            [jnp.concatenate(rows, axis=0), jnp.concatenate(ends, axis=0)], axis=1
-        )
+    left, right = pl.pallas_call(
+        pass_kernel,
+        out_shape=(jax.ShapeDtypeStruct((16, LANES), F32),) * 2,
+        in_specs=[vmem] * 4,
+        out_specs=(vmem, vmem),
+        name="pass_on",
+    )(up, down, left, right)
+    left = lax.ppermute(left, "gy", torus("gy", -1))
+    right = lax.ppermute(right, "gy", torus("gy", 1))
 
     fdens, fsens = pl.pallas_call(
         owner_kernel,
@@ -383,7 +442,7 @@
         in_specs=[vmem] * 8,
         out_specs=(vmem, vmem),
         name="owner",
-    )(up, down, left, right, by_side(recv_target), by_side(recv_weight), dens_rows, sens_rows)
+    )(up, down, left, right, recv_target[0], recv_weight[0], dens_rows, sens_rows)
     return fdens.reshape(elems), fsens.reshape(elems), ritz.reshape(())
 
 

time: 132 us -> 109 us (0.83)
  Pallas kernels: 80.1 us -> 62 us
  waiting for transfers between devices: 10.4 us -> 26.4 us
  local copies, waits for them, and re-layouts: 9.59 us -> 1.19 us
  starting transfers between devices: 24.3 us -> 17.3 us
  other arithmetic: 6.06 us -> 1.6 us
    pallas_call x2 -> x3, Pallas kernels: 77.9 us -> 59.7 us  [the longest x1 35.2 us: project_and_gram(): pl.pallas_call(lambda *refs: gram_kernel(elems, per_step, *refs), grid=(s...]
    ppermute x9, waiting for transfers between devices: 6.53 us -> 15.2 us  [sum_over_devices(): lax.ppermute(value, AXES, swapped(sizes, axis, s))]
    ppermute x4, waiting for transfers between devices: 3.9 us -> 9.73 us  [the longest x1 3.88 us: per_device(): right = lax.ppermute(right, 'gy', torus('gy', 1))]
    squeeze x5 -> x0, local copies, waits for them, and re-layouts: 4.07 us -> none  [the longest x2 1.68 us: by_side(): rows = [table[0, main:main + 1] for main in (1, 6, 3, 4)]]
    ppermute x9, starting transfers between devices: 18.3 us -> 14.7 us  [sum_over_devices(): lax.ppermute(value, AXES, swapped(sizes, axis, s))]
    ppermute x4, starting transfers between devices: 5.98 us -> 2.54 us  [the longest x1 1.46 us: per_device(): right = lax.ppermute(right, 'gy', torus('gy', 1))]
    ppermute x1, waiting for transfers between devices: 0.01 us -> 1.46 us  [sum_over_devices(): value = value + lax.ppermute(value, AXES, swapped(sizes, 1, 1))]
    mul x3 -> x0, local copies, waits for them, and re-layouts: 1.36 us -> none  [per_device(): factors[:, None, None, :] * eye[None, :, :, None]]
  transfers between devices with their start and end apart: 14 -> 14, of which waited for: 9 -> 14; matrix products, arithmetic and copies ran while one was open for 6% -> 0% of each run, Pallas kernels for 0% -> 0%
where the time goes in v2:
time: 109 us
  Pallas kernels  62 us (57%)
  waiting for transfers between devices  26.4 us (24%)
  starting transfers between devices  17.3 us (16%)
  other arithmetic  1.6 us (1%)
  local copies, waits for them, and re-layouts  1.19 us (1%)
    pallas_call x1, Pallas kernels, project_and_gram(): pl.pallas_call(lambda *refs: gram_kernel(elems, per_step, *refs), grid=(s...  35.2 us
    pallas_call x1, Pallas kernels, energies(): pl.pallas_call(lambda *refs: energy_kernel(scale, *refs), out_shape=(jax....  23.2 us
    ppermute x9, waiting for transfers between devices, sum_over_devices(): lax.ppermute(value, AXES, swapped(sizes, axis, s))  15.2 us
    ppermute x9, starting transfers between devices, sum_over_devices(): lax.ppermute(value, AXES, swapped(sizes, axis, s))  14.7 us
    ppermute x1, waiting for transfers between devices, per_device(): right = lax.ppermute(right, 'gy', torus('gy', 1))  3.88 us
    ppermute x1, waiting for transfers between devices, per_device(): down = lax.ppermute(down, 'gx', torus('gx', 1))  2.94 us
    pallas_call x1, Pallas kernels, per_device(): pl.pallas_call(owner_kernel, out_shape=(jax.ShapeDtypeStruct((elems // LA...  2.26 us
  transfers between devices with their start and end apart: 14, of which 14 were waited for; matrix products, arithmetic and copies ran while one was open for 0% of the time, Pallas kernels for 0%

profile of v2, /device:TPU:0, one launch (start us, length us, event | category | flops | bytes accessed | tf_op | source)
XLA Modules:
  0.0 109.2 jit_solution(18397149783285500570)
XLA Ops:
  0.6 35.2 %gram.1 = (bf16[288,384,128]{2,1,0:T(8,128)(2,1)}, f32[136,128]{1,0:T(8,128)}) custom-call(s32[8,2304]{1,0:T(8,128)} %refs_0_.1, bf16[3,128,2304]{2,1,0:T(8,128)(2,1)} %refs_1_.1, f32[18,128]{1,0:T(8,128)} %bitcast.7, bf16[24,24]{1,0:T(8,128)(2,1)} %refs_3_.1, bf16[24,24]{1,0:T(8,128)(2,1)} %refs_4_.2), custom_call_target="tpu_custom_call" | custom-call | tf_op jit(solution)/shard_map/gram/pallas_call | solution.py:273
  35.8 0.1 collective-permute-start
  35.9 1.5 %collective-permute-done = f32[136,128]{1,0:T(8,128)S(1)} collective-permute-done((f32[136,128]{1,0:T(8,128)}, f32[136,128]{1,0:T(8,128)S(1)}, u32[]{:S(2)}, u32[]{:S(2)}) %collective-permute-start) | collective-permute-done | bytes 69664 | tf_op jit(solution)/shard_map/ppermute | solution.py:397
  37.4 0.9 add.30
  38.3 2.9 %collective-permute-start.3 = (f32[136,128]{1,0:T(8,128)S(1)}, f32[136,128]{1,0:T(8,128)S(1)}, u32[]{:S(2)}, u32[]{:S(2)}) collective-permute-start(f32[136,128]{1,0:T(8,128)S(1)} %add.30), channel_id=1, source_target_pairs={{0,3},{1,0},{2,1},{3,2},{4,7},{5,4},{6,5},{7,6},{8,11},{9,8},{10,9... | collective-permute-start | bytes 208904 | tf_op jit(solution)/shard_map/ppermute | solution.py:400
  41.1 0.9 collective-permute-start.2
  42.0 0.8 collective-permute-start.1
  42.9 1.6 %collective-permute-done.3 = f32[136,128]{1,0:T(8,128)S(1)} collective-permute-done((f32[136,128]{1,0:T(8,128)S(1)}, f32[136,128]{1,0:T(8,128)S(1)}, u32[]{:S(2)}, u32[]{:S(2)}) %collective-permute-start.3) | collective-permute-done | bytes 69664 | tf_op jit(solution)/shard_map/ppermute | solution.py:400
  44.5 2.9 %collective-permute-done.2 = f32[136,128]{1,0:T(8,128)S(1)} collective-permute-done((f32[136,128]{1,0:T(8,128)S(1)}, f32[136,128]{1,0:T(8,128)S(1)}, u32[]{:S(2)}, u32[]{:S(2)}) %collective-permute-start.2) | collective-permute-done | bytes 69664 | tf_op jit(solution)/shard_map/ppermute | solution.py:400
  47.4 0.7 collective-permute-done.1
  48.1 3.1 %collective-permute-start.6 = (f32[136,128]{1,0:T(8,128)S(1)}, f32[136,128]{1,0:T(8,128)S(1)}, u32[]{:S(2)}, u32[]{:S(2)}) collective-permute-start(f32[136,128]{1,0:T(8,128)S(1)} %add_add_fusion.2), channel_id=1, source_target_pairs={{0,12},{1,13},{2,14},{3,15},{4,0},{5,1},{6,2},{7,3},{8,4},{9,5},{1... | collective-permute-start | bytes 208904 | tf_op jit(solution)/shard_map/ppermute | solution.py:400
  51.2 0.7 collective-permute-start.5
  51.9 1.0 collective-permute-start.4
  52.8 0.3 collective-permute-done.6
  53.1 3.9 %collective-permute-done.5 = f32[136,128]{1,0:T(8,128)S(1)} collective-permute-done((f32[136,128]{1,0:T(8,128)S(1)}, f32[136,128]{1,0:T(8,128)S(1)}, u32[]{:S(2)}, u32[]{:S(2)}) %collective-permute-start.5) | collective-permute-done | bytes 69664 | tf_op jit(solution)/shard_map/ppermute | solution.py:400
  57.0 0.7 collective-permute-done.4
  57.8 4.1 %collective-permute-start.9 = (f32[136,128]{1,0:T(8,128)S(1)}, f32[136,128]{1,0:T(8,128)S(1)}, u32[]{:S(2)}, u32[]{:S(2)}) collective-permute-start(f32[136,128]{1,0:T(8,128)S(1)} %add_add_fusion.1), channel_id=1, source_target_pairs={{0,96},{1,97},{2,98},{3,99},{4,100},{5,101},{6,102},{7,103},{8,104... | collective-permute-start | bytes 208904 | tf_op jit(solution)/shard_map/ppermute | solution.py:400
  61.9 0.0 collective-permute-start.8
  61.9 1.3 %collective-permute-start.7 = (f32[136,128]{1,0:T(8,128)S(1)}, f32[136,128]{1,0:T(8,128)S(1)}, u32[]{:S(2)}, u32[]{:S(2)}) collective-permute-start(f32[136,128]{1,0:T(8,128)S(1)} %add_add_fusion.1), channel_id=1, source_target_pairs={{0,32},{1,33},{2,34},{3,35},{4,36},{5,37},{6,38},{7,39},{8,40},{9,... | collective-permute-start | bytes 208904 | tf_op jit(solution)/shard_map/ppermute | solution.py:400
  63.2 0.7 collective-permute-done.9
  63.9 4.0 %collective-permute-done.8 = f32[136,128]{1,0:T(8,128)S(1)} collective-permute-done((f32[136,128]{1,0:T(8,128)S(1)}, f32[136,128]{1,0:T(8,128)S(1)}, u32[]{:S(2)}, u32[]{:S(2)}) %collective-permute-start.8) | collective-permute-done | bytes 69664 | tf_op jit(solution)/shard_map/ppermute | solution.py:400
  67.8 0.4 collective-permute-done.7
  68.2 0.7 add_add_fusion.refs_0_
  68.8 23.2 %energy.1 = (f32[18,128]{1,0:T(8,128)}, f32[16,128]{1,0:T(8,128)}, f32[16,128]{1,0:T(8,128)}, f32[8,128]{1,0:T(8,128)}, f32[8,128]{1,0:T(8,128)}, /*index=5*/f32[1,1]{1,0:T(1,128)}) custom-call(f32[136,128]{1,0:T(8,128)} %add_add_fusion.refs_0_, bf16[288,384,128]{2,1,0:T(8,128)(2,1)} %get-tuple-element.16.refs_1_, f32[18,128]{1,0:T(8,128)} %bitcast.8, ...), custom_call_target="tpu_custom_call" | custom-call | tf_op jit(solution)/shard_map/energy/pallas_call | solution.py:308
  92.1 0.0 collective-permute-start.10
  92.1 0.5 collective-permute-start.11
  92.6 1.1 collective-permute-done.10.up_ref
  93.7 0.0 copy-start
  93.7 2.9 %collective-permute-done.11.down_ref = f32[16,128]{1,0:T(8,128)S(1)} collective-permute-done((f32[16,128]{1,0:T(8,128)}, f32[16,128]{1,0:T(8,128)S(1)}, u32[]{:S(2)}, u32[]{:S(2)}) %collective-permute-start.11) | collective-permute-done | bytes 8224 | tf_op jit(solution)/shard_map/ppermute | solution.py:427
  96.6 0.0 copy-start.1
  96.6 0.0 copy-done
  96.6 0.6 copy-done.1
  97.2 1.3 %pass_on.1 = (f32[16,128]{1,0:T(8,128)}, f32[16,128]{1,0:T(8,128)}) custom-call(f32[16,128]{1,0:T(8,128)} %copy-done, f32[16,128]{1,0:T(8,128)} %copy-done.1, f32[8,128]{1,0:T(8,128)} %get-tuple-element.19.left_ref, f32[8,128]{1,0:T(8,128)} %get-tuple-element.20.right_ref), custom_call_target="tpu_custom_call" | custom-call | tf_op jit(solution)/shard_map/pass_on/pallas_call | solution.py:429
  98.6 0.6 collective-permute-start.12
  99.1 1.5 %collective-permute-start.13 = (f32[16,128]{1,0:T(8,128)}, f32[16,128]{1,0:T(8,128)S(1)}, u32[]{:S(2)}, u32[]{:S(2)}) collective-permute-start(f32[16,128]{1,0:T(8,128)} %get-tuple-element.22), channel_id=1, source_target_pairs={{0,1},{1,2},{2,3},{3,4},{4,5},{5,6},{6,7},{7,8},{8,9},{9,10},{10,1... | collective-permute-start | bytes 24584 | tf_op jit(solution)/shard_map/ppermute | solution.py:437
  100.6 1.8 %collective-permute-done.12.left_ref = f32[16,128]{1,0:T(8,128)S(1)} collective-permute-done((f32[16,128]{1,0:T(8,128)}, f32[16,128]{1,0:T(8,128)S(1)}, u32[]{:S(2)}, u32[]{:S(2)}) %collective-permute-start.12) | collective-permute-done | bytes 8224 | tf_op jit(solution)/shard_map/ppermute | solution.py:436
  102.4 0.0 copy-start.2
  102.4 3.9 %collective-permute-done.13.right_ref = f32[16,128]{1,0:T(8,128)S(1)} collective-permute-done((f32[16,128]{1,0:T(8,128)}, f32[16,128]{1,0:T(8,128)S(1)}, u32[]{:S(2)}, u32[]{:S(2)}) %collective-permute-start.13) | collective-permute-done | bytes 8224 | tf_op jit(solution)/shard_map/ppermute | solution.py:437
  106.3 0.0 copy-start.3
  106.3 0.0 copy-done.2
  106.3 0.6 copy-done.3
  106.9 2.3 %owner.1 = (f32[18,128]{1,0:T(8,128)}, f32[18,128]{1,0:T(8,128)}) custom-call(f32[16,128]{1,0:T(8,128)} %copy-done, f32[16,128]{1,0:T(8,128)} %copy-done.1, f32[16,128]{1,0:T(8,128)} %copy-done.2, f32[16,128]{1,0:T(8,128)} %copy-done.3, s32[8,96]{1,0:T(8,128)} %bitcast.10, f32[8,96]{1,0:T(8,128)} %bitcast.11, f32[18,128]{1,0:T(8,128)} %bitcast.9, ...), custom_call_target="tpu_custom_call" | custom-call | tf_op jit(solution)/shard_map/owner/pallas_call | solution.py:439
  (2 shorter events, 0.0 us)
Async XLA Ops:
  35.8 1.6 %collective-permute-start = (f32[136,128]{1,0:T(8,128)}, f32[136,128]{1,0:T(8,128)S(1)}, u32[]{:S(2)}, u32[]{:S(2)}) collective-permute-start(f32[136,128]{1,0:T(8,128)} %get-tuple-element.15), channel_id=1, source_target_pairs={{0,16},{1,17},{2,18},{3,19},{4,20},{5,21},{6,22},{7,23},{8,24},{9,... | collective-permute-start | bytes 208904 | tf_op jit(solution)/shard_map/ppermute | solution.py:397
  38.3 6.2 %collective-permute-start.3 = (f32[136,128]{1,0:T(8,128)S(1)}, f32[136,128]{1,0:T(8,128)S(1)}, u32[]{:S(2)}, u32[]{:S(2)}) collective-permute-start(f32[136,128]{1,0:T(8,128)S(1)} %add.30), channel_id=1, source_target_pairs={{0,3},{1,0},{2,1},{3,2},{4,7},{5,4},{6,5},{7,6},{8,11},{9,8},{10,9... | collective-permute-start | bytes 208904 | tf_op jit(solution)/shard_map/ppermute | solution.py:400
  41.1 6.3 %collective-permute-start.2 = (f32[136,128]{1,0:T(8,128)S(1)}, f32[136,128]{1,0:T(8,128)S(1)}, u32[]{:S(2)}, u32[]{:S(2)}) collective-permute-start(f32[136,128]{1,0:T(8,128)S(1)} %add.30), channel_id=1, source_target_pairs={{0,2},{1,3},{2,0},{3,1},{4,6},{5,7},{6,4},{7,5},{8,10},{9,11},{10,... | collective-permute-start | bytes 208904 | tf_op jit(solution)/shard_map/ppermute | solution.py:400
  42.0 6.1 %collective-permute-start.1 = (f32[136,128]{1,0:T(8,128)S(1)}, f32[136,128]{1,0:T(8,128)S(1)}, u32[]{:S(2)}, u32[]{:S(2)}) collective-permute-start(f32[136,128]{1,0:T(8,128)S(1)} %add.30), channel_id=1, source_target_pairs={{0,1},{1,2},{2,3},{3,0},{4,5},{5,6},{6,7},{7,4},{8,9},{9,10},{10,1... | collective-permute-start | bytes 208904 | tf_op jit(solution)/shard_map/ppermute | solution.py:400
  48.1 5.0 %collective-permute-start.6 = (f32[136,128]{1,0:T(8,128)S(1)}, f32[136,128]{1,0:T(8,128)S(1)}, u32[]{:S(2)}, u32[]{:S(2)}) collective-permute-start(f32[136,128]{1,0:T(8,128)S(1)} %add_add_fusion.2), channel_id=1, source_target_pairs={{0,12},{1,13},{2,14},{3,15},{4,0},{5,1},{6,2},{7,3},{8,4},{9,5},{1... | collective-permute-start | bytes 208904 | tf_op jit(solution)/shard_map/ppermute | solution.py:400
  51.2 5.9 %collective-permute-start.5 = (f32[136,128]{1,0:T(8,128)S(1)}, f32[136,128]{1,0:T(8,128)S(1)}, u32[]{:S(2)}, u32[]{:S(2)}) collective-permute-start(f32[136,128]{1,0:T(8,128)S(1)} %add_add_fusion.2), channel_id=1, source_target_pairs={{0,8},{1,9},{2,10},{3,11},{4,12},{5,13},{6,14},{7,15},{8,0},{9,1},... | collective-permute-start | bytes 208904 | tf_op jit(solution)/shard_map/ppermute | solution.py:400
  51.9 5.9 %collective-permute-start.4 = (f32[136,128]{1,0:T(8,128)S(1)}, f32[136,128]{1,0:T(8,128)S(1)}, u32[]{:S(2)}, u32[]{:S(2)}) collective-permute-start(f32[136,128]{1,0:T(8,128)S(1)} %add_add_fusion.2), channel_id=1, source_target_pairs={{0,4},{1,5},{2,6},{3,7},{4,8},{5,9},{6,10},{7,11},{8,12},{9,13},{1... | collective-permute-start | bytes 208904 | tf_op jit(solution)/shard_map/ppermute | solution.py:400
  57.8 6.1 %collective-permute-start.9 = (f32[136,128]{1,0:T(8,128)S(1)}, f32[136,128]{1,0:T(8,128)S(1)}, u32[]{:S(2)}, u32[]{:S(2)}) collective-permute-start(f32[136,128]{1,0:T(8,128)S(1)} %add_add_fusion.1), channel_id=1, source_target_pairs={{0,96},{1,97},{2,98},{3,99},{4,100},{5,101},{6,102},{7,103},{8,104... | collective-permute-start | bytes 208904 | tf_op jit(solution)/shard_map/ppermute | solution.py:400
  61.9 5.9 %collective-permute-start.8 = (f32[136,128]{1,0:T(8,128)S(1)}, f32[136,128]{1,0:T(8,128)S(1)}, u32[]{:S(2)}, u32[]{:S(2)}) collective-permute-start(f32[136,128]{1,0:T(8,128)S(1)} %add_add_fusion.1), channel_id=1, source_target_pairs={{0,64},{1,65},{2,66},{3,67},{4,68},{5,69},{6,70},{7,71},{8,72},{9,... | collective-permute-start | bytes 208904 | tf_op jit(solution)/shard_map/ppermute | solution.py:400
  61.9 6.3 %collective-permute-start.7 = (f32[136,128]{1,0:T(8,128)S(1)}, f32[136,128]{1,0:T(8,128)S(1)}, u32[]{:S(2)}, u32[]{:S(2)}) collective-permute-start(f32[136,128]{1,0:T(8,128)S(1)} %add_add_fusion.1), channel_id=1, source_target_pairs={{0,32},{1,33},{2,34},{3,35},{4,36},{5,37},{6,38},{7,39},{8,40},{9,... | collective-permute-start | bytes 208904 | tf_op jit(solution)/shard_map/ppermute | solution.py:400
  92.1 1.6 %collective-permute-start.10 = (f32[16,128]{1,0:T(8,128)}, f32[16,128]{1,0:T(8,128)S(1)}, u32[]{:S(2)}, u32[]{:S(2)}) collective-permute-start(f32[16,128]{1,0:T(8,128)} %get-tuple-element.17), channel_id=1, source_target_pairs={{0,112},{16,0},{32,16},{48,32},{64,48},{80,64},{96,80},{112,96},{1... | collective-permute-start | bytes 24584 | tf_op jit(solution)/shard_map/ppermute | solution.py:426
  92.1 4.5 %collective-permute-start.11 = (f32[16,128]{1,0:T(8,128)}, f32[16,128]{1,0:T(8,128)S(1)}, u32[]{:S(2)}, u32[]{:S(2)}) collective-permute-start(f32[16,128]{1,0:T(8,128)} %get-tuple-element.18), channel_id=1, source_target_pairs={{0,16},{16,32},{32,48},{48,64},{64,80},{80,96},{96,112},{112,0},{1... | collective-permute-start | bytes 24584 | tf_op jit(solution)/shard_map/ppermute | solution.py:427
  93.7 2.9 %copy-start = (f32[16,128]{1,0:T(8,128)}, f32[16,128]{1,0:T(8,128)S(1)}, u32[]{:S(2)}) copy-start(f32[16,128]{1,0:T(8,128)S(1)} %collective-permute-done.10.up_ref) | copy-start | bytes 24580
  96.6 0.6 copy-start.1
  98.6 3.9 %collective-permute-start.12 = (f32[16,128]{1,0:T(8,128)}, f32[16,128]{1,0:T(8,128)S(1)}, u32[]{:S(2)}, u32[]{:S(2)}) collective-permute-start(f32[16,128]{1,0:T(8,128)} %get-tuple-element.21), channel_id=1, source_target_pairs={{0,15},{1,0},{2,1},{3,2},{4,3},{5,4},{6,5},{7,6},{8,7},{9,8},{10,9... | collective-permute-start | bytes 24584 | tf_op jit(solution)/shard_map/ppermute | solution.py:436
  99.1 7.2 %collective-permute-start.13 = (f32[16,128]{1,0:T(8,128)}, f32[16,128]{1,0:T(8,128)S(1)}, u32[]{:S(2)}, u32[]{:S(2)}) collective-permute-start(f32[16,128]{1,0:T(8,128)} %get-tuple-element.22), channel_id=1, source_target_pairs={{0,1},{1,2},{2,3},{3,4},{4,5},{5,6},{6,7},{7,8},{8,9},{9,10},{10,1... | collective-permute-start | bytes 24584 | tf_op jit(solution)/shard_map/ppermute | solution.py:437
  102.4 3.9 %copy-start.2 = (f32[16,128]{1,0:T(8,128)}, f32[16,128]{1,0:T(8,128)S(1)}, u32[]{:S(2)}) copy-start(f32[16,128]{1,0:T(8,128)S(1)} %collective-permute-done.12.left_ref) | copy-start | bytes 24580
  106.3 0.6 copy-start.3

commit v3 on v2

--- a/solution.py
+++ b/solution.py
@@ -9,7 +9,8 @@
 RIM = 2
 LANES = 128
 GROUP = 8
-UNIT = 32
+UNIT = 128
+STRIP = 32
 ROWS = 24 * GROUP
 AXES = ("gx", "gy")
 VMEM_LIMIT = 60 * 1024 * 1024
@@ -103,7 +104,7 @@
             for h in range(2):
                 part = full[:, h * LANES : (h + 1) * LANES]
                 chunk = 2 * q + h
-                p_ref[local * 4 + chunk] = part
+                p_ref[local * (UNIT // GROUP) + chunk] = part
                 wide = part.astype(F32).reshape(2, 24, 8, LANES)
                 dens = dcol[pl.ds(pl.multiple_of(unit * UNIT + chunk * 8, 8), 8), :]
                 for kind, factor in enumerate((dens * dens * dens, dens)):
@@ -111,8 +112,8 @@
                     kept[2 + kind, chunk] = (wide[kind] * factor[None]).reshape(ROWS, LANES).astype(BF16)
 
     def add_grams(kept):
-        left = jnp.concatenate([kept[2 + kind].reshape(4 * ROWS, LANES) for kind in range(2)], axis=1)
-        right = jnp.concatenate([kept[kind].reshape(4 * ROWS, LANES) for kind in range(2)], axis=1)
+        left = jnp.concatenate([kept[2 + kind].reshape(UNIT // GROUP * ROWS, LANES) for kind in range(2)], axis=1)
+        right = jnp.concatenate([kept[kind].reshape(UNIT // GROUP * ROWS, LANES) for kind in range(2)], axis=1)
         full = lax.dot_general(left, right, (((0,), (0,)), ((), ())), preferred_element_type=F32)
         acc[0] += full[:LANES, :LANES]
         acc[1] += full[LANES:, LANES:]
@@ -146,18 +147,40 @@
 def invert_spd(gram):
     lane = iota((8, LANES), 1)
     sub = iota((8, LANES), 0)
-    regs = [gram[8 * g : 8 * g + 8, :] for g in range(16)]
-    for k in range(LANES):
-        own, at = k // 8, k % 8
-        row = regs[own][at : at + 1, :]
-        inverse = 1.0 / row[:, k : k + 1]
-        row = jnp.where(lane[:1] == k, inverse, row * inverse)
-        row = jnp.broadcast_to(row, (8, LANES))
-        here = lane == k
-        for g in range(16):
-            col = jnp.broadcast_to(regs[g][:, k : k + 1], (8, LANES))
-            new = jnp.where(here, 0.0, regs[g]) - col * row
-            regs[g] = jnp.where(sub == at, row, new) if g == own else new
+
+    def column(reg, k):
+        return jnp.broadcast_to(reg[:, k : k + 1], (8, LANES))
+
+    def row(reg, k):
+        return jnp.broadcast_to(reg[k : k + 1, :], (8, LANES))
+
+    regs = [gram[8 * g : 8 * g + 8, :] for g in range(LANES // 8)]
+    for own in range(LANES // 8):
+        first = 8 * own
+        inside = (lane >= first) & (lane < first + 8)
+        cols = [[column(reg, first + j) for j in range(8)] for reg in regs]
+        held = list(cols[own])
+        panel = jnp.where(inside, jnp.where(lane == first + sub, 1.0, 0.0), regs[own])
+        for k in range(8):
+            inverse = 1.0 / row(held[k], k)
+            here = sub == k
+            for at in range(k + 1, 9):
+                value = held[at] if at < 8 else panel
+                pivot = row(value, k)
+                value = jnp.where(here, 0.0, value) - jnp.where(here, -pivot, held[k] * pivot) * inverse
+                if at < 8:
+                    held[at] = value
+                else:
+                    panel = value
+        rows = [row(panel, j) for j in range(8)]
+        for g in range(LANES // 8):
+            if g == own:
+                regs[g] = panel
+                continue
+            value = jnp.where(inside, 0.0, regs[g])
+            for j in range(8):
+                value = value - cols[g][j] * rows[j]
+            regs[g] = value
     return jnp.concatenate(regs, axis=0)
 
 
@@ -224,25 +247,25 @@
     both[0:LANES, 0:LANES] = inv_mass.astype(BF16)
     both[LANES:, LANES:] = sandwich.astype(BF16)
 
-    per_piece = span * GROUP // UNIT
+    per_piece = span * GROUP // STRIP
     for i in range(pieces):
         copies[i].wait()
 
         def body(it, _, i=i):
             unit = i * per_piece + it
-            stiffs = p_vmem[pl.ds(unit * 4, 4), 0:ROWS, :].reshape(4 * ROWS, LANES)
-            masses = p_vmem[pl.ds(unit * 4, 4), ROWS:, :].reshape(4 * ROWS, LANES)
+            stiffs = p_vmem[pl.ds(unit * (STRIP // GROUP), STRIP // GROUP), 0:ROWS, :].reshape(STRIP // GROUP * ROWS, LANES)
+            masses = p_vmem[pl.ds(unit * (STRIP // GROUP), STRIP // GROUP), ROWS:, :].reshape(STRIP // GROUP * ROWS, LANES)
             inner = jnp.dot(
                 jnp.concatenate([stiffs, masses], axis=1), both[...], preferred_element_type=F32
             )
-            part_stiff = (inner[:, :LANES] * stiffs.astype(F32)).reshape(4, 24, 8, LANES).sum(axis=1)
-            part_mass = (inner[:, LANES:] * masses.astype(F32)).reshape(4, 24, 8, LANES).sum(axis=1)
-            at = pl.ds(pl.multiple_of(unit * UNIT, UNIT), UNIT)
+            part_stiff = (inner[:, :LANES] * stiffs.astype(F32)).reshape(STRIP // GROUP, 24, 8, LANES).sum(axis=1)
+            part_mass = (inner[:, LANES:] * masses.astype(F32)).reshape(STRIP // GROUP, 24, 8, LANES).sum(axis=1)
+            at = pl.ds(pl.multiple_of(unit * STRIP, STRIP), STRIP)
             dens = dcol[at, :]
-            total[at, :] = 3.0 * dens * dens * part_stiff.reshape(UNIT, LANES) - part_mass.reshape(UNIT, LANES)
+            total[at, :] = 3.0 * dens * dens * part_stiff.reshape(STRIP, LANES) - part_mass.reshape(STRIP, LANES)
             return 0
 
-        lax.fori_loop(0, per_piece, body, 0, unroll=6)
+        lax.fori_loop(0, per_piece, body, 0, unroll=12)
 
     for j in range(elems // LANES):
         block = total[pl.ds(j * LANES, LANES), :]
@@ -367,10 +390,12 @@
     stacked = jnp.concatenate([jnp.concatenate(v, axis=1) for v in values], axis=0)
     high, mid, low = split3(stacked)
     left = jnp.concatenate([high, mid, low, jnp.zeros((7, 4 * LANES), BF16)], axis=0)
-    for j in range(dens_ref.shape[0]):
-        hit = targets == iota((LANES, 4 * LANES), 0) + j * LANES
+    last = dens_ref.shape[0] - 1
+    for j in range(last + 1):
+        part = slice(0 if j in (0, last) else 2 * LANES, 4 * LANES)
+        hit = targets[:, part] == iota((LANES, part.stop - part.start), 0) + j * LANES
         hot = jnp.where(hit, 1.0, 0.0).astype(BF16)
-        sums = lax.dot_general(left, hot, (((1,), (1,)), ((), ())), preferred_element_type=F32)
+        sums = lax.dot_general(left[:, part], hot, (((1,), (1,)), ((), ())), preferred_element_type=F32)
         sums = sums[0:3] + sums[3:6] + sums[6:9]
         under = 1.0 + sums[0:1]
         fdens_ref[j : j + 1, :] = (dens_ref[j : j + 1, :] + sums[1:2]) / under

time: 109 us -> 100 us (0.917)
  Pallas kernels: 62 us -> 52.9 us
    pallas_call x1, Pallas kernels: 23.2 us -> 18.8 us  [energies(): pl.pallas_call(lambda *refs: energy_kernel(scale, *refs), out_shape=(jax....]
    pallas_call x1, Pallas kernels: 35.2 us -> 30.8 us  [project_and_gram(): pl.pallas_call(lambda *refs: gram_kernel(elems, per_step, *refs), grid=(s...]
where the time goes in v3:
time: 100 us
  Pallas kernels  52.9 us (53%)
  waiting for transfers between devices  26.5 us (26%)
  starting transfers between devices  17.2 us (17%)
  other arithmetic  1.6 us (2%)
  local copies, waits for them, and re-layouts  1.19 us (1%)
    pallas_call x1, Pallas kernels, project_and_gram(): pl.pallas_call(lambda *refs: gram_kernel(elems, per_step, *refs), grid=(s...  30.8 us
    pallas_call x1, Pallas kernels, energies(): pl.pallas_call(lambda *refs: energy_kernel(scale, *refs), out_shape=(jax....  18.8 us
    ppermute x9, waiting for transfers between devices, sum_over_devices(): lax.ppermute(value, AXES, swapped(sizes, axis, s))  15.3 us
    ppermute x9, starting transfers between devices, sum_over_devices(): lax.ppermute(value, AXES, swapped(sizes, axis, s))  14.5 us
    ppermute x1, waiting for transfers between devices, per_device(): right = lax.ppermute(right, 'gy', torus('gy', 1))  3.88 us
    ppermute x1, waiting for transfers between devices, per_device(): down = lax.ppermute(down, 'gx', torus('gx', 1))  2.94 us
  transfers between devices with their start and end apart: 14, of which 14 were waited for; matrix products, arithmetic and copies ran while one was open for 0% of the time, Pallas kernels for 0%

profile of v3, /device:TPU:0, one launch (start us, length us, event | category | flops | bytes accessed | tf_op | source)
XLA Modules:
  0.0 100.1 jit_solution(12106000465816654322)
XLA Ops:
  0.6 30.8 %gram.1 = (bf16[288,384,128]{2,1,0:T(8,128)(2,1)}, f32[136,128]{1,0:T(8,128)}) custom-call(s32[8,2304]{1,0:T(8,128)} %refs_0_.1, bf16[3,128,2304]{2,1,0:T(8,128)(2,1)} %refs_1_.1, f32[18,128]{1,0:T(8,128)} %bitcast.7, bf16[24,24]{1,0:T(8,128)(2,1)} %refs_3_.1, bf16[24,24]{1,0:T(8,128)(2,1)} %refs_4_.2), custom_call_target="tpu_custom_call" | custom-call | tf_op jit(solution)/shard_map/gram/pallas_call | solution.py:296
  31.4 0.1 collective-permute-start
  31.5 1.5 %collective-permute-done = f32[136,128]{1,0:T(8,128)S(1)} collective-permute-done((f32[136,128]{1,0:T(8,128)}, f32[136,128]{1,0:T(8,128)S(1)}, u32[]{:S(2)}, u32[]{:S(2)}) %collective-permute-start) | collective-permute-done | bytes 69664 | tf_op jit(solution)/shard_map/ppermute | solution.py:422
  33.0 0.9 add.30
  33.9 2.9 %collective-permute-start.3 = (f32[136,128]{1,0:T(8,128)S(1)}, f32[136,128]{1,0:T(8,128)S(1)}, u32[]{:S(2)}, u32[]{:S(2)}) collective-permute-start(f32[136,128]{1,0:T(8,128)S(1)} %add.30), channel_id=1, source_target_pairs={{0,3},{1,0},{2,1},{3,2},{4,7},{5,4},{6,5},{7,6},{8,11},{9,8},{10,9... | collective-permute-start | bytes 208904 | tf_op jit(solution)/shard_map/ppermute | solution.py:425
  36.8 0.8 collective-permute-start.2
  37.6 0.9 collective-permute-start.1
  38.4 1.7 %collective-permute-done.3 = f32[136,128]{1,0:T(8,128)S(1)} collective-permute-done((f32[136,128]{1,0:T(8,128)S(1)}, f32[136,128]{1,0:T(8,128)S(1)}, u32[]{:S(2)}, u32[]{:S(2)}) %collective-permute-start.3) | collective-permute-done | bytes 69664 | tf_op jit(solution)/shard_map/ppermute | solution.py:425
  40.1 2.9 %collective-permute-done.2 = f32[136,128]{1,0:T(8,128)S(1)} collective-permute-done((f32[136,128]{1,0:T(8,128)S(1)}, f32[136,128]{1,0:T(8,128)S(1)}, u32[]{:S(2)}, u32[]{:S(2)}) %collective-permute-start.2) | collective-permute-done | bytes 69664 | tf_op jit(solution)/shard_map/ppermute | solution.py:425
  43.1 0.7 collective-permute-done.1
  43.8 3.1 %collective-permute-start.6 = (f32[136,128]{1,0:T(8,128)S(1)}, f32[136,128]{1,0:T(8,128)S(1)}, u32[]{:S(2)}, u32[]{:S(2)}) collective-permute-start(f32[136,128]{1,0:T(8,128)S(1)} %add_add_fusion.2), channel_id=1, source_target_pairs={{0,12},{1,13},{2,14},{3,15},{4,0},{5,1},{6,2},{7,3},{8,4},{9,5},{1... | collective-permute-start | bytes 208904 | tf_op jit(solution)/shard_map/ppermute | solution.py:425
  46.9 0.6 collective-permute-start.5
  47.5 0.9 collective-permute-start.4
  48.5 0.4 collective-permute-done.6
  48.8 3.9 %collective-permute-done.5 = f32[136,128]{1,0:T(8,128)S(1)} collective-permute-done((f32[136,128]{1,0:T(8,128)S(1)}, f32[136,128]{1,0:T(8,128)S(1)}, u32[]{:S(2)}, u32[]{:S(2)}) %collective-permute-start.5) | collective-permute-done | bytes 69664 | tf_op jit(solution)/shard_map/ppermute | solution.py:425
  52.7 0.7 collective-permute-done.4
  53.5 4.0 %collective-permute-start.9 = (f32[136,128]{1,0:T(8,128)S(1)}, f32[136,128]{1,0:T(8,128)S(1)}, u32[]{:S(2)}, u32[]{:S(2)}) collective-permute-start(f32[136,128]{1,0:T(8,128)S(1)} %add_add_fusion.1), channel_id=1, source_target_pairs={{0,96},{1,97},{2,98},{3,99},{4,100},{5,101},{6,102},{7,103},{8,104... | collective-permute-start | bytes 208904 | tf_op jit(solution)/shard_map/ppermute | solution.py:425
  57.5 0.0 collective-permute-start.8
  57.5 1.3 %collective-permute-start.7 = (f32[136,128]{1,0:T(8,128)S(1)}, f32[136,128]{1,0:T(8,128)S(1)}, u32[]{:S(2)}, u32[]{:S(2)}) collective-permute-start(f32[136,128]{1,0:T(8,128)S(1)} %add_add_fusion.1), channel_id=1, source_target_pairs={{0,32},{1,33},{2,34},{3,35},{4,36},{5,37},{6,38},{7,39},{8,40},{9,... | collective-permute-start | bytes 208904 | tf_op jit(solution)/shard_map/ppermute | solution.py:425
  58.8 0.7 collective-permute-done.9
  59.5 4.0 %collective-permute-done.8 = f32[136,128]{1,0:T(8,128)S(1)} collective-permute-done((f32[136,128]{1,0:T(8,128)S(1)}, f32[136,128]{1,0:T(8,128)S(1)}, u32[]{:S(2)}, u32[]{:S(2)}) %collective-permute-start.8) | collective-permute-done | bytes 69664 | tf_op jit(solution)/shard_map/ppermute | solution.py:425
  63.4 0.4 collective-permute-done.7
  63.8 0.7 add_add_fusion.refs_0_
  64.4 18.8 %energy.1 = (f32[18,128]{1,0:T(8,128)}, f32[16,128]{1,0:T(8,128)}, f32[16,128]{1,0:T(8,128)}, f32[8,128]{1,0:T(8,128)}, f32[8,128]{1,0:T(8,128)}, /*index=5*/f32[1,1]{1,0:T(1,128)}) custom-call(f32[136,128]{1,0:T(8,128)} %add_add_fusion.refs_0_, bf16[288,384,128]{2,1,0:T(8,128)(2,1)} %get-tuple-element.16.refs_1_, f32[18,128]{1,0:T(8,128)} %bitcast.8, ...), custom_call_target="tpu_custom_call" | custom-call | tf_op jit(solution)/shard_map/energy/pallas_call | solution.py:331
  83.3 0.0 collective-permute-start.10
  83.3 0.5 collective-permute-start.11
  83.8 1.1 %collective-permute-done.10.up_ref = f32[16,128]{1,0:T(8,128)S(1)} collective-permute-done((f32[16,128]{1,0:T(8,128)}, f32[16,128]{1,0:T(8,128)S(1)}, u32[]{:S(2)}, u32[]{:S(2)}) %collective-permute-start.10) | collective-permute-done | bytes 8224 | tf_op jit(solution)/shard_map/ppermute | solution.py:451
  84.9 0.0 copy-start
  84.9 2.9 %collective-permute-done.11.down_ref = f32[16,128]{1,0:T(8,128)S(1)} collective-permute-done((f32[16,128]{1,0:T(8,128)}, f32[16,128]{1,0:T(8,128)S(1)}, u32[]{:S(2)}, u32[]{:S(2)}) %collective-permute-start.11) | collective-permute-done | bytes 8224 | tf_op jit(solution)/shard_map/ppermute | solution.py:452
  87.8 0.0 copy-start.1
  87.8 0.0 copy-done
  87.8 0.6 copy-done.1
  88.4 1.3 %pass_on.1 = (f32[16,128]{1,0:T(8,128)}, f32[16,128]{1,0:T(8,128)}) custom-call(f32[16,128]{1,0:T(8,128)} %copy-done, f32[16,128]{1,0:T(8,128)} %copy-done.1, f32[8,128]{1,0:T(8,128)} %get-tuple-element.19.left_ref, f32[8,128]{1,0:T(8,128)} %get-tuple-element.20.right_ref), custom_call_target="tpu_custom_call" | custom-call | tf_op jit(solution)/shard_map/pass_on/pallas_call | solution.py:454
  89.8 0.6 collective-permute-start.12
  90.3 1.5 %collective-permute-start.13 = (f32[16,128]{1,0:T(8,128)}, f32[16,128]{1,0:T(8,128)S(1)}, u32[]{:S(2)}, u32[]{:S(2)}) collective-permute-start(f32[16,128]{1,0:T(8,128)} %get-tuple-element.22), channel_id=1, source_target_pairs={{0,1},{1,2},{2,3},{3,4},{4,5},{5,6},{6,7},{7,8},{8,9},{9,10},{10,1... | collective-permute-start | bytes 24584 | tf_op jit(solution)/shard_map/ppermute | solution.py:462
  91.8 1.8 %collective-permute-done.12.left_ref = f32[16,128]{1,0:T(8,128)S(1)} collective-permute-done((f32[16,128]{1,0:T(8,128)}, f32[16,128]{1,0:T(8,128)S(1)}, u32[]{:S(2)}, u32[]{:S(2)}) %collective-permute-start.12) | collective-permute-done | bytes 8224 | tf_op jit(solution)/shard_map/ppermute | solution.py:461
  93.6 0.0 copy-start.2
  93.6 3.9 %collective-permute-done.13.right_ref = f32[16,128]{1,0:T(8,128)S(1)} collective-permute-done((f32[16,128]{1,0:T(8,128)}, f32[16,128]{1,0:T(8,128)S(1)}, u32[]{:S(2)}, u32[]{:S(2)}) %collective-permute-start.13) | collective-permute-done | bytes 8224 | tf_op jit(solution)/shard_map/ppermute | solution.py:462
  97.5 0.0 copy-start.3
  97.5 0.0 copy-done.2
  97.5 0.6 copy-done.3
  98.1 2.0 %owner.1 = (f32[18,128]{1,0:T(8,128)}, f32[18,128]{1,0:T(8,128)}) custom-call(f32[16,128]{1,0:T(8,128)} %copy-done, f32[16,128]{1,0:T(8,128)} %copy-done.1, f32[16,128]{1,0:T(8,128)} %copy-done.2, f32[16,128]{1,0:T(8,128)} %copy-done.3, s32[8,96]{1,0:T(8,128)} %bitcast.10, f32[8,96]{1,0:T(8,128)} %bitcast.11, f32[18,128]{1,0:T(8,128)} %bitcast.9, ...), custom_call_target="tpu_custom_call" | custom-call | tf_op jit(solution)/shard_map/owner/pallas_call | solution.py:464
  (2 shorter events, 0.0 us)
Async XLA Ops:
  31.4 1.6 %collective-permute-start = (f32[136,128]{1,0:T(8,128)}, f32[136,128]{1,0:T(8,128)S(1)}, u32[]{:S(2)}, u32[]{:S(2)}) collective-permute-start(f32[136,128]{1,0:T(8,128)} %get-tuple-element.15), channel_id=1, source_target_pairs={{0,16},{1,17},{2,18},{3,19},{4,20},{5,21},{6,22},{7,23},{8,24},{9,... | collective-permute-start | bytes 208904 | tf_op jit(solution)/shard_map/ppermute | solution.py:422
  33.9 6.3 %collective-permute-start.3 = (f32[136,128]{1,0:T(8,128)S(1)}, f32[136,128]{1,0:T(8,128)S(1)}, u32[]{:S(2)}, u32[]{:S(2)}) collective-permute-start(f32[136,128]{1,0:T(8,128)S(1)} %add.30), channel_id=1, source_target_pairs={{0,3},{1,0},{2,1},{3,2},{4,7},{5,4},{6,5},{7,6},{8,11},{9,8},{10,9... | collective-permute-start | bytes 208904 | tf_op jit(solution)/shard_map/ppermute | solution.py:425
  36.8 6.3 %collective-permute-start.2 = (f32[136,128]{1,0:T(8,128)S(1)}, f32[136,128]{1,0:T(8,128)S(1)}, u32[]{:S(2)}, u32[]{:S(2)}) collective-permute-start(f32[136,128]{1,0:T(8,128)S(1)} %add.30), channel_id=1, source_target_pairs={{0,2},{1,3},{2,0},{3,1},{4,6},{5,7},{6,4},{7,5},{8,10},{9,11},{10,... | collective-permute-start | bytes 208904 | tf_op jit(solution)/shard_map/ppermute | solution.py:425
  37.6 6.2 %collective-permute-start.1 = (f32[136,128]{1,0:T(8,128)S(1)}, f32[136,128]{1,0:T(8,128)S(1)}, u32[]{:S(2)}, u32[]{:S(2)}) collective-permute-start(f32[136,128]{1,0:T(8,128)S(1)} %add.30), channel_id=1, source_target_pairs={{0,1},{1,2},{2,3},{3,0},{4,5},{5,6},{6,7},{7,4},{8,9},{9,10},{10,1... | collective-permute-start | bytes 208904 | tf_op jit(solution)/shard_map/ppermute | solution.py:425
  43.8 5.0 %collective-permute-start.6 = (f32[136,128]{1,0:T(8,128)S(1)}, f32[136,128]{1,0:T(8,128)S(1)}, u32[]{:S(2)}, u32[]{:S(2)}) collective-permute-start(f32[136,128]{1,0:T(8,128)S(1)} %add_add_fusion.2), channel_id=1, source_target_pairs={{0,12},{1,13},{2,14},{3,15},{4,0},{5,1},{6,2},{7,3},{8,4},{9,5},{1... | collective-permute-start | bytes 208904 | tf_op jit(solution)/shard_map/ppermute | solution.py:425
  46.9 5.9 %collective-permute-start.5 = (f32[136,128]{1,0:T(8,128)S(1)}, f32[136,128]{1,0:T(8,128)S(1)}, u32[]{:S(2)}, u32[]{:S(2)}) collective-permute-start(f32[136,128]{1,0:T(8,128)S(1)} %add_add_fusion.2), channel_id=1, source_target_pairs={{0,8},{1,9},{2,10},{3,11},{4,12},{5,13},{6,14},{7,15},{8,0},{9,1},... | collective-permute-start | bytes 208904 | tf_op jit(solution)/shard_map/ppermute | solution.py:425
  47.5 5.9 %collective-permute-start.4 = (f32[136,128]{1,0:T(8,128)S(1)}, f32[136,128]{1,0:T(8,128)S(1)}, u32[]{:S(2)}, u32[]{:S(2)}) collective-permute-start(f32[136,128]{1,0:T(8,128)S(1)} %add_add_fusion.2), channel_id=1, source_target_pairs={{0,4},{1,5},{2,6},{3,7},{4,8},{5,9},{6,10},{7,11},{8,12},{9,13},{1... | collective-permute-start | bytes 208904 | tf_op jit(solution)/shard_map/ppermute | solution.py:425
  53.5 6.0 %collective-permute-start.9 = (f32[136,128]{1,0:T(8,128)S(1)}, f32[136,128]{1,0:T(8,128)S(1)}, u32[]{:S(2)}, u32[]{:S(2)}) collective-permute-start(f32[136,128]{1,0:T(8,128)S(1)} %add_add_fusion.1), channel_id=1, source_target_pairs={{0,96},{1,97},{2,98},{3,99},{4,100},{5,101},{6,102},{7,103},{8,104... | collective-permute-start | bytes 208904 | tf_op jit(solution)/shard_map/ppermute | solution.py:425
  57.5 5.9 %collective-permute-start.8 = (f32[136,128]{1,0:T(8,128)S(1)}, f32[136,128]{1,0:T(8,128)S(1)}, u32[]{:S(2)}, u32[]{:S(2)}) collective-permute-start(f32[136,128]{1,0:T(8,128)S(1)} %add_add_fusion.1), channel_id=1, source_target_pairs={{0,64},{1,65},{2,66},{3,67},{4,68},{5,69},{6,70},{7,71},{8,72},{9,... | collective-permute-start | bytes 208904 | tf_op jit(solution)/shard_map/ppermute | solution.py:425
  57.5 6.3 %collective-permute-start.7 = (f32[136,128]{1,0:T(8,128)S(1)}, f32[136,128]{1,0:T(8,128)S(1)}, u32[]{:S(2)}, u32[]{:S(2)}) collective-permute-start(f32[136,128]{1,0:T(8,128)S(1)} %add_add_fusion.1), channel_id=1, source_target_pairs={{0,32},{1,33},{2,34},{3,35},{4,36},{5,37},{6,38},{7,39},{8,40},{9,... | collective-permute-start | bytes 208904 | tf_op jit(solution)/shard_map/ppermute | solution.py:425
  83.3 1.6 %collective-permute-start.10 = (f32[16,128]{1,0:T(8,128)}, f32[16,128]{1,0:T(8,128)S(1)}, u32[]{:S(2)}, u32[]{:S(2)}) collective-permute-start(f32[16,128]{1,0:T(8,128)} %get-tuple-element.17), channel_id=1, source_target_pairs={{0,112},{16,0},{32,16},{48,32},{64,48},{80,64},{96,80},{112,96},{1... | collective-permute-start | bytes 24584 | tf_op jit(solution)/shard_map/ppermute | solution.py:451
  83.3 4.5 %collective-permute-start.11 = (f32[16,128]{1,0:T(8,128)}, f32[16,128]{1,0:T(8,128)S(1)}, u32[]{:S(2)}, u32[]{:S(2)}) collective-permute-start(f32[16,128]{1,0:T(8,128)} %get-tuple-element.18), channel_id=1, source_target_pairs={{0,16},{16,32},{32,48},{48,64},{64,80},{80,96},{96,112},{112,0},{1... | collective-permute-start | bytes 24584 | tf_op jit(solution)/shard_map/ppermute | solution.py:452
  84.9 2.9 %copy-start = (f32[16,128]{1,0:T(8,128)}, f32[16,128]{1,0:T(8,128)S(1)}, u32[]{:S(2)}) copy-start(f32[16,128]{1,0:T(8,128)S(1)} %collective-permute-done.10.up_ref) | copy-start | bytes 24580
  87.8 0.6 copy-start.1
  89.8 3.9 %collective-permute-start.12 = (f32[16,128]{1,0:T(8,128)}, f32[16,128]{1,0:T(8,128)S(1)}, u32[]{:S(2)}, u32[]{:S(2)}) collective-permute-start(f32[16,128]{1,0:T(8,128)} %get-tuple-element.21), channel_id=1, source_target_pairs={{0,15},{1,0},{2,1},{3,2},{4,3},{5,4},{6,5},{7,6},{8,7},{9,8},{10,9... | collective-permute-start | bytes 24584 | tf_op jit(solution)/shard_map/ppermute | solution.py:461
  90.3 7.2 %collective-permute-start.13 = (f32[16,128]{1,0:T(8,128)}, f32[16,128]{1,0:T(8,128)S(1)}, u32[]{:S(2)}, u32[]{:S(2)}) collective-permute-start(f32[16,128]{1,0:T(8,128)} %get-tuple-element.22), channel_id=1, source_target_pairs={{0,1},{1,2},{2,3},{3,4},{4,5},{5,6},{6,7},{7,8},{8,9},{9,10},{10,1... | collective-permute-start | bytes 24584 | tf_op jit(solution)/shard_map/ppermute | solution.py:462
  93.6 3.9 %copy-start.2 = (f32[16,128]{1,0:T(8,128)}, f32[16,128]{1,0:T(8,128)S(1)}, u32[]{:S(2)}) copy-start(f32[16,128]{1,0:T(8,128)S(1)} %collective-permute-done.12.left_ref) | copy-start | bytes 24580
  97.5 0.6 copy-start.3

commit v4 on v3

--- a/solution.py
+++ b/solution.py
@@ -13,7 +13,7 @@
 STRIP = 32
 ROWS = 24 * GROUP
 AXES = ("gx", "gy")
-VMEM_LIMIT = 60 * 1024 * 1024
+VMEM_LIMIT = 44 * 1024 * 1024
 F32 = jnp.float32
 BF16 = jnp.bfloat16
 HIGHEST = lax.Precision.HIGHEST
@@ -214,8 +214,8 @@
 
 
 def energy_kernel(
-    scale, gram_ref, p_hbm, dens_ref, slot_ref, count_ref, sens_ref, up_ref, down_ref, left_ref, right_ref, ritz_ref,
-    p_vmem, dcol, both, total, sems
+    scale, gram_any, p_hbm, dens_ref, slot_ref, count_ref, sens_ref, up_ref, down_ref, side_ref, ritz_ref,
+    gram_ref, p_vmem, dcol, both, total, gram_sem, sems
 ):
     elems = dcol.shape[0]
     groups = elems // GROUP
@@ -227,12 +227,15 @@
         )
         for i in range(pieces)
     ]
+    gram_copy = pltpu.make_async_copy(gram_any, gram_ref, gram_sem)
+    gram_copy.start()
     for copy in copies:
         copy.start()
     density_columns(dens_ref, dcol)
     slots, live = rim_places(slot_ref[...], count_ref, elems)
     tile_dens = jnp.take_along_axis(rims(dcol, 1.0 / LANES), slots, axis=1) * live
 
+    gram_copy.wait()
     row, col = iota((LANES, LANES), 0), iota((LANES, LANES), 1)
     packed = gram_ref[0:LANES, :]
     above = jnp.where(row < col, packed, 0.0)
@@ -271,19 +274,12 @@
         block = total[pl.ds(j * LANES, LANES), :]
         sens_ref[j : j + 1, :] = jnp.sum(block.T, axis=0, keepdims=True) * scale
     tile_sens = jnp.take_along_axis(rims(total, scale), slots, axis=1) * live
-    for ref, first, count in ((up_ref, 0, 3), (down_ref, 5, 3), (left_ref, 3, 1), (right_ref, 4, 1)):
+    tiles = (live, tile_dens, tile_sens)
+    for ref, directions in ((up_ref, (0, 2, 1)), (down_ref, (5, 7, 6)), (side_ref, (3, 4))):
         ref[...] = jnp.zeros_like(ref)
-        for ch, value in enumerate((live, tile_dens, tile_sens)):
-            ref[count * ch : count * ch + count, :] = value[first : first + count]
-
-
-def pass_kernel(up_ref, down_ref, left_ref, right_ref, to_left_ref, to_right_ref):
-    for out, own, at in ((to_left_ref, left_ref, 0), (to_right_ref, right_ref, 2)):
-        out[...] = jnp.zeros_like(out)
-        for ch in range(3):
-            out[3 * ch : 3 * ch + 1, :] = own[ch : ch + 1, :]
-            out[3 * ch + 1 : 3 * ch + 2, :] = up_ref[3 * ch + at : 3 * ch + at + 1, :]
-            out[3 * ch + 2 : 3 * ch + 3, :] = down_ref[3 * ch + at : 3 * ch + at + 1, :]
+        for n, k in enumerate(directions):
+            for ch, value in enumerate(tiles):
+                ref[3 * n + ch : 3 * n + ch + 1, :] = value[k : k + 1]
 
 
 def project_and_gram(connectivity, block_vectors, dens_rows, stiff_factor, mass_factor):
@@ -335,16 +331,17 @@
             jax.ShapeDtypeStruct((16, LANES), F32),
             jax.ShapeDtypeStruct((16, LANES), F32),
             jax.ShapeDtypeStruct((8, LANES), F32),
-            jax.ShapeDtypeStruct((8, LANES), F32),
             jax.ShapeDtypeStruct((1, 1), F32),
         ),
-        in_specs=[vmem, pl.BlockSpec(memory_space=pl.ANY), vmem, vmem, smem],
-        out_specs=(vmem,) * 5 + (smem,),
+        in_specs=[pl.BlockSpec(memory_space=pl.ANY)] * 2 + [vmem, vmem, smem],
+        out_specs=(vmem,) * 4 + (smem,),
         scratch_shapes=[
+            pltpu.VMEM((LANES + 8, LANES), F32),
             pltpu.VMEM((groups, 2 * ROWS, LANES), BF16),
             pltpu.VMEM((elems, LANES), F32),
             pltpu.VMEM((2 * LANES, 2 * LANES), BF16),
             pltpu.VMEM((elems, LANES), F32),
+            pltpu.SemaphoreType.DMA,
             pltpu.SemaphoreType.DMA((6,)),
         ],
         compiler_params=pltpu.CompilerParams(vmem_limit_bytes=VMEM_LIMIT),
@@ -360,7 +357,14 @@
     return high, mid, low
 
 
-def owner_kernel(up_ref, down_ref, left_ref, right_ref, target_ref, weight_ref, dens_ref, sens_ref, fdens_ref, fsens_ref):
+def owner_kernel(
+    up_any, down_any, left_any, right_any, target_ref, weight_ref, dens_ref, sens_ref, fdens_ref, fsens_ref,
+    up_ref, down_ref, left_ref, right_ref, sems
+):
+    pairs = ((up_any, up_ref), (down_any, down_ref), (left_any, left_ref), (right_any, right_ref))
+    copies = [pltpu.make_async_copy(src, dst, sems.at[i]) for i, (src, dst) in enumerate(pairs)]
+    for copy in copies:
+        copy.start()
     lane = iota((1, LANES), 1)
 
     def lanes_of(main, corner):
@@ -373,17 +377,19 @@
 
     weights = by_side(weight_ref[...])
     targets = jnp.concatenate(by_side(target_ref[...]), axis=1)
+    for copy in copies:
+        copy.wait()
     values = [[], [], []]
     for ch in range(3):
-        up = up_ref[3 * ch + 1 : 3 * ch + 2, :]
-        down = down_ref[3 * ch + 1 : 3 * ch + 2, :]
-        left = left_ref[3 * ch : 3 * ch + 3, :]
-        right = right_ref[3 * ch : 3 * ch + 3, :]
+
+        def at(ref, first):
+            return ref[first + ch : first + ch + 1, :]
+
         sides = (
-            lanes_of(up, left[1:2]),
-            lanes_of(down, left[2:3]),
-            lanes_of(left[0:1], right[1:2]),
-            lanes_of(right[0:1], right[2:3]),
+            lanes_of(at(up_ref, 6), at(left_ref, 8)),
+            lanes_of(at(down_ref, 6), at(left_ref, 16)),
+            lanes_of(at(left_ref, 0), at(right_ref, 11)),
+            lanes_of(at(right_ref, 3), at(right_ref, 19)),
         )
         for side in range(4):
             values[ch].append(sides[side] * weights[side])
@@ -446,26 +452,27 @@
     proj, gram = project_and_gram(connectivity, block_vectors, dens_rows, stiff_factor, mass_factor)
     gram = sum_over_devices(gram, sizes)
 
-    sens_rows, up, down, left, right, ritz = energies(scale, gram, proj, dens_rows, send_slot[0], send_count)
+    sens_rows, up, down, side, ritz = energies(scale, gram, proj, dens_rows, send_slot[0], send_count)
 
     up = lax.ppermute(up, "gx", torus("gx", -1))
     down = lax.ppermute(down, "gx", torus("gx", 1))
+    packet = jnp.concatenate([side, up[:8], down[:8]], axis=0)
+    left = lax.ppermute(packet, "gy", torus("gy", -1))
+    right = lax.ppermute(packet, "gy", torus("gy", 1))
+
     vmem = pl.BlockSpec(memory_space=pltpu.VMEM)
-    left, right = pl.pallas_call(
-        pass_kernel,
-        out_shape=(jax.ShapeDtypeStruct((16, LANES), F32),) * 2,
-        in_specs=[vmem] * 4,
-        out_specs=(vmem, vmem),
-        name="pass_on",
-    )(up, down, left, right)
-    left = lax.ppermute(left, "gy", torus("gy", -1))
-    right = lax.ppermute(right, "gy", torus("gy", 1))
-
     fdens, fsens = pl.pallas_call(
         owner_kernel,
         out_shape=(jax.ShapeDtypeStruct((elems // LANES, LANES), F32),) * 2,
-        in_specs=[vmem] * 8,
+        in_specs=[pl.BlockSpec(memory_space=pl.ANY)] * 4 + [vmem] * 4,
         out_specs=(vmem, vmem),
+        scratch_shapes=[
+            pltpu.VMEM((16, LANES), F32),
+            pltpu.VMEM((16, LANES), F32),
+            pltpu.VMEM((24, LANES), F32),
+            pltpu.VMEM((24, LANES), F32),
+            pltpu.SemaphoreType.DMA((4,)),
+        ],
         name="owner",
     )(up, down, left, right, recv_target[0], recv_weight[0], dens_rows, sens_rows)
     return fdens.reshape(elems), fsens.reshape(elems), ritz.reshape(())

time: 100 us -> 100 us (level)
  local copies, waits for them, and re-layouts: 1.19 us -> 6.96 us
  waiting for transfers between devices: 26.5 us -> 22 us
  Pallas kernels: 52.9 us -> 49 us
  starting transfers between devices: 17.2 us -> 20.5 us
  other arithmetic: 1.6 us -> 0.08 us
    unnamed x8 -> x24, local copies, waits for them, and re-layouts: 1.19 us -> 6.95 us
    ppermute x2, waiting for transfers between devices: 5.72 us -> 1.67 us  [the longest x1 1.67 us: per_device(): right = lax.ppermute(packet, 'gy', torus('gy', 1))]
    ppermute x2, starting transfers between devices: 2.03 us -> 5.4 us  [the longest x1 5.33 us: per_device(): left = lax.ppermute(packet, 'gy', torus('gy', -1))]
    pallas_call x1, Pallas kernels: 30.8 us -> 29 us  [project_and_gram(): pl.pallas_call(lambda *refs: gram_kernel(elems, per_step, *refs), grid=(s...]
    pallas_call x1, Pallas kernels: 18.8 us -> 17.3 us  [energies(): pl.pallas_call(lambda *refs: energy_kernel(scale, *refs), out_shape=(jax....]
    pallas_call x1 -> x0, Pallas kernels: 1.33 us -> none  [per_device(): pl.pallas_call(pass_kernel, out_shape=(jax.ShapeDtypeStruct((16, LANES),...]
  transfers between devices with their start and end apart: 14 -> 14, of which waited for: 14 -> 13; matrix products, arithmetic and copies ran while one was open for 0% -> 0% of each run, Pallas kernels for 0% -> 0%
where the time goes in v4:
time: 100 us; the launch traced here: 99.5 us
  Pallas kernels  49 us (49%)
  waiting for transfers between devices  22 us (22%)
  starting transfers between devices  20.5 us (20%)
  local copies, waits for them, and re-layouts  6.96 us (7%)
    pallas_call x1, Pallas kernels, project_and_gram(): pl.pallas_call(lambda *refs: gram_kernel(elems, per_step, *refs), grid=(s...  29 us
    pallas_call x1, Pallas kernels, energies(): pl.pallas_call(lambda *refs: energy_kernel(scale, *refs), out_shape=(jax....  17.3 us
    ppermute x9, waiting for transfers between devices, sum_over_devices(): lax.ppermute(value, AXES, swapped(sizes, axis, s))  15.3 us
    ppermute x9, starting transfers between devices, sum_over_devices(): lax.ppermute(value, AXES, swapped(sizes, axis, s))  14.5 us
    unnamed x24, local copies, waits for them, and re-layouts  6.95 us
    ppermute x1, starting transfers between devices, per_device(): left = lax.ppermute(packet, 'gy', torus('gy', -1))  5.33 us
    ppermute x1, waiting for transfers between devices, per_device(): down = lax.ppermute(down, 'gx', torus('gx', 1))  2.92 us
    pallas_call x1, Pallas kernels, per_device(): pl.pallas_call(owner_kernel, out_shape=(jax.ShapeDtypeStruct((elems // LA...  2.68 us
  transfers between devices with their start and end apart: 14, of which 13 were waited for; matrix products, arithmetic and copies ran while one was open for 0% of the time, Pallas kernels for 0%

profile of v4, /device:TPU:0, one launch (start us, length us, event | category | flops | bytes accessed | tf_op | source)
XLA Modules:
  0.0 99.5 jit_solution(14355716161609428329)
XLA Ops:
  0.6 0.0 copy-start
  0.6 1.5 %copy-done = bf16[3,128,2304]{2,1,0:T(8,128)(2,1)S(1)} copy-done((bf16[3,128,2304]{2,1,0:T(8,128)(2,1)S(1)}, bf16[3,128,2304]{2,1,0:T(8,128)(2,1)}, u32[]{:S(2)}) %copy-start) | copy-done | bytes 1769496
  2.1 0.0 copy-start.1
  2.1 0.7 copy-done.1
  2.8 0.0 copy-start.2
  2.8 0.9 copy-done.2
  3.7 0.7 copy-done.4
  4.4 0.7 copy-done.5
  5.1 29.0 %gram.1 = (bf16[288,384,128]{2,1,0:T(8,128)(2,1)}, f32[136,128]{1,0:T(8,128)S(1)}) custom-call(s32[8,2304]{1,0:T(8,128)S(1)} %copy-done.2, bf16[3,128,2304]{2,1,0:T(8,128)(2,1)S(1)} %copy-done, f32[18,128]{1,0:T(8,128)S(1)} %bitcast.8, bf16[24,24]{1,0:T(8,128)(2,1)S(1)} %copy-done.4, bf16[24,24]{1,0:T(8,128)(2,1)S(1)} %copy-done.5), custom_call_target="tpu_custom_call" | custom-call | tf_op jit(solution)/shard_map/gram/pallas_call | solution.py:292
  34.1 0.1 collective-permute-start
  34.2 1.2 %collective-permute-done = f32[136,128]{1,0:T(8,128)S(1)} collective-permute-done((f32[136,128]{1,0:T(8,128)S(1)}, f32[136,128]{1,0:T(8,128)S(1)}, u32[]{:S(2)}, u32[]{:S(2)}) %collective-permute-start) | collective-permute-done | bytes 69664 | tf_op jit(solution)/shard_map/ppermute | solution.py:428
  35.5 2.9 %collective-permute-start.3 = (f32[136,128]{1,0:T(8,128)S(1)}, f32[136,128]{1,0:T(8,128)S(1)}, u32[]{:S(2)}, u32[]{:S(2)}) collective-permute-start(f32[136,128]{1,0:T(8,128)S(1)} %add.30), channel_id=1, source_target_pairs={{0,3},{1,0},{2,1},{3,2},{4,7},{5,4},{6,5},{7,6},{8,11},{9,8},{10,9... | collective-permute-start | bytes 208904 | tf_op jit(solution)/shard_map/ppermute | solution.py:431
  38.4 0.8 collective-permute-start.2
  39.2 0.8 collective-permute-start.1
  40.0 1.7 %collective-permute-done.3 = f32[136,128]{1,0:T(8,128)S(1)} collective-permute-done((f32[136,128]{1,0:T(8,128)S(1)}, f32[136,128]{1,0:T(8,128)S(1)}, u32[]{:S(2)}, u32[]{:S(2)}) %collective-permute-start.3) | collective-permute-done | bytes 69664 | tf_op jit(solution)/shard_map/ppermute | solution.py:431
  41.7 2.9 %collective-permute-done.2 = f32[136,128]{1,0:T(8,128)S(1)} collective-permute-done((f32[136,128]{1,0:T(8,128)S(1)}, f32[136,128]{1,0:T(8,128)S(1)}, u32[]{:S(2)}, u32[]{:S(2)}) %collective-permute-start.2) | collective-permute-done | bytes 69664 | tf_op jit(solution)/shard_map/ppermute | solution.py:431
  44.6 0.7 collective-permute-done.1
  45.4 3.1 %collective-permute-start.6 = (f32[136,128]{1,0:T(8,128)S(1)}, f32[136,128]{1,0:T(8,128)S(1)}, u32[]{:S(2)}, u32[]{:S(2)}) collective-permute-start(f32[136,128]{1,0:T(8,128)S(1)} %add_add_fusion.2), channel_id=1, source_target_pairs={{0,12},{1,13},{2,14},{3,15},{4,0},{5,1},{6,2},{7,3},{8,4},{9,5},{1... | collective-permute-start | bytes 208904 | tf_op jit(solution)/shard_map/ppermute | solution.py:431
  48.5 0.6 collective-permute-start.5
  49.1 1.0 collective-permute-start.4
  50.0 0.4 collective-permute-done.6
  50.4 3.9 %collective-permute-done.5 = f32[136,128]{1,0:T(8,128)S(1)} collective-permute-done((f32[136,128]{1,0:T(8,128)S(1)}, f32[136,128]{1,0:T(8,128)S(1)}, u32[]{:S(2)}, u32[]{:S(2)}) %collective-permute-start.5) | collective-permute-done | bytes 69664 | tf_op jit(solution)/shard_map/ppermute | solution.py:431
  54.3 0.7 collective-permute-done.4
  55.0 4.1 %collective-permute-start.9 = (f32[136,128]{1,0:T(8,128)S(1)}, f32[136,128]{1,0:T(8,128)S(1)}, u32[]{:S(2)}, u32[]{:S(2)}) collective-permute-start(f32[136,128]{1,0:T(8,128)S(1)} %add_add_fusion.1), channel_id=1, source_target_pairs={{0,96},{1,97},{2,98},{3,99},{4,100},{5,101},{6,102},{7,103},{8,104... | collective-permute-start | bytes 208904 | tf_op jit(solution)/shard_map/ppermute | solution.py:431
  59.1 0.0 collective-permute-start.8
  59.1 1.2 %collective-permute-start.7 = (f32[136,128]{1,0:T(8,128)S(1)}, f32[136,128]{1,0:T(8,128)S(1)}, u32[]{:S(2)}, u32[]{:S(2)}) collective-permute-start(f32[136,128]{1,0:T(8,128)S(1)} %add_add_fusion.1), channel_id=1, source_target_pairs={{0,32},{1,33},{2,34},{3,35},{4,36},{5,37},{6,38},{7,39},{8,40},{9,... | collective-permute-start | bytes 208904 | tf_op jit(solution)/shard_map/ppermute | solution.py:431
  60.3 0.7 collective-permute-done.9
  61.1 4.0 %collective-permute-done.8 = f32[136,128]{1,0:T(8,128)S(1)} collective-permute-done((f32[136,128]{1,0:T(8,128)S(1)}, f32[136,128]{1,0:T(8,128)S(1)}, u32[]{:S(2)}, u32[]{:S(2)}) %collective-permute-start.8) | collective-permute-done | bytes 69664 | tf_op jit(solution)/shard_map/ppermute | solution.py:431
  65.0 0.4 collective-permute-done.7
  65.4 0.0 copy-start.6
  65.4 0.7 copy-done.6
  66.1 0.7 copy-done.7
  66.7 17.3 %energy.1 = (f32[18,128]{1,0:T(8,128)S(1)}, f32[16,128]{1,0:T(8,128)S(1)}, f32[16,128]{1,0:T(8,128)S(1)}, f32[8,128]{1,0:T(8,128)S(1)}, f32[1,1]{1,0:T(1,128)}) custom-call(f32[136,128]{1,0:T(8,128)S(1)} %add_add_fusion.refs_0_, bf16[288,384,128]{2,1,0:T(8,128)(2,1)} %get-tuple-element.13.refs_1_, f32[18,128]{1,0:T(8,128)S(1)} %bitcast.9, ...), custom_call_target="tpu_custom_call" | custom-call | tf_op jit(solution)/shard_map/energy/pallas_call | solution.py:327
  84.1 0.0 copy-start.3
  84.1 0.6 copy-done.3
  84.7 0.0 collective-permute-start.10
  84.7 0.5 collective-permute-start.11
  85.2 0.9 collective-permute-done.10.up_any
  86.1 2.9 %collective-permute-done.11.down_any = f32[16,128]{1,0:T(8,128)S(1)} collective-permute-done((f32[16,128]{1,0:T(8,128)S(1)}, f32[16,128]{1,0:T(8,128)S(1)}, u32[]{:S(2)}, u32[]{:S(2)}) %collective-permute-start.11) | collective-permute-done | bytes 8224 | tf_op jit(solution)/shard_map/ppermute | solution.py:458
  89.0 0.1 collective-permute-start.13
  89.1 5.3 %collective-permute-start.12 = (f32[24,128]{1,0:T(8,128)S(1)}, f32[24,128]{1,0:T(8,128)S(1)}, u32[]{:S(2)}, u32[]{:S(2)}) collective-permute-start(f32[24,128]{1,0:T(8,128)S(1)} %pad_maximum_fusion), channel_id=1, source_target_pairs={{0,15},{1,0},{2,1},{3,2},{4,3},{5,4},{6,5},{7,6},{8,7},{9,8},{10,9... | collective-permute-start | bytes 36872 | tf_op jit(solution)/shard_map/ppermute | solution.py:460
  94.4 1.7 %collective-permute-done.13.right_any = f32[24,128]{1,0:T(8,128)S(1)} collective-permute-done((f32[24,128]{1,0:T(8,128)S(1)}, f32[24,128]{1,0:T(8,128)S(1)}, u32[]{:S(2)}, u32[]{:S(2)}) %collective-permute-start.13) | collective-permute-done | bytes 12320 | tf_op jit(solution)/shard_map/ppermute | solution.py:461
  96.1 0.0 collective-permute-done.12.left_any
  96.1 0.0 copy-done.8
  96.1 0.0 copy-done.9
  96.1 0.6 copy-done.10
  96.7 0.0 copy-done.11
  96.7 2.7 %owner.1 = (f32[18,128]{1,0:T(8,128)}, f32[18,128]{1,0:T(8,128)}) custom-call(f32[16,128]{1,0:T(8,128)} %copy-done.8, f32[16,128]{1,0:T(8,128)} %copy-done.9, f32[24,128]{1,0:T(8,128)} %copy-done.11, f32[24,128]{1,0:T(8,128)} %copy-done.10, s32[8,96]{1,0:T(8,128)} %bitcast.11, f32[8,96]{1,0:T(8,128)} %bitcast.12, f32[18,128]{1,0:T(8,128)} %bitcast.7, ...), custom_call_target="tpu_custom_call" | custom-call | tf_op jit(solution)/shard_map/owner/pallas_call | solution.py:464
  (14 shorter events, 0.1 us)
Async XLA Ops:
  0.6 1.5 %copy-start = (bf16[3,128,2304]{2,1,0:T(8,128)(2,1)S(1)}, bf16[3,128,2304]{2,1,0:T(8,128)(2,1)}, u32[]{:S(2)}) copy-start(bf16[3,128,2304]{2,1,0:T(8,128)(2,1)} %refs_1_.1) | copy-start | bytes 5308420
  2.1 0.7 copy-start.1
  2.8 0.9 copy-start.2
  3.7 0.7 copy-start.4
  4.4 0.7 copy-start.5
  34.1 1.3 %collective-permute-start = (f32[136,128]{1,0:T(8,128)S(1)}, f32[136,128]{1,0:T(8,128)S(1)}, u32[]{:S(2)}, u32[]{:S(2)}) collective-permute-start(f32[136,128]{1,0:T(8,128)S(1)} %get-tuple-element.12), channel_id=1, source_target_pairs={{0,16},{1,17},{2,18},{3,19},{4,20},{5,21},{6,22},{7,23},{8,24},{9,... | collective-permute-start | bytes 208904 | tf_op jit(solution)/shard_map/ppermute | solution.py:428
  35.5 6.3 %collective-permute-start.3 = (f32[136,128]{1,0:T(8,128)S(1)}, f32[136,128]{1,0:T(8,128)S(1)}, u32[]{:S(2)}, u32[]{:S(2)}) collective-permute-start(f32[136,128]{1,0:T(8,128)S(1)} %add.30), channel_id=1, source_target_pairs={{0,3},{1,0},{2,1},{3,2},{4,7},{5,4},{6,5},{7,6},{8,11},{9,8},{10,9... | collective-permute-start | bytes 208904 | tf_op jit(solution)/shard_map/ppermute | solution.py:431
  38.4 6.3 %collective-permute-start.2 = (f32[136,128]{1,0:T(8,128)S(1)}, f32[136,128]{1,0:T(8,128)S(1)}, u32[]{:S(2)}, u32[]{:S(2)}) collective-permute-start(f32[136,128]{1,0:T(8,128)S(1)} %add.30), channel_id=1, source_target_pairs={{0,2},{1,3},{2,0},{3,1},{4,6},{5,7},{6,4},{7,5},{8,10},{9,11},{10,... | collective-permute-start | bytes 208904 | tf_op jit(solution)/shard_map/ppermute | solution.py:431
  39.2 6.1 %collective-permute-start.1 = (f32[136,128]{1,0:T(8,128)S(1)}, f32[136,128]{1,0:T(8,128)S(1)}, u32[]{:S(2)}, u32[]{:S(2)}) collective-permute-start(f32[136,128]{1,0:T(8,128)S(1)} %add.30), channel_id=1, source_target_pairs={{0,1},{1,2},{2,3},{3,0},{4,5},{5,6},{6,7},{7,4},{8,9},{9,10},{10,1... | collective-permute-start | bytes 208904 | tf_op jit(solution)/shard_map/ppermute | solution.py:431
  45.4 5.0 %collective-permute-start.6 = (f32[136,128]{1,0:T(8,128)S(1)}, f32[136,128]{1,0:T(8,128)S(1)}, u32[]{:S(2)}, u32[]{:S(2)}) collective-permute-start(f32[136,128]{1,0:T(8,128)S(1)} %add_add_fusion.2), channel_id=1, source_target_pairs={{0,12},{1,13},{2,14},{3,15},{4,0},{5,1},{6,2},{7,3},{8,4},{9,5},{1... | collective-permute-start | bytes 208904 | tf_op jit(solution)/shard_map/ppermute | solution.py:431
  48.5 5.9 %collective-permute-start.5 = (f32[136,128]{1,0:T(8,128)S(1)}, f32[136,128]{1,0:T(8,128)S(1)}, u32[]{:S(2)}, u32[]{:S(2)}) collective-permute-start(f32[136,128]{1,0:T(8,128)S(1)} %add_add_fusion.2), channel_id=1, source_target_pairs={{0,8},{1,9},{2,10},{3,11},{4,12},{5,13},{6,14},{7,15},{8,0},{9,1},... | collective-permute-start | bytes 208904 | tf_op jit(solution)/shard_map/ppermute | solution.py:431
  49.1 6.0 %collective-permute-start.4 = (f32[136,128]{1,0:T(8,128)S(1)}, f32[136,128]{1,0:T(8,128)S(1)}, u32[]{:S(2)}, u32[]{:S(2)}) collective-permute-start(f32[136,128]{1,0:T(8,128)S(1)} %add_add_fusion.2), channel_id=1, source_target_pairs={{0,4},{1,5},{2,6},{3,7},{4,8},{5,9},{6,10},{7,11},{8,12},{9,13},{1... | collective-permute-start | bytes 208904 | tf_op jit(solution)/shard_map/ppermute | solution.py:431
  55.0 6.0 %collective-permute-start.9 = (f32[136,128]{1,0:T(8,128)S(1)}, f32[136,128]{1,0:T(8,128)S(1)}, u32[]{:S(2)}, u32[]{:S(2)}) collective-permute-start(f32[136,128]{1,0:T(8,128)S(1)} %add_add_fusion.1), channel_id=1, source_target_pairs={{0,96},{1,97},{2,98},{3,99},{4,100},{5,101},{6,102},{7,103},{8,104... | collective-permute-start | bytes 208904 | tf_op jit(solution)/shard_map/ppermute | solution.py:431
  59.1 5.9 %collective-permute-start.8 = (f32[136,128]{1,0:T(8,128)S(1)}, f32[136,128]{1,0:T(8,128)S(1)}, u32[]{:S(2)}, u32[]{:S(2)}) collective-permute-start(f32[136,128]{1,0:T(8,128)S(1)} %add_add_fusion.1), channel_id=1, source_target_pairs={{0,64},{1,65},{2,66},{3,67},{4,68},{5,69},{6,70},{7,71},{8,72},{9,... | collective-permute-start | bytes 208904 | tf_op jit(solution)/shard_map/ppermute | solution.py:431
  59.1 6.3 %collective-permute-start.7 = (f32[136,128]{1,0:T(8,128)S(1)}, f32[136,128]{1,0:T(8,128)S(1)}, u32[]{:S(2)}, u32[]{:S(2)}) collective-permute-start(f32[136,128]{1,0:T(8,128)S(1)} %add_add_fusion.1), channel_id=1, source_target_pairs={{0,32},{1,33},{2,34},{3,35},{4,36},{5,37},{6,38},{7,39},{8,40},{9,... | collective-permute-start | bytes 208904 | tf_op jit(solution)/shard_map/ppermute | solution.py:431
  65.4 0.7 copy-start.6
  66.1 0.7 copy-start.7
  84.1 0.6 copy-start.3
  84.7 1.4 %collective-permute-start.10 = (f32[16,128]{1,0:T(8,128)S(1)}, f32[16,128]{1,0:T(8,128)S(1)}, u32[]{:S(2)}, u32[]{:S(2)}) collective-permute-start(f32[16,128]{1,0:T(8,128)S(1)} %get-tuple-element.14), channel_id=1, source_target_pairs={{0,112},{16,0},{32,16},{48,32},{64,48},{80,64},{96,80},{112,96},{1... | collective-permute-start | bytes 24584 | tf_op jit(solution)/shard_map/ppermute | solution.py:457
  84.7 4.3 %collective-permute-start.11 = (f32[16,128]{1,0:T(8,128)S(1)}, f32[16,128]{1,0:T(8,128)S(1)}, u32[]{:S(2)}, u32[]{:S(2)}) collective-permute-start(f32[16,128]{1,0:T(8,128)S(1)} %get-tuple-element.15), channel_id=1, source_target_pairs={{0,16},{16,32},{32,48},{48,64},{64,80},{80,96},{96,112},{112,0},{1... | collective-permute-start | bytes 24584 | tf_op jit(solution)/shard_map/ppermute | solution.py:458
  86.1 10.0 %copy-start.8 = (f32[16,128]{1,0:T(8,128)}, f32[16,128]{1,0:T(8,128)S(1)}, u32[]{:S(2)}) copy-start(f32[16,128]{1,0:T(8,128)S(1)} %collective-permute-done.10.up_any) | copy-start | bytes 24580
  89.0 7.1 %copy-start.9 = (f32[16,128]{1,0:T(8,128)}, f32[16,128]{1,0:T(8,128)S(1)}, u32[]{:S(2)}) copy-start(f32[16,128]{1,0:T(8,128)S(1)} %collective-permute-done.11.down_any) | copy-start | bytes 24580
  89.0 7.1 %collective-permute-start.13 = (f32[24,128]{1,0:T(8,128)S(1)}, f32[24,128]{1,0:T(8,128)S(1)}, u32[]{:S(2)}, u32[]{:S(2)}) collective-permute-start(f32[24,128]{1,0:T(8,128)S(1)} %pad_maximum_fusion), channel_id=1, source_target_pairs={{0,1},{1,2},{2,3},{3,4},{4,5},{5,6},{6,7},{7,8},{8,9},{9,10},{10,1... | collective-permute-start | bytes 36872 | tf_op jit(solution)/shard_map/ppermute | solution.py:461
  89.1 7.0 %collective-permute-start.12 = (f32[24,128]{1,0:T(8,128)S(1)}, f32[24,128]{1,0:T(8,128)S(1)}, u32[]{:S(2)}, u32[]{:S(2)}) collective-permute-start(f32[24,128]{1,0:T(8,128)S(1)} %pad_maximum_fusion), channel_id=1, source_target_pairs={{0,15},{1,0},{2,1},{3,2},{4,3},{5,4},{6,5},{7,6},{8,7},{9,8},{10,9... | collective-permute-start | bytes 36872 | tf_op jit(solution)/shard_map/ppermute | solution.py:460
  96.1 0.6 copy-start.10
  96.1 0.6 copy-start.11

commit v5 on v4

--- a/solution.py
+++ b/solution.py
@@ -13,7 +13,7 @@
 STRIP = 32
 ROWS = 24 * GROUP
 AXES = ("gx", "gy")
-VMEM_LIMIT = 44 * 1024 * 1024
+MIB = 1024 * 1024
 F32 = jnp.float32
 BF16 = jnp.bfloat16
 HIGHEST = lax.Precision.HIGHEST
@@ -314,7 +314,7 @@
             pltpu.VMEM((2, LANES, LANES), F32),
             pltpu.SemaphoreType.DMA((8,)),
         ],
-        compiler_params=pltpu.CompilerParams(vmem_limit_bytes=VMEM_LIMIT),
+        compiler_params=pltpu.CompilerParams(vmem_limit_bytes=60 * MIB),
         name="gram",
     )(connectivity, block_vectors, dens_rows, stiff_factor, mass_factor)
 
@@ -344,7 +344,7 @@
             pltpu.SemaphoreType.DMA,
             pltpu.SemaphoreType.DMA((6,)),
         ],
-        compiler_params=pltpu.CompilerParams(vmem_limit_bytes=VMEM_LIMIT),
+        compiler_params=pltpu.CompilerParams(vmem_limit_bytes=44 * MIB),
         name="energy",
     )(gram, proj, dens_rows, send_slot, send_count)
 
@@ -473,6 +473,7 @@
             pltpu.VMEM((24, LANES), F32),
             pltpu.SemaphoreType.DMA((4,)),
         ],
+        compiler_params=pltpu.CompilerParams(vmem_limit_bytes=8 * MIB),
         name="owner",
     )(up, down, left, right, recv_target[0], recv_weight[0], dens_rows, sens_rows)
     return fdens.reshape(elems), fsens.reshape(elems), ritz.reshape(())

time: 100 us -> 96.4 us (0.964)
  local copies, waits for them, and re-layouts: 6.96 us -> 2.05 us
    unnamed x24 -> x10, local copies, waits for them, and re-layouts: 6.95 us -> 2.05 us
    pallas_call x1, Pallas kernels: 29 us -> 30.8 us  [project_and_gram(): pl.pallas_call(lambda *refs: gram_kernel(elems, per_step, *refs), grid=(s...]
    pallas_call x1, Pallas kernels: 2.68 us -> 1.3 us  [per_device(): pl.pallas_call(owner_kernel, out_shape=(jax.ShapeDtypeStruct((elems // LA...]
where the time goes in v5:
time: 96.4 us; the launch traced here: 96.1 us
  Pallas kernels  49.4 us (51%)
  waiting for transfers between devices  22.2 us (23%)
  starting transfers between devices  20.6 us (21%)
  local copies, waits for them, and re-layouts  2.05 us (2%)
  other arithmetic  0.97 us (1%)
    pallas_call x1, Pallas kernels, project_and_gram(): pl.pallas_call(lambda *refs: gram_kernel(elems, per_step, *refs), grid=(s...  30.8 us
    pallas_call x1, Pallas kernels, energies(): pl.pallas_call(lambda *refs: energy_kernel(scale, *refs), out_shape=(jax....  17.3 us
    ppermute x9, waiting for transfers between devices, sum_over_devices(): lax.ppermute(value, AXES, swapped(sizes, axis, s))  15.3 us
    ppermute x9, starting transfers between devices, sum_over_devices(): lax.ppermute(value, AXES, swapped(sizes, axis, s))  14.6 us
    ppermute x1, starting transfers between devices, per_device(): left = lax.ppermute(packet, 'gy', torus('gy', -1))  5.34 us
    ppermute x1, waiting for transfers between devices, per_device(): down = lax.ppermute(down, 'gx', torus('gx', 1))  2.94 us
    unnamed x10, local copies, waits for them, and re-layouts  2.05 us
  transfers between devices with their start and end apart: 14, of which 13 were waited for; matrix products, arithmetic and copies ran while one was open for 0% of the time, Pallas kernels for 0%

profile of v5, /device:TPU:0, one launch (start us, length us, event | category | flops | bytes accessed | tf_op | source)
XLA Modules:
  0.0 96.1 jit_solution(11858780111313559794)
XLA Ops:
  0.6 0.0 copy-start.2
  0.6 0.0 copy-start.1
  0.7 30.8 %gram.1 = (bf16[288,384,128]{2,1,0:T(8,128)(2,1)}, f32[136,128]{1,0:T(8,128)}) custom-call(s32[8,2304]{1,0:T(8,128)} %refs_0_.1, bf16[3,128,2304]{2,1,0:T(8,128)(2,1)} %refs_1_.1, f32[18,128]{1,0:T(8,128)} %bitcast.7, bf16[24,24]{1,0:T(8,128)(2,1)} %refs_3_.1, bf16[24,24]{1,0:T(8,128)(2,1)} %refs_4_.2), custom_call_target="tpu_custom_call" | custom-call | tf_op jit(solution)/shard_map/gram/pallas_call | solution.py:292
  31.4 0.1 collective-permute-start
  31.5 1.5 %collective-permute-done = f32[136,128]{1,0:T(8,128)S(1)} collective-permute-done((f32[136,128]{1,0:T(8,128)}, f32[136,128]{1,0:T(8,128)S(1)}, u32[]{:S(2)}, u32[]{:S(2)}) %collective-permute-start) | collective-permute-done | bytes 69664 | tf_op jit(solution)/shard_map/ppermute | solution.py:428
  33.0 0.9 add.30
  33.9 3.0 %collective-permute-start.3 = (f32[136,128]{1,0:T(8,128)S(1)}, f32[136,128]{1,0:T(8,128)S(1)}, u32[]{:S(2)}, u32[]{:S(2)}) collective-permute-start(f32[136,128]{1,0:T(8,128)S(1)} %add.30), channel_id=1, source_target_pairs={{0,3},{1,0},{2,1},{3,2},{4,7},{5,4},{6,5},{7,6},{8,11},{9,8},{10,9... | collective-permute-start | bytes 208904 | tf_op jit(solution)/shard_map/ppermute | solution.py:431
  36.8 0.7 collective-permute-start.2
  37.6 0.9 collective-permute-start.1
  38.5 1.7 %collective-permute-done.3 = f32[136,128]{1,0:T(8,128)S(1)} collective-permute-done((f32[136,128]{1,0:T(8,128)S(1)}, f32[136,128]{1,0:T(8,128)S(1)}, u32[]{:S(2)}, u32[]{:S(2)}) %collective-permute-start.3) | collective-permute-done | bytes 69664 | tf_op jit(solution)/shard_map/ppermute | solution.py:431
  40.2 2.9 %collective-permute-done.2 = f32[136,128]{1,0:T(8,128)S(1)} collective-permute-done((f32[136,128]{1,0:T(8,128)S(1)}, f32[136,128]{1,0:T(8,128)S(1)}, u32[]{:S(2)}, u32[]{:S(2)}) %collective-permute-start.2) | collective-permute-done | bytes 69664 | tf_op jit(solution)/shard_map/ppermute | solution.py:431
  43.1 0.7 collective-permute-done.1
  43.8 3.1 %collective-permute-start.6 = (f32[136,128]{1,0:T(8,128)S(1)}, f32[136,128]{1,0:T(8,128)S(1)}, u32[]{:S(2)}, u32[]{:S(2)}) collective-permute-start(f32[136,128]{1,0:T(8,128)S(1)} %add_add_fusion.2), channel_id=1, source_target_pairs={{0,12},{1,13},{2,14},{3,15},{4,0},{5,1},{6,2},{7,3},{8,4},{9,5},{1... | collective-permute-start | bytes 208904 | tf_op jit(solution)/shard_map/ppermute | solution.py:431
  46.9 0.6 collective-permute-start.5
  47.5 1.0 %collective-permute-start.4 = (f32[136,128]{1,0:T(8,128)S(1)}, f32[136,128]{1,0:T(8,128)S(1)}, u32[]{:S(2)}, u32[]{:S(2)}) collective-permute-start(f32[136,128]{1,0:T(8,128)S(1)} %add_add_fusion.2), channel_id=1, source_target_pairs={{0,4},{1,5},{2,6},{3,7},{4,8},{5,9},{6,10},{7,11},{8,12},{9,13},{1... | collective-permute-start | bytes 208904 | tf_op jit(solution)/shard_map/ppermute | solution.py:431
  48.5 0.3 collective-permute-done.6
  48.8 3.9 %collective-permute-done.5 = f32[136,128]{1,0:T(8,128)S(1)} collective-permute-done((f32[136,128]{1,0:T(8,128)S(1)}, f32[136,128]{1,0:T(8,128)S(1)}, u32[]{:S(2)}, u32[]{:S(2)}) %collective-permute-start.5) | collective-permute-done | bytes 69664 | tf_op jit(solution)/shard_map/ppermute | solution.py:431
  52.7 0.7 collective-permute-done.4
  53.5 4.1 %collective-permute-start.9 = (f32[136,128]{1,0:T(8,128)S(1)}, f32[136,128]{1,0:T(8,128)S(1)}, u32[]{:S(2)}, u32[]{:S(2)}) collective-permute-start(f32[136,128]{1,0:T(8,128)S(1)} %add_add_fusion.1), channel_id=1, source_target_pairs={{0,96},{1,97},{2,98},{3,99},{4,100},{5,101},{6,102},{7,103},{8,104... | collective-permute-start | bytes 208904 | tf_op jit(solution)/shard_map/ppermute | solution.py:431
  57.6 0.0 collective-permute-start.8
  57.6 1.2 %collective-permute-start.7 = (f32[136,128]{1,0:T(8,128)S(1)}, f32[136,128]{1,0:T(8,128)S(1)}, u32[]{:S(2)}, u32[]{:S(2)}) collective-permute-start(f32[136,128]{1,0:T(8,128)S(1)} %add_add_fusion.1), channel_id=1, source_target_pairs={{0,32},{1,33},{2,34},{3,35},{4,36},{5,37},{6,38},{7,39},{8,40},{9,... | collective-permute-start | bytes 208904 | tf_op jit(solution)/shard_map/ppermute | solution.py:431
  58.8 0.7 collective-permute-done.9
  59.5 4.0 %collective-permute-done.8 = f32[136,128]{1,0:T(8,128)S(1)} collective-permute-done((f32[136,128]{1,0:T(8,128)S(1)}, f32[136,128]{1,0:T(8,128)S(1)}, u32[]{:S(2)}, u32[]{:S(2)}) %collective-permute-start.8) | collective-permute-done | bytes 69664 | tf_op jit(solution)/shard_map/ppermute | solution.py:431
  63.5 0.4 collective-permute-done.7
  63.9 0.0 copy-start
  63.9 0.7 copy-done
  64.6 0.0 copy-start.3
  64.6 0.7 copy-done.3
  65.2 0.0 copy-start.4
  65.3 0.7 copy-done.4
  65.9 17.3 %energy.1 = (f32[18,128]{1,0:T(8,128)S(1)}, f32[16,128]{1,0:T(8,128)S(1)}, f32[16,128]{1,0:T(8,128)S(1)}, f32[8,128]{1,0:T(8,128)S(1)}, f32[1,1]{1,0:T(1,128)}) custom-call(f32[136,128]{1,0:T(8,128)S(1)} %add_add_fusion.refs_0_, bf16[288,384,128]{2,1,0:T(8,128)(2,1)} %get-tuple-element.13.refs_1_, f32[18,128]{1,0:T(8,128)S(1)} %bitcast.8, ...), custom_call_target="tpu_custom_call" | custom-call | tf_op jit(solution)/shard_map/energy/pallas_call | solution.py:327
  83.3 0.0 collective-permute-start.10
  83.3 0.5 collective-permute-start.11
  83.8 0.9 collective-permute-done.10.up_any
  84.6 2.9 %collective-permute-done.11.down_any = f32[16,128]{1,0:T(8,128)S(1)} collective-permute-done((f32[16,128]{1,0:T(8,128)S(1)}, f32[16,128]{1,0:T(8,128)S(1)}, u32[]{:S(2)}, u32[]{:S(2)}) %collective-permute-start.11) | collective-permute-done | bytes 8224 | tf_op jit(solution)/shard_map/ppermute | solution.py:458
  87.6 0.0 collective-permute-start.13
  87.6 5.3 %collective-permute-start.12 = (f32[24,128]{1,0:T(8,128)S(1)}, f32[24,128]{1,0:T(8,128)S(1)}, u32[]{:S(2)}, u32[]{:S(2)}) collective-permute-start(f32[24,128]{1,0:T(8,128)S(1)} %pad_maximum_fusion), channel_id=1, source_target_pairs={{0,15},{1,0},{2,1},{3,2},{4,3},{5,4},{6,5},{7,6},{8,7},{9,8},{10,9... | collective-permute-start | bytes 36872 | tf_op jit(solution)/shard_map/ppermute | solution.py:460
  92.9 1.7 %collective-permute-done.13.right_any = f32[24,128]{1,0:T(8,128)S(1)} collective-permute-done((f32[24,128]{1,0:T(8,128)S(1)}, f32[24,128]{1,0:T(8,128)S(1)}, u32[]{:S(2)}, u32[]{:S(2)}) %collective-permute-start.13) | collective-permute-done | bytes 12320 | tf_op jit(solution)/shard_map/ppermute | solution.py:461
  94.6 0.0 collective-permute-done.12.left_any
  94.6 0.0 copy-done.2
  94.6 0.0 copy-done.1
  94.6 1.3 %owner.1 = (f32[18,128]{1,0:T(8,128)}, f32[18,128]{1,0:T(8,128)}) custom-call(f32[16,128]{1,0:T(8,128)S(1)} %collective-permute-done.10.up_any, f32[16,128]{1,0:T(8,128)S(1)} %collective-permute-done.11.down_any, f32[24,128]{1,0:T(8,128)S(1)} %collective-permute-done.12.left_any, f32[24,128]{1,0:T(8,128)S(1)} %collective-permute-done.13.right_any, ...), custom_call_target="tpu_custom_call" | custom-call | tf_op jit(solution)/shard_map/owner/pallas_call | solution.py:464
  (6 shorter events, 0.1 us)
Async XLA Ops:
  0.6 94.0 %copy-start.2 = (f32[1,8,96]{2,1,0:T(8,128)S(1)}, f32[1,8,96]{2,1,0:T(8,128)}, u32[]{:S(2)}) copy-start(f32[1,8,96]{2,1,0:T(8,128)} %param.17) | copy-start | bytes 9220
  0.6 94.0 %copy-start.1 = (s32[1,8,96]{2,1,0:T(8,128)S(1)}, s32[1,8,96]{2,1,0:T(8,128)}, u32[]{:S(2)}) copy-start(s32[1,8,96]{2,1,0:T(8,128)} %param.16) | copy-start | bytes 9220
  31.4 1.6 %collective-permute-start = (f32[136,128]{1,0:T(8,128)}, f32[136,128]{1,0:T(8,128)S(1)}, u32[]{:S(2)}, u32[]{:S(2)}) collective-permute-start(f32[136,128]{1,0:T(8,128)} %get-tuple-element.12), channel_id=1, source_target_pairs={{0,16},{1,17},{2,18},{3,19},{4,20},{5,21},{6,22},{7,23},{8,24},{9,... | collective-permute-start | bytes 208904 | tf_op jit(solution)/shard_map/ppermute | solution.py:428
  33.9 6.3 %collective-permute-start.3 = (f32[136,128]{1,0:T(8,128)S(1)}, f32[136,128]{1,0:T(8,128)S(1)}, u32[]{:S(2)}, u32[]{:S(2)}) collective-permute-start(f32[136,128]{1,0:T(8,128)S(1)} %add.30), channel_id=1, source_target_pairs={{0,3},{1,0},{2,1},{3,2},{4,7},{5,4},{6,5},{7,6},{8,11},{9,8},{10,9... | collective-permute-start | bytes 208904 | tf_op jit(solution)/shard_map/ppermute | solution.py:431
  36.8 6.3 %collective-permute-start.2 = (f32[136,128]{1,0:T(8,128)S(1)}, f32[136,128]{1,0:T(8,128)S(1)}, u32[]{:S(2)}, u32[]{:S(2)}) collective-permute-start(f32[136,128]{1,0:T(8,128)S(1)} %add.30), channel_id=1, source_target_pairs={{0,2},{1,3},{2,0},{3,1},{4,6},{5,7},{6,4},{7,5},{8,10},{9,11},{10,... | collective-permute-start | bytes 208904 | tf_op jit(solution)/shard_map/ppermute | solution.py:431
  37.6 6.2 %collective-permute-start.1 = (f32[136,128]{1,0:T(8,128)S(1)}, f32[136,128]{1,0:T(8,128)S(1)}, u32[]{:S(2)}, u32[]{:S(2)}) collective-permute-start(f32[136,128]{1,0:T(8,128)S(1)} %add.30), channel_id=1, source_target_pairs={{0,1},{1,2},{2,3},{3,0},{4,5},{5,6},{6,7},{7,4},{8,9},{9,10},{10,1... | collective-permute-start | bytes 208904 | tf_op jit(solution)/shard_map/ppermute | solution.py:431
  43.8 5.0 %collective-permute-start.6 = (f32[136,128]{1,0:T(8,128)S(1)}, f32[136,128]{1,0:T(8,128)S(1)}, u32[]{:S(2)}, u32[]{:S(2)}) collective-permute-start(f32[136,128]{1,0:T(8,128)S(1)} %add_add_fusion.2), channel_id=1, source_target_pairs={{0,12},{1,13},{2,14},{3,15},{4,0},{5,1},{6,2},{7,3},{8,4},{9,5},{1... | collective-permute-start | bytes 208904 | tf_op jit(solution)/shard_map/ppermute | solution.py:431
  46.9 5.9 %collective-permute-start.5 = (f32[136,128]{1,0:T(8,128)S(1)}, f32[136,128]{1,0:T(8,128)S(1)}, u32[]{:S(2)}, u32[]{:S(2)}) collective-permute-start(f32[136,128]{1,0:T(8,128)S(1)} %add_add_fusion.2), channel_id=1, source_target_pairs={{0,8},{1,9},{2,10},{3,11},{4,12},{5,13},{6,14},{7,15},{8,0},{9,1},... | collective-permute-start | bytes 208904 | tf_op jit(solution)/shard_map/ppermute | solution.py:431
  47.5 5.9 %collective-permute-start.4 = (f32[136,128]{1,0:T(8,128)S(1)}, f32[136,128]{1,0:T(8,128)S(1)}, u32[]{:S(2)}, u32[]{:S(2)}) collective-permute-start(f32[136,128]{1,0:T(8,128)S(1)} %add_add_fusion.2), channel_id=1, source_target_pairs={{0,4},{1,5},{2,6},{3,7},{4,8},{5,9},{6,10},{7,11},{8,12},{9,13},{1... | collective-permute-start | bytes 208904 | tf_op jit(solution)/shard_map/ppermute | solution.py:431
  53.5 6.1 %collective-permute-start.9 = (f32[136,128]{1,0:T(8,128)S(1)}, f32[136,128]{1,0:T(8,128)S(1)}, u32[]{:S(2)}, u32[]{:S(2)}) collective-permute-start(f32[136,128]{1,0:T(8,128)S(1)} %add_add_fusion.1), channel_id=1, source_target_pairs={{0,96},{1,97},{2,98},{3,99},{4,100},{5,101},{6,102},{7,103},{8,104... | collective-permute-start | bytes 208904 | tf_op jit(solution)/shard_map/ppermute | solution.py:431
  57.6 5.9 %collective-permute-start.8 = (f32[136,128]{1,0:T(8,128)S(1)}, f32[136,128]{1,0:T(8,128)S(1)}, u32[]{:S(2)}, u32[]{:S(2)}) collective-permute-start(f32[136,128]{1,0:T(8,128)S(1)} %add_add_fusion.1), channel_id=1, source_target_pairs={{0,64},{1,65},{2,66},{3,67},{4,68},{5,69},{6,70},{7,71},{8,72},{9,... | collective-permute-start | bytes 208904 | tf_op jit(solution)/shard_map/ppermute | solution.py:431
  57.6 6.3 %collective-permute-start.7 = (f32[136,128]{1,0:T(8,128)S(1)}, f32[136,128]{1,0:T(8,128)S(1)}, u32[]{:S(2)}, u32[]{:S(2)}) collective-permute-start(f32[136,128]{1,0:T(8,128)S(1)} %add_add_fusion.1), channel_id=1, source_target_pairs={{0,32},{1,33},{2,34},{3,35},{4,36},{5,37},{6,38},{7,39},{8,40},{9,... | collective-permute-start | bytes 208904 | tf_op jit(solution)/shard_map/ppermute | solution.py:431
  63.9 0.7 copy-start
  64.6 0.7 copy-start.3
  65.2 0.7 copy-start.4
  83.3 1.4 %collective-permute-start.10 = (f32[16,128]{1,0:T(8,128)S(1)}, f32[16,128]{1,0:T(8,128)S(1)}, u32[]{:S(2)}, u32[]{:S(2)}) collective-permute-start(f32[16,128]{1,0:T(8,128)S(1)} %get-tuple-element.14), channel_id=1, source_target_pairs={{0,112},{16,0},{32,16},{48,32},{64,48},{80,64},{96,80},{112,96},{1... | collective-permute-start | bytes 24584 | tf_op jit(solution)/shard_map/ppermute | solution.py:457
  83.3 4.3 %collective-permute-start.11 = (f32[16,128]{1,0:T(8,128)S(1)}, f32[16,128]{1,0:T(8,128)S(1)}, u32[]{:S(2)}, u32[]{:S(2)}) collective-permute-start(f32[16,128]{1,0:T(8,128)S(1)} %get-tuple-element.15), channel_id=1, source_target_pairs={{0,16},{16,32},{32,48},{48,64},{64,80},{80,96},{96,112},{112,0},{1... | collective-permute-start | bytes 24584 | tf_op jit(solution)/shard_map/ppermute | solution.py:458
  87.6 7.0 %collective-permute-start.13 = (f32[24,128]{1,0:T(8,128)S(1)}, f32[24,128]{1,0:T(8,128)S(1)}, u32[]{:S(2)}, u32[]{:S(2)}) collective-permute-start(f32[24,128]{1,0:T(8,128)S(1)} %pad_maximum_fusion), channel_id=1, source_target_pairs={{0,1},{1,2},{2,3},{3,4},{4,5},{5,6},{6,7},{7,8},{8,9},{9,10},{10,1... | collective-permute-start | bytes 36872 | tf_op jit(solution)/shard_map/ppermute | solution.py:461
  87.6 7.0 %collective-permute-start.12 = (f32[24,128]{1,0:T(8,128)S(1)}, f32[24,128]{1,0:T(8,128)S(1)}, u32[]{:S(2)}, u32[]{:S(2)}) collective-permute-start(f32[24,128]{1,0:T(8,128)S(1)} %pad_maximum_fusion), channel_id=1, source_target_pairs={{0,15},{1,0},{2,1},{3,2},{4,3},{5,4},{6,5},{7,6},{8,7},{9,8},{10,9... | collective-permute-start | bytes 36872 | tf_op jit(solution)/shard_map/ppermute | solution.py:460

commit v6 on v5

--- a/solution.py
+++ b/solution.py
@@ -268,7 +268,7 @@
             total[at, :] = 3.0 * dens * dens * part_stiff.reshape(STRIP, LANES) - part_mass.reshape(STRIP, LANES)
             return 0
 
-        lax.fori_loop(0, per_piece, body, 0, unroll=12)
+        lax.fori_loop(0, per_piece, body, 0, unroll=18)
 
     for j in range(elems // LANES):
         block = total[pl.ds(j * LANES, LANES), :]
@@ -342,7 +342,7 @@
             pltpu.VMEM((2 * LANES, 2 * LANES), BF16),
             pltpu.VMEM((elems, LANES), F32),
             pltpu.SemaphoreType.DMA,
-            pltpu.SemaphoreType.DMA((6,)),
+            pltpu.SemaphoreType.DMA((4,)),
         ],
         compiler_params=pltpu.CompilerParams(vmem_limit_bytes=44 * MIB),
         name="energy",

time: 96.4 us -> 95.8 us (level)
  no operation moved by 1% of the time
where the time goes in v6:
time: 95.8 us; the launch traced here: 95.5 us
  Pallas kernels  48.9 us (51%)
  waiting for transfers between devices  22.1 us (23%)
  starting transfers between devices  20.7 us (22%)
  local copies, waits for them, and re-layouts  2.05 us (2%)
  other arithmetic  0.97 us (1%)
    pallas_call x1, Pallas kernels, project_and_gram(): pl.pallas_call(lambda *refs: gram_kernel(elems, per_step, *refs), grid=(s...  30.8 us
    pallas_call x1, Pallas kernels, energies(): pl.pallas_call(lambda *refs: energy_kernel(scale, *refs), out_shape=(jax....  16.8 us
    ppermute x9, waiting for transfers between devices, sum_over_devices(): lax.ppermute(value, AXES, swapped(sizes, axis, s))  15.2 us
    ppermute x9, starting transfers between devices, sum_over_devices(): lax.ppermute(value, AXES, swapped(sizes, axis, s))  14.7 us
    ppermute x1, starting transfers between devices, per_device(): left = lax.ppermute(packet, 'gy', torus('gy', -1))  5.34 us
    ppermute x1, waiting for transfers between devices, per_device(): down = lax.ppermute(down, 'gx', torus('gx', 1))  2.94 us
    unnamed x10, local copies, waits for them, and re-layouts  2.05 us
  transfers between devices with their start and end apart: 14, of which 13 were waited for; matrix products, arithmetic and copies ran while one was open for 0% of the time, Pallas kernels for 0%

profile of v6, /device:TPU:0, one launch (start us, length us, event | category | flops | bytes accessed | tf_op | source)
XLA Modules:
  0.0 95.5 jit_solution(12498662904210049130)
XLA Ops:
  0.6 0.0 copy-start.2
  0.6 0.0 copy-start.1
  0.7 30.8 %gram.1 = (bf16[288,384,128]{2,1,0:T(8,128)(2,1)}, f32[136,128]{1,0:T(8,128)}) custom-call(s32[8,2304]{1,0:T(8,128)} %refs_0_.1, bf16[3,128,2304]{2,1,0:T(8,128)(2,1)} %refs_1_.1, f32[18,128]{1,0:T(8,128)} %bitcast.7, bf16[24,24]{1,0:T(8,128)(2,1)} %refs_3_.1, bf16[24,24]{1,0:T(8,128)(2,1)} %refs_4_.2), custom_call_target="tpu_custom_call" | custom-call | tf_op jit(solution)/shard_map/gram/pallas_call | solution.py:292
  31.5 0.1 collective-permute-start
  31.6 1.5 %collective-permute-done = f32[136,128]{1,0:T(8,128)S(1)} collective-permute-done((f32[136,128]{1,0:T(8,128)}, f32[136,128]{1,0:T(8,128)S(1)}, u32[]{:S(2)}, u32[]{:S(2)}) %collective-permute-start) | collective-permute-done | bytes 69664 | tf_op jit(solution)/shard_map/ppermute | solution.py:428
  33.1 0.9 add.30
  33.9 2.8 %collective-permute-start.3 = (f32[136,128]{1,0:T(8,128)S(1)}, f32[136,128]{1,0:T(8,128)S(1)}, u32[]{:S(2)}, u32[]{:S(2)}) collective-permute-start(f32[136,128]{1,0:T(8,128)S(1)} %add.30), channel_id=1, source_target_pairs={{0,3},{1,0},{2,1},{3,2},{4,7},{5,4},{6,5},{7,6},{8,11},{9,8},{10,9... | collective-permute-start | bytes 208904 | tf_op jit(solution)/shard_map/ppermute | solution.py:431
  36.8 0.9 collective-permute-start.2
  37.7 0.9 collective-permute-start.1
  38.5 1.6 %collective-permute-done.3 = f32[136,128]{1,0:T(8,128)S(1)} collective-permute-done((f32[136,128]{1,0:T(8,128)S(1)}, f32[136,128]{1,0:T(8,128)S(1)}, u32[]{:S(2)}, u32[]{:S(2)}) %collective-permute-start.3) | collective-permute-done | bytes 69664 | tf_op jit(solution)/shard_map/ppermute | solution.py:431
  40.1 2.9 %collective-permute-done.2 = f32[136,128]{1,0:T(8,128)S(1)} collective-permute-done((f32[136,128]{1,0:T(8,128)S(1)}, f32[136,128]{1,0:T(8,128)S(1)}, u32[]{:S(2)}, u32[]{:S(2)}) %collective-permute-start.2) | collective-permute-done | bytes 69664 | tf_op jit(solution)/shard_map/ppermute | solution.py:431
  43.0 0.7 collective-permute-done.1
  43.7 3.1 %collective-permute-start.6 = (f32[136,128]{1,0:T(8,128)S(1)}, f32[136,128]{1,0:T(8,128)S(1)}, u32[]{:S(2)}, u32[]{:S(2)}) collective-permute-start(f32[136,128]{1,0:T(8,128)S(1)} %add_add_fusion.2), channel_id=1, source_target_pairs={{0,12},{1,13},{2,14},{3,15},{4,0},{5,1},{6,2},{7,3},{8,4},{9,5},{1... | collective-permute-start | bytes 208904 | tf_op jit(solution)/shard_map/ppermute | solution.py:431
  46.9 0.6 collective-permute-start.5
  47.5 1.0 %collective-permute-start.4 = (f32[136,128]{1,0:T(8,128)S(1)}, f32[136,128]{1,0:T(8,128)S(1)}, u32[]{:S(2)}, u32[]{:S(2)}) collective-permute-start(f32[136,128]{1,0:T(8,128)S(1)} %add_add_fusion.2), channel_id=1, source_target_pairs={{0,4},{1,5},{2,6},{3,7},{4,8},{5,9},{6,10},{7,11},{8,12},{9,13},{1... | collective-permute-start | bytes 208904 | tf_op jit(solution)/shard_map/ppermute | solution.py:431
  48.5 0.3 collective-permute-done.6
  48.8 3.9 %collective-permute-done.5 = f32[136,128]{1,0:T(8,128)S(1)} collective-permute-done((f32[136,128]{1,0:T(8,128)S(1)}, f32[136,128]{1,0:T(8,128)S(1)}, u32[]{:S(2)}, u32[]{:S(2)}) %collective-permute-start.5) | collective-permute-done | bytes 69664 | tf_op jit(solution)/shard_map/ppermute | solution.py:431
  52.7 0.7 collective-permute-done.4
  53.5 4.1 %collective-permute-start.9 = (f32[136,128]{1,0:T(8,128)S(1)}, f32[136,128]{1,0:T(8,128)S(1)}, u32[]{:S(2)}, u32[]{:S(2)}) collective-permute-start(f32[136,128]{1,0:T(8,128)S(1)} %add_add_fusion.1), channel_id=1, source_target_pairs={{0,96},{1,97},{2,98},{3,99},{4,100},{5,101},{6,102},{7,103},{8,104... | collective-permute-start | bytes 208904 | tf_op jit(solution)/shard_map/ppermute | solution.py:431
  57.6 0.0 collective-permute-start.8
  57.6 1.2 %collective-permute-start.7 = (f32[136,128]{1,0:T(8,128)S(1)}, f32[136,128]{1,0:T(8,128)S(1)}, u32[]{:S(2)}, u32[]{:S(2)}) collective-permute-start(f32[136,128]{1,0:T(8,128)S(1)} %add_add_fusion.1), channel_id=1, source_target_pairs={{0,32},{1,33},{2,34},{3,35},{4,36},{5,37},{6,38},{7,39},{8,40},{9,... | collective-permute-start | bytes 208904 | tf_op jit(solution)/shard_map/ppermute | solution.py:431
  58.9 0.7 collective-permute-done.9
  59.6 4.0 %collective-permute-done.8 = f32[136,128]{1,0:T(8,128)S(1)} collective-permute-done((f32[136,128]{1,0:T(8,128)S(1)}, f32[136,128]{1,0:T(8,128)S(1)}, u32[]{:S(2)}, u32[]{:S(2)}) %collective-permute-start.8) | collective-permute-done | bytes 69664 | tf_op jit(solution)/shard_map/ppermute | solution.py:431
  63.5 0.4 collective-permute-done.7
  63.9 0.0 copy-start
  63.9 0.7 copy-done
  64.6 0.0 copy-start.3
  64.6 0.7 copy-done.3
  65.3 0.0 copy-start.4
  65.3 0.7 copy-done.4
  66.0 16.8 %energy.1 = (f32[18,128]{1,0:T(8,128)S(1)}, f32[16,128]{1,0:T(8,128)S(1)}, f32[16,128]{1,0:T(8,128)S(1)}, f32[8,128]{1,0:T(8,128)S(1)}, f32[1,1]{1,0:T(1,128)}) custom-call(f32[136,128]{1,0:T(8,128)S(1)} %add_add_fusion.refs_0_, bf16[288,384,128]{2,1,0:T(8,128)(2,1)} %get-tuple-element.13.refs_1_, f32[18,128]{1,0:T(8,128)S(1)} %bitcast.8, ...), custom_call_target="tpu_custom_call" | custom-call | tf_op jit(solution)/shard_map/energy/pallas_call | solution.py:327
  82.7 0.0 collective-permute-start.10
  82.7 0.5 collective-permute-start.11
  83.2 0.9 collective-permute-done.10.up_any
  84.1 2.9 %collective-permute-done.11.down_any = f32[16,128]{1,0:T(8,128)S(1)} collective-permute-done((f32[16,128]{1,0:T(8,128)S(1)}, f32[16,128]{1,0:T(8,128)S(1)}, u32[]{:S(2)}, u32[]{:S(2)}) %collective-permute-start.11) | collective-permute-done | bytes 8224 | tf_op jit(solution)/shard_map/ppermute | solution.py:458
  87.0 0.0 collective-permute-start.13
  87.1 5.3 %collective-permute-start.12 = (f32[24,128]{1,0:T(8,128)S(1)}, f32[24,128]{1,0:T(8,128)S(1)}, u32[]{:S(2)}, u32[]{:S(2)}) collective-permute-start(f32[24,128]{1,0:T(8,128)S(1)} %pad_maximum_fusion), channel_id=1, source_target_pairs={{0,15},{1,0},{2,1},{3,2},{4,3},{5,4},{6,5},{7,6},{8,7},{9,8},{10,9... | collective-permute-start | bytes 36872 | tf_op jit(solution)/shard_map/ppermute | solution.py:460
  92.4 1.7 %collective-permute-done.13.right_any = f32[24,128]{1,0:T(8,128)S(1)} collective-permute-done((f32[24,128]{1,0:T(8,128)S(1)}, f32[24,128]{1,0:T(8,128)S(1)}, u32[]{:S(2)}, u32[]{:S(2)}) %collective-permute-start.13) | collective-permute-done | bytes 12320 | tf_op jit(solution)/shard_map/ppermute | solution.py:461
  94.1 0.0 collective-permute-done.12.left_any
  94.1 0.0 copy-done.2
  94.1 0.0 copy-done.1
  94.1 1.3 %owner.1 = (f32[18,128]{1,0:T(8,128)}, f32[18,128]{1,0:T(8,128)}) custom-call(f32[16,128]{1,0:T(8,128)S(1)} %collective-permute-done.10.up_any, f32[16,128]{1,0:T(8,128)S(1)} %collective-permute-done.11.down_any, f32[24,128]{1,0:T(8,128)S(1)} %collective-permute-done.12.left_any, f32[24,128]{1,0:T(8,128)S(1)} %collective-permute-done.13.right_any, ...), custom_call_target="tpu_custom_call" | custom-call | tf_op jit(solution)/shard_map/owner/pallas_call | solution.py:464
  (6 shorter events, 0.1 us)
Async XLA Ops:
  0.6 93.4 %copy-start.2 = (f32[1,8,96]{2,1,0:T(8,128)S(1)}, f32[1,8,96]{2,1,0:T(8,128)}, u32[]{:S(2)}) copy-start(f32[1,8,96]{2,1,0:T(8,128)} %param.17) | copy-start | bytes 9220
  0.6 93.4 %copy-start.1 = (s32[1,8,96]{2,1,0:T(8,128)S(1)}, s32[1,8,96]{2,1,0:T(8,128)}, u32[]{:S(2)}) copy-start(s32[1,8,96]{2,1,0:T(8,128)} %param.16) | copy-start | bytes 9220
  31.5 1.6 %collective-permute-start = (f32[136,128]{1,0:T(8,128)}, f32[136,128]{1,0:T(8,128)S(1)}, u32[]{:S(2)}, u32[]{:S(2)}) collective-permute-start(f32[136,128]{1,0:T(8,128)} %get-tuple-element.12), channel_id=1, source_target_pairs={{0,16},{1,17},{2,18},{3,19},{4,20},{5,21},{6,22},{7,23},{8,24},{9,... | collective-permute-start | bytes 208904 | tf_op jit(solution)/shard_map/ppermute | solution.py:428
  33.9 6.2 %collective-permute-start.3 = (f32[136,128]{1,0:T(8,128)S(1)}, f32[136,128]{1,0:T(8,128)S(1)}, u32[]{:S(2)}, u32[]{:S(2)}) collective-permute-start(f32[136,128]{1,0:T(8,128)S(1)} %add.30), channel_id=1, source_target_pairs={{0,3},{1,0},{2,1},{3,2},{4,7},{5,4},{6,5},{7,6},{8,11},{9,8},{10,9... | collective-permute-start | bytes 208904 | tf_op jit(solution)/shard_map/ppermute | solution.py:431
  36.8 6.3 %collective-permute-start.2 = (f32[136,128]{1,0:T(8,128)S(1)}, f32[136,128]{1,0:T(8,128)S(1)}, u32[]{:S(2)}, u32[]{:S(2)}) collective-permute-start(f32[136,128]{1,0:T(8,128)S(1)} %add.30), channel_id=1, source_target_pairs={{0,2},{1,3},{2,0},{3,1},{4,6},{5,7},{6,4},{7,5},{8,10},{9,11},{10,... | collective-permute-start | bytes 208904 | tf_op jit(solution)/shard_map/ppermute | solution.py:431
  37.7 6.1 %collective-permute-start.1 = (f32[136,128]{1,0:T(8,128)S(1)}, f32[136,128]{1,0:T(8,128)S(1)}, u32[]{:S(2)}, u32[]{:S(2)}) collective-permute-start(f32[136,128]{1,0:T(8,128)S(1)} %add.30), channel_id=1, source_target_pairs={{0,1},{1,2},{2,3},{3,0},{4,5},{5,6},{6,7},{7,4},{8,9},{9,10},{10,1... | collective-permute-start | bytes 208904 | tf_op jit(solution)/shard_map/ppermute | solution.py:431
  43.7 5.1 %collective-permute-start.6 = (f32[136,128]{1,0:T(8,128)S(1)}, f32[136,128]{1,0:T(8,128)S(1)}, u32[]{:S(2)}, u32[]{:S(2)}) collective-permute-start(f32[136,128]{1,0:T(8,128)S(1)} %add_add_fusion.2), channel_id=1, source_target_pairs={{0,12},{1,13},{2,14},{3,15},{4,0},{5,1},{6,2},{7,3},{8,4},{9,5},{1... | collective-permute-start | bytes 208904 | tf_op jit(solution)/shard_map/ppermute | solution.py:431
  46.9 5.9 %collective-permute-start.5 = (f32[136,128]{1,0:T(8,128)S(1)}, f32[136,128]{1,0:T(8,128)S(1)}, u32[]{:S(2)}, u32[]{:S(2)}) collective-permute-start(f32[136,128]{1,0:T(8,128)S(1)} %add_add_fusion.2), channel_id=1, source_target_pairs={{0,8},{1,9},{2,10},{3,11},{4,12},{5,13},{6,14},{7,15},{8,0},{9,1},... | collective-permute-start | bytes 208904 | tf_op jit(solution)/shard_map/ppermute | solution.py:431
  47.5 5.9 %collective-permute-start.4 = (f32[136,128]{1,0:T(8,128)S(1)}, f32[136,128]{1,0:T(8,128)S(1)}, u32[]{:S(2)}, u32[]{:S(2)}) collective-permute-start(f32[136,128]{1,0:T(8,128)S(1)} %add_add_fusion.2), channel_id=1, source_target_pairs={{0,4},{1,5},{2,6},{3,7},{4,8},{5,9},{6,10},{7,11},{8,12},{9,13},{1... | collective-permute-start | bytes 208904 | tf_op jit(solution)/shard_map/ppermute | solution.py:431
  53.5 6.1 %collective-permute-start.9 = (f32[136,128]{1,0:T(8,128)S(1)}, f32[136,128]{1,0:T(8,128)S(1)}, u32[]{:S(2)}, u32[]{:S(2)}) collective-permute-start(f32[136,128]{1,0:T(8,128)S(1)} %add_add_fusion.1), channel_id=1, source_target_pairs={{0,96},{1,97},{2,98},{3,99},{4,100},{5,101},{6,102},{7,103},{8,104... | collective-permute-start | bytes 208904 | tf_op jit(solution)/shard_map/ppermute | solution.py:431
  57.6 5.9 %collective-permute-start.8 = (f32[136,128]{1,0:T(8,128)S(1)}, f32[136,128]{1,0:T(8,128)S(1)}, u32[]{:S(2)}, u32[]{:S(2)}) collective-permute-start(f32[136,128]{1,0:T(8,128)S(1)} %add_add_fusion.1), channel_id=1, source_target_pairs={{0,64},{1,65},{2,66},{3,67},{4,68},{5,69},{6,70},{7,71},{8,72},{9,... | collective-permute-start | bytes 208904 | tf_op jit(solution)/shard_map/ppermute | solution.py:431
  57.6 6.3 %collective-permute-start.7 = (f32[136,128]{1,0:T(8,128)S(1)}, f32[136,128]{1,0:T(8,128)S(1)}, u32[]{:S(2)}, u32[]{:S(2)}) collective-permute-start(f32[136,128]{1,0:T(8,128)S(1)} %add_add_fusion.1), channel_id=1, source_target_pairs={{0,32},{1,33},{2,34},{3,35},{4,36},{5,37},{6,38},{7,39},{8,40},{9,... | collective-permute-start | bytes 208904 | tf_op jit(solution)/shard_map/ppermute | solution.py:431
  63.9 0.7 copy-start
  64.6 0.7 copy-start.3
  65.3 0.7 copy-start.4
  82.7 1.4 %collective-permute-start.10 = (f32[16,128]{1,0:T(8,128)S(1)}, f32[16,128]{1,0:T(8,128)S(1)}, u32[]{:S(2)}, u32[]{:S(2)}) collective-permute-start(f32[16,128]{1,0:T(8,128)S(1)} %get-tuple-element.14), channel_id=1, source_target_pairs={{0,112},{16,0},{32,16},{48,32},{64,48},{80,64},{96,80},{112,96},{1... | collective-permute-start | bytes 24584 | tf_op jit(solution)/shard_map/ppermute | solution.py:457
  82.7 4.3 %collective-permute-start.11 = (f32[16,128]{1,0:T(8,128)S(1)}, f32[16,128]{1,0:T(8,128)S(1)}, u32[]{:S(2)}, u32[]{:S(2)}) collective-permute-start(f32[16,128]{1,0:T(8,128)S(1)} %get-tuple-element.15), channel_id=1, source_target_pairs={{0,16},{16,32},{32,48},{48,64},{64,80},{80,96},{96,112},{112,0},{1... | collective-permute-start | bytes 24584 | tf_op jit(solution)/shard_map/ppermute | solution.py:458
  87.0 7.0 %collective-permute-start.13 = (f32[24,128]{1,0:T(8,128)S(1)}, f32[24,128]{1,0:T(8,128)S(1)}, u32[]{:S(2)}, u32[]{:S(2)}) collective-permute-start(f32[24,128]{1,0:T(8,128)S(1)} %pad_maximum_fusion), channel_id=1, source_target_pairs={{0,1},{1,2},{2,3},{3,4},{4,5},{5,6},{6,7},{7,8},{8,9},{9,10},{10,1... | collective-permute-start | bytes 36872 | tf_op jit(solution)/shard_map/ppermute | solution.py:461
  87.1 7.0 %collective-permute-start.12 = (f32[24,128]{1,0:T(8,128)S(1)}, f32[24,128]{1,0:T(8,128)S(1)}, u32[]{:S(2)}, u32[]{:S(2)}) collective-permute-start(f32[24,128]{1,0:T(8,128)S(1)} %pad_maximum_fusion), channel_id=1, source_target_pairs={{0,15},{1,0},{2,1},{3,2},{4,3},{5,4},{6,5},{7,6},{8,7},{9,8},{10,9... | collective-permute-start | bytes 36872 | tf_op jit(solution)/shard_map/ppermute | solution.py:460
